TPU v7x, 128 devices: a whole 4x4x4 slice. The times are simulated.
128 devices in a mesh: grp: 8 (over y, core), tile: 16 (over z, x).
Axes of the slice: x: 4, y: 4, z: 4, core: 2. Of those that a mesh axis runs over, the one named last changes fastest.
Arguments:
- prior_replicas: float32 [256, 8, 128, 1024], P('grp', None, 'tile'), may hold values from -140 to 140
- conductivity_map: float32 [8, 128, 1024], P(None, 'tile'), may hold values from 0.03 to 0.16
- member_slot: int32 [256], P('grp'), may hold values from 0 to 15, as said below
- merge_sketch: float32 [3, 32, 16], replicated, may hold values from -1 to 1
- obs_cells: int32 [4096], replicated, may hold values from 0 to 131071
- obs_values: float32 [4096], replicated, may hold values from -6 to 6
- obs_var: float32 [4096], replicated, may hold values from 30 to 300
Outputs:
- predicted_replicas: float32 [256, 8, 128, 1024], P('grp', None, 'tile')
- posterior_mean: float32 [128, 1024], P('tile', 'grp')
Inputs may be any that keep to these rules, and one draw needn't show every extreme that they name: `member_slot`: within each group of 32 members every column 0 to 15 is named by exactly 2 members.
All inputs are finite; a program needn't handle non-finite values.
Results may differ from a plain program's by a relative error of at most 0.0001.
Values sent between devices are 32-bit elements; how exact they have to be, the bound alone decides.
No kernel may reach another device: no remote copies, remote signals or barrier semaphores. Data moves between devices by JAX's collectives and lax.ppermute only.
A program may use at most 128 MiB of HBM per device.

v0:
```python
import jax
import jax.numpy as jnp
from jax import lax
from jax.sharding import PartitionSpec as P


def with_halo(value, sides, width):
    for axis, dim in sides:
        size, length = (lax.axis_size(axis), value.shape[dim])
        up = [(i, (i + 1) % size) for i in range(size - 1)]
        down = [(j, i) for i, j in up]
        last = lax.slice_in_dim(value, length - width, length, axis=dim)
        leading = lax.slice_in_dim(value, 0, width, axis=dim)
        before = lax.ppermute(last, axis, up)
        after = lax.ppermute(leading, axis, down)
        value = jnp.concatenate([before, value, after], axis=dim)
    return value


def from_partner(value, axis, apart):
    return lax.ppermute(value, axis, [(i, i ^ 1 << apart) for i in range(lax.axis_size(axis))])


def advance_timestep(enlarged_diffusivity, diffusivity):
    centre = enlarged_diffusivity[:, :, 1:-1, :]
    level_pad = jnp.pad(centre, ((0, 0), (1, 1), (0, 0), (0, 0)))
    cross_pad = jnp.pad(centre, ((0, 0), (0, 0), (0, 0), (1, 1)))
    lateral_neighbour = level_pad[:, 2:] + level_pad[:, :-2]
    lateral_neighbour = lateral_neighbour + cross_pad[..., 2:] + cross_pad[..., :-2]
    lateral_neighbour = (
        lateral_neighbour + enlarged_diffusivity[:, :, 2:, :] + enlarged_diffusivity[:, :, :-2, :]
    )
    return centre + diffusivity[None] * (lateral_neighbour - 6.0 * centre)


def margin_refresh(heat_distribution, diffusivity):
    enlarged_diffusivity = with_halo(heat_distribution, (("tile", 2),), 1)
    return advance_timestep(enlarged_diffusivity, diffusivity)


def compress(stack):
    grams = jnp.einsum("krc,ksc->krs", stack, stack, precision=lax.Precision.HIGHEST)
    grams = lax.psum(grams, "tile")
    lower = jnp.linalg.cholesky(grams)
    solved = jax.vmap(lambda a, b: jax.scipy.linalg.solve_triangular(a, b, lower=True))(
        lower, stack
    )
    scale = jnp.diagonal(lower, axis1=1, axis2=2)
    return solved * scale[:, :, None]


def local(
    prior_replicas, conductivity_map, member_slot, merge_sketch, obs_cells, obs_values, obs_var
):
    shard_replicas, depth_tiers_array, shard_lines, margin_thickness = prior_replicas.shape
    rank = merge_sketch.shape[2]
    shard_points = shard_lines * margin_thickness
    group_count = lax.axis_size("grp")
    member_total = shard_replicas * group_count
    predicted_replicas = margin_refresh(
        margin_refresh(prior_replicas, conductivity_map), conductivity_map
    )
    uppermost_tier = predicted_replicas[:, depth_tiers_array - 1].reshape(
        shard_replicas, shard_points
    )
    surface_mean = lax.psum(jnp.sum(uppermost_tier, axis=0), "grp") / member_total
    member_deviations = uppermost_tier - surface_mean[None, :]
    indicator_vector = (member_slot[:, None] == jnp.arange(rank, dtype=jnp.int32)[None, :]).astype(
        jnp.float32
    )
    sketch_block = jnp.einsum(
        "mr,mc->rc", indicator_vector, member_deviations, precision=lax.Precision.HIGHEST
    )
    basis = compress(sketch_block[None])[0]
    level_count = group_count.bit_length() - 1
    group = lax.axis_index("grp")
    for level in range(level_count):
        partner = from_partner(basis, "grp", level)
        upper_side = group // (1 << level) % 2 == 1
        first = jnp.where(upper_side, partner, basis)
        second = jnp.where(upper_side, basis, partner)
        joined = jnp.concatenate([first, second], axis=0)
        mixed = jnp.einsum(
            "kr,kc->rc", merge_sketch[level], joined, precision=lax.Precision.HIGHEST
        )
        basis = compress(mixed[None])[0]
    start = lax.axis_index("tile") * shard_points
    local_cell = obs_cells - start
    inside = ((local_cell >= 0) & (local_cell < shard_points)).astype(jnp.float32)
    safe_cell = jnp.clip(local_cell, 0, shard_points - 1)
    picked = basis[:, safe_cell] * inside[None, :]
    picked_mean = surface_mean[safe_cell] * inside
    picked, picked_mean = lax.psum((picked, picked_mean), "tile")
    innovation = obs_values - picked_mean
    weighted = picked / obs_var[None, :]
    system_part = jnp.dot(weighted, picked.T, precision=lax.Precision.HIGHEST)
    rhs = jnp.dot(weighted, innovation, precision=lax.Precision.HIGHEST)
    system = (member_total - 1) * jnp.eye(rank, dtype=jnp.float32) + system_part
    factor = jnp.linalg.cholesky(system)
    coefficients = jax.scipy.linalg.cho_solve((factor, True), rhs)
    column_width = margin_thickness // group_count
    column_start = lax.axis_index("grp") * column_width
    mean_grid = surface_mean.reshape(shard_lines, margin_thickness)
    basis_grid = basis.reshape(rank, shard_lines, margin_thickness)
    mean_cols = lax.dynamic_slice_in_dim(mean_grid, column_start, column_width, 1)
    basis_cols = lax.dynamic_slice_in_dim(basis_grid, column_start, column_width, 2)
    posterior_mean = mean_cols + jnp.einsum(
        "r,rxy->xy", coefficients, basis_cols, precision=lax.Precision.HIGHEST
    )
    return (predicted_replicas, posterior_mean)


def solution(mesh):
    in_specs = (P("grp", None, "tile", None), P(None, "tile", None), P("grp"), P(), P(), P(), P())
    out_specs = (P("grp", None, "tile", None), P("tile", "grp"))
    return jax.shard_map(local, mesh=mesh, in_specs=in_specs, out_specs=out_specs, check_vma=False)
```

profile of v0, /device:TPU:1, one launch (start us, length us, event | category | flops | bytes accessed | tf_op | source)
XLA Modules:
  0.0 493.6 jit_solution(3694299883525280292)
XLA Ops:
  7.2 11.0 %copy.57 = f32[32,8,8,1024]{3,1,2,0:T(8,128)S(1)} copy(f32[32,8,8,1024]{3,2,1,0:T(8,128)} %param.10) | data formatting | bytes 16777216 | tf_op args[0]
  19.6 4.6 collective-permute-start.1
  24.5 20.2 %collective-permute-done = f32[32,8,1,1024]{3,1,2,0:T(8,128)S(1)} collective-permute-done((f32[32,8,1,1024]{3,1,2,0:T(8,128)S(1)}, f32[32,8,1,1024]{3,1,2,0:T(8,128)S(1)}, u32[]{:S(2)}, u32[]{:S(2)}) %collective-permute-start) | collective-permute-done | bytes 1048608 | tf_op jit(solution)/shard_map/ppermute | solution.py:15
  45.5 6.2 %fusion.13 = f32[32,8,8,1024]{3,1,2,0:T(8,128)S(1)} fusion(f32[32,8,8,1024]{3,1,2,0:T(8,128)S(1)} %copy.57, f32[32,8,1,1024]{3,1,2,0:T(8,128)S(1)} %collective-permute-done.1, f32[32,8,1,1024]{3,1,2,0:T(8,128)S(1)} %collective-permute-done, f32[8,8,1024]{2,0,1:T(8,128)S(1)} %copy.49), kind=kLoop, calls=%fused_computation.31 | loop fusion | flops 23068672 | bytes 19136512 | tf_op jit(solution)/shard_map/add | solution.py:33
  53.3 16.5 %collective-permute-start.3 = (f32[32,8,1,1024]{3,1,2,0:T(8,128)S(1)}, f32[32,8,1,1024]{3,1,2,0:T(8,128)S(1)}, u32[]{:S(2)}, u32[]{:S(2)}) collective-permute-start(f32[32,8,1,1024]{3,1,2,0:T(8,128)S(1)} %get-tuple-element.15), channel_id=1, source_target_pairs={{0,1},{1,2},{2,3},{3,4},{4,5},{5,6},{6,7},{7,8},{8,9},{9,10},{10,1... | collective-permute-start | bytes 3145736 | tf_op jit(solution)/shard_map/ppermute | solution.py:14
  69.8 7.7 %collective-permute-done.2 = f32[32,8,1,1024]{3,1,2,0:T(8,128)S(1)} collective-permute-done((f32[32,8,1,1024]{3,1,2,0:T(8,128)S(1)}, f32[32,8,1,1024]{3,1,2,0:T(8,128)S(1)}, u32[]{:S(2)}, u32[]{:S(2)}) %collective-permute-start.2) | collective-permute-done | bytes 1048608 | tf_op jit(solution)/shard_map/ppermute | solution.py:15
  78.4 6.2 %fusion.20 = f32[32,8,8,1024]{3,1,2,0:T(8,128)S(1)} fusion(f32[32,8,8,1024]{3,1,2,0:T(8,128)S(1)} %fusion.13, f32[32,8,1,1024]{3,1,2,0:T(8,128)S(1)} %collective-permute-done.3, f32[32,8,1,1024]{3,1,2,0:T(8,128)S(1)} %collective-permute-done.2, f32[8,8,1024]{2,0,1:T(8,128)S(1)} %copy.49), kind=kLoop, calls=%fused_computation.38 | loop fusion | flops 23068672 | bytes 19136512 | tf_op jit(solution)/shard_map/add | solution.py:33
  84.6 3.2 copy-done
  87.8 3.4 slice_reduce_fusion
  91.3 23.6 %psum.49 = f32[8192]{0:T(1024)S(1)} all-reduce(f32[8192]{0:T(1024)S(1)} %bitcast.171), channel_id=1, replica_groups=mesh['grp'=8,'tile'=16] {'grp'}, use_global_device_ids=true, to_apply=%region_1.2 | all-reduce | flops 8192 | bytes 65536 | tf_op jit(solution)/shard_map/psum | solution.py:66
  116.9 36.5 %psum.50 = f32[1,16,16]{1,2,0:T(8,128)S(1)} all-reduce(f32[1,16,16]{1,2,0:T(8,128)S(1)} %convolution_bitcast_fusion.7), channel_id=1, replica_groups=mesh['grp'=8,'tile'=16] {'tile'}, use_global_device_ids=true, to_apply=%region_2.3 | all-reduce | flops 256 | bytes 2048 | tf_op jit(solution)/shard_map/psum | solution.py:43
  158.8 10.8 %collective-permute-start.4 = (f32[16,8192]{1,0:T(8,128)S(1)}, f32[16,8192]{1,0:T(8,128)S(1)}, u32[]{:S(2)}, u32[]{:S(2)}) collective-permute-start(f32[16,8192]{1,0:T(8,128)S(1)} %fusion.1), channel_id=1, source_target_pairs={{0,16},{16,0},{32,48},{48,32},{64,80},{80,64},{96,112},{112,96},{1... | collective-permute-start | bytes 1572872 | tf_op jit(solution)/shard_map/ppermute | solution.py:21
  172.7 29.1 %psum.51 = f32[1,16,16]{1,2,0:T(8,128)S(1)} all-reduce(f32[1,16,16]{1,2,0:T(8,128)S(1)} %convolution_bitcast_fusion.6), channel_id=1, replica_groups=mesh['grp'=8,'tile'=16] {'tile'}, use_global_device_ids=true, to_apply=%region_5.8 | all-reduce | flops 256 | bytes 2048 | tf_op jit(solution)/shard_map/psum | solution.py:43
  207.4 8.0 %collective-permute-done.5 = f32[16,8192]{1,0:T(8,128)S(1)} collective-permute-done((f32[16,8192]{1,0:T(8,128)S(1)}, f32[16,8192]{1,0:T(8,128)S(1)}, u32[]{:S(2)}, u32[]{:S(2)}) %collective-permute-start.5) | collective-permute-done | bytes 524320 | tf_op jit(solution)/shard_map/ppermute | solution.py:21
  217.0 30.7 %psum.52 = f32[1,16,16]{1,2,0:T(8,128)S(1)} all-reduce(f32[1,16,16]{1,2,0:T(8,128)S(1)} %convolution_bitcast_fusion.5), channel_id=1, replica_groups=mesh['grp'=8,'tile'=16] {'tile'}, use_global_device_ids=true, to_apply=%region_6.9 | all-reduce | flops 256 | bytes 2048 | tf_op jit(solution)/shard_map/psum | solution.py:43
  253.2 23.0 %gather_fusion.5 = f32[4096]{0:T(1024)S(1)} fusion(f32[8192]{0:T(1024)S(1)} %broadcast_multiply_fusion, s32[4096]{0:T(1024)S(1)} %fusion.52), kind=kCustom, calls=%fused_computation.5 | custom fusion | bytes 49152 | tf_op jit(solution)/shard_map/gather | solution.py:92
  277.9 56.0 %all-reduce.4 = (f32[4096]{0:T(1024)S(1)}, f32[1,16,16]{1,2,0:T(8,128)S(1)}) all-reduce(f32[4096]{0:T(1024)S(1)} %broadcast_select_fusion.6, f32[1,16,16]{1,2,0:T(8,128)S(1)} %convolution_bitcast_fusion.4), channel_id=1, replica_groups=mesh['grp'=8,'tile'=16] {'tile'}, use_global_device_ids=true, to_apply=%region_11.14 | all-reduce | flops 4352 | bytes 34816 | tf_op jit(solution)/shard_map/psum | solution.py:93
  339.2 2.7 copy.66
  341.9 13.1 %gather_fusion.4 = f32[4096,16]{1,0:T(8,128)S(1)} fusion(f32[16,8192]{0,1:T(8,128)} %copy.66, s32[4096]{0:T(1024)S(1)} %fusion.52), kind=kCustom, calls=%fused_computation.4 | custom fusion | bytes 540672 | tf_op jit(solution)/shard_map/gather | solution.py:91
  355.1 1.9 multiply_bitcast_fusion
  357.0 15.2 %copy.68 = f32[32,8,8,1024]{3,2,1,0:T(8,128)} copy(f32[32,8,8,1024]{3,1,2,0:T(8,128)} %copy-done) | data formatting | bytes 16777216
  372.6 99.3 %all-reduce.7.cloned.1.call-done = f32[16,4096]{0,1:T(8,128)} async-done(((f32[16,4096]{0,1:T(8,128)}), f32[16,4096]{0,1:T(8,128)}) %all-reduce.7.cloned.1.call-update) | async-done | bytes 262160 | tf_op jit(solution)/shard_map/psum | solution.py:93
  471.9 6.3 %fusion.25 = f32[16,16]{1,0:T(8,128)S(1)} fusion(f32[16,4096]{0,1:T(8,128)} %all-reduce.7.cloned.1.call-done, f32[4096]{0:T(1024)S(1)} %copy-done.6), kind=kOutput, calls=%fused_computation.48 | convolution fusion | flops 12648448 | bytes 279552 | tf_op jit(solution)/shard_map/dot_general | solution.py:96
  482.3 3.0 fusion.27
  (95 shorter events, 40.6 us)
Async XLA Ops:
  7.2 17.1 %copy-start.1 = (f32[8,8,1024]{2,1,0:T(8,128)S(1)}, f32[8,8,1024]{2,1,0:T(8,128)}, u32[]{:S(2)}) copy-start(f32[8,8,1024]{2,1,0:T(8,128)} %param.11) | copy-start | bytes 786436
  7.2 464.7 %all-reduce.7.cloned.1.call-start = ((), (), s32[]{:S(2)}) async-start(), calls=%async_computation | async-start | bytes 4194304 | tf_op jit(solution)/shard_map/psum | solution.py:93
  18.3 26.3 %collective-permute-start = (f32[32,8,1,1024]{3,1,2,0:T(8,128)S(1)}, f32[32,8,1,1024]{3,1,2,0:T(8,128)S(1)}, u32[]{:S(2)}, u32[]{:S(2)}) collective-permute-start(f32[32,8,1,1024]{3,1,2,0:T(8,128)S(1)} %get-tuple-element.16), channel_id=1, source_target_pairs={{1,0},{2,1},{3,2},{4,3},{5,4},{6,5},{7,6},{8,7},{9,8},{10,9},{11,1... | collective-permute-start | bytes 3145736 | tf_op jit(solution)/shard_map/ppermute | solution.py:15
  19.6 25.9 %collective-permute-start.1 = (f32[32,8,1,1024]{3,1,2,0:T(8,128)S(1)}, f32[32,8,1,1024]{3,1,2,0:T(8,128)S(1)}, u32[]{:S(2)}, u32[]{:S(2)}) collective-permute-start(f32[32,8,1,1024]{3,1,2,0:T(8,128)S(1)} %get-tuple-element.17), channel_id=1, source_target_pairs={{0,1},{1,2},{2,3},{3,4},{4,5},{5,6},{6,7},{7,8},{8,9},{9,10},{10,1... | collective-permute-start | bytes 3145736 | tf_op jit(solution)/shard_map/ppermute | solution.py:14
  52.0 25.5 %collective-permute-start.2 = (f32[32,8,1,1024]{3,1,2,0:T(8,128)S(1)}, f32[32,8,1,1024]{3,1,2,0:T(8,128)S(1)}, u32[]{:S(2)}, u32[]{:S(2)}) collective-permute-start(f32[32,8,1,1024]{3,1,2,0:T(8,128)S(1)} %get-tuple-element.14), channel_id=1, source_target_pairs={{1,0},{2,1},{3,2},{4,3},{5,4},{6,5},{7,6},{8,7},{9,8},{10,9},{11,1... | collective-permute-start | bytes 3145736 | tf_op jit(solution)/shard_map/ppermute | solution.py:15
  53.3 25.1 %collective-permute-start.3 = (f32[32,8,1,1024]{3,1,2,0:T(8,128)S(1)}, f32[32,8,1,1024]{3,1,2,0:T(8,128)S(1)}, u32[]{:S(2)}, u32[]{:S(2)}) collective-permute-start(f32[32,8,1,1024]{3,1,2,0:T(8,128)S(1)} %get-tuple-element.15), channel_id=1, source_target_pairs={{0,1},{1,2},{2,3},{3,4},{4,5},{5,6},{6,7},{7,8},{8,9},{9,10},{10,1... | collective-permute-start | bytes 3145736 | tf_op jit(solution)/shard_map/ppermute | solution.py:14
  69.8 45.7 %copy-start.5 = (s32[32]{0:T(128)S(1)}, s32[32]{0:T(128)}, u32[]{:S(2)}) copy-start(s32[32]{0:T(128)} %param.12) | copy-start | bytes 388
  84.6 3.2 copy-start
  87.8 83.4 %copy-start.3 = (f32[3,32,16]{1,2,0:T(8,128)S(1)}, f32[3,32,16]{1,2,0:T(8,128)}, u32[]{:S(2)}) copy-start(f32[3,32,16]{1,2,0:T(8,128)} %param.13) | copy-start | bytes 18436
  115.5 137.6 %copy-start.2 = (s32[4096]{0:T(1024)S(1)}, s32[4096]{0:T(1024)}, u32[]{:S(2)}) copy-start(s32[4096]{0:T(1024)} %param.14) | copy-start | bytes 49156
  158.8 12.3 %collective-permute-start.4 = (f32[16,8192]{1,0:T(8,128)S(1)}, f32[16,8192]{1,0:T(8,128)S(1)}, u32[]{:S(2)}, u32[]{:S(2)}) collective-permute-start(f32[16,8192]{1,0:T(8,128)S(1)} %fusion.1), channel_id=1, source_target_pairs={{0,16},{16,0},{32,48},{48,32},{64,80},{80,64},{96,112},{112,96},{1... | collective-permute-start | bytes 1572872 | tf_op jit(solution)/shard_map/ppermute | solution.py:21
  207.2 8.1 %collective-permute-start.5 = (f32[16,8192]{1,0:T(8,128)S(1)}, f32[16,8192]{1,0:T(8,128)S(1)}, u32[]{:S(2)}, u32[]{:S(2)}) collective-permute-start(f32[16,8192]{1,0:T(8,128)S(1)} %fusion.3), channel_id=1, source_target_pairs={{0,32},{16,48},{32,0},{48,16},{64,96},{80,112},{96,64},{112,80},{1... | collective-permute-start | bytes 1572872 | tf_op jit(solution)/shard_map/ppermute | solution.py:21
  253.0 23.2 %collective-permute-start.6 = (f32[16,8192]{1,0:T(8,128)S(1)}, f32[16,8192]{1,0:T(8,128)S(1)}, u32[]{:S(2)}, u32[]{:S(2)}) collective-permute-start(f32[16,8192]{1,0:T(8,128)S(1)} %fusion.5), channel_id=1, source_target_pairs={{0,64},{16,80},{32,96},{48,112},{64,0},{80,16},{96,32},{112,48},{1... | collective-permute-start | bytes 1572872 | tf_op jit(solution)/shard_map/ppermute | solution.py:21
  357.0 15.5 %copy-start.4 = (f32[4096]{0:T(1024)S(1)}, f32[4096]{0:T(1024)}, u32[]{:S(2)}) copy-start(f32[4096]{0:T(1024)} %param.15) | copy-start | bytes 49156
  357.0 114.9 %copy-start.6 = (f32[4096]{0:T(1024)S(1)}, f32[4096]{0:T(1024)}, u32[]{:S(2)}) copy-start(f32[4096]{0:T(1024)} %param.16) | copy-start | bytes 49156
Sparse Core Ops, SparseCore 0:
  357.1 114.7 all-reduce.6
where the time goes:
time: 502 us; the launch traced here: 494 us
  blocking collectives  176 us (35%)
  waiting for transfers between devices  139 us (28%)
  local copies, waits for them, and re-layouts  72.8 us (15%)
  other arithmetic  38.8 us (8%)
  starting transfers between devices  34.7 us (7%)
  matrix products  18.1 us (4%)
  between operations  14.9 us (3%)
    psum x1, waiting for transfers between devices, local(): picked, picked_mean = lax.psum((picked, picked_mean), 'tile')  99.3 us
    psum x3, blocking collectives, compress(): grams = lax.psum(grams, 'tile')  96.2 us
    psum x1, blocking collectives, local(): picked, picked_mean = lax.psum((picked, picked_mean), 'tile')  56 us
    unnamed x20, local copies, waits for them, and re-layouts  30.5 us
    ppermute x2, waiting for transfers between devices, with_halo(): after = lax.ppermute(leading, axis, down)  27.9 us
    psum x1, blocking collectives, local(): lax.psum(jnp.sum(uppermost_tier, axis=0), 'grp') / member_total  23.6 us
    gather x1, local copies, waits for them, and re-layouts, local(): picked_mean = surface_mean[safe_cell] * inside  23 us
    ppermute x2, starting transfers between devices, with_halo(): before = lax.ppermute(last, axis, up)  21.1 us
  transfers between devices with their start and end apart: 8, of which 7 were waited for; matrix products, arithmetic and copies ran while one was open for 8% of the time, Pallas kernels for 0%

commit v1 on v0

v1 whole, which is shorter than its diff:
```python
import jax
import jax.numpy as jnp
from jax import lax
from jax.experimental import pallas as pl
from jax.experimental.pallas import tpu as pltpu
from jax.sharding import PartitionSpec as P

HI = lax.Precision.HIGHEST
VMEM = pl.BlockSpec(memory_space=pltpu.VMEM)
SMEM = pl.BlockSpec(memory_space=pltpu.SMEM)
CHUNKS = (8, 8, 8, 8)
F32 = jnp.float32


def shape(*dims):
    return jax.ShapeDtypeStruct(dims, F32)


def cost(nbytes, flops=0):
    return pl.CostEstimate(flops=flops, bytes_accessed=nbytes, transcendentals=0)


def lanes_sum(v):
    width = v.shape[1]
    lane = lax.broadcasted_iota(jnp.int32, v.shape, 1)
    left = jnp.where(lane == 0, 0.0, pltpu.roll(v, 1, 1))
    right = jnp.where(lane == width - 1, 0.0, pltpu.roll(v, width - 1, 1))
    return left + right


def rows_sum(v, before, after):
    rows = v.shape[0]
    row = lax.broadcasted_iota(jnp.int32, v.shape, 0)
    up = jnp.where(row == 0, before, pltpu.roll(v, 1, 0))
    down = jnp.where(row == rows - 1, after, pltpu.roll(v, rows - 1, 0))
    return up + down


def pair_kernel(slot_ref, k_ref, a_ref, b_ref, c_ref, sum_ref, low_ref, high_ref):
    step = pl.program_id(0)
    members = a_ref.shape[0]

    @pl.when(step == 0)
    def _():
        sum_ref[...] = jnp.zeros_like(sum_ref)

    for m in range(members):
        slot = slot_ref[step * members + m]
        for level, ref in enumerate((a_ref, b_ref, c_ref)):
            sum_ref[level, slot] += ref[m, 0]

    @pl.when(step == pl.num_programs(0) - 1)
    def _():
        rank = sum_ref.shape[1]
        for s in range(rank):
            for part, (level, lo, hi) in enumerate(((1, 0, 7), (2, 0, 7), (2, 1, 6))):
                at = part * rank + s
                low_ref[at : at + 1, :] = sum_ref[level, s, lo : lo + 1, :]
                high_ref[at : at + 1, :] = sum_ref[level, s, hi : hi + 1, :]
        for level in range(k_ref.shape[0]):
            at = 3 * rank + level
            low_ref[at : at + 1, :] = k_ref[level, 0:1, :]
            high_ref[at : at + 1, :] = k_ref[level, 7:8, :]


def pair_sums(prior, slots, k, rank):
    members, levels, rows, width = prior.shape
    block = 4
    specs = [
        pl.BlockSpec((block, 1, rows, width), lambda i, s, l=l: (i, l, 0, 0))
        for l in (levels - 3, levels - 2, levels - 1)
    ]
    edge = 3 * rank + levels
    return pl.pallas_call(
        pair_kernel,
        grid_spec=pltpu.PrefetchScalarGridSpec(
            num_scalar_prefetch=1,
            grid=(members // block,),
            in_specs=[pl.BlockSpec((levels, rows, width), lambda i, s: (0, 0, 0))] + specs,
            out_specs=[
                pl.BlockSpec((3, rank, rows, width), lambda i, s: (0, 0, 0, 0)),
                pl.BlockSpec((edge, width), lambda i, s: (0, 0)),
                pl.BlockSpec((edge, width), lambda i, s: (0, 0)),
            ],
        ),
        out_shape=[shape(3, rank, rows, width), shape(edge, width), shape(edge, width)],
        compiler_params=pltpu.CompilerParams(vmem_limit_bytes=32 << 20),
        cost_estimate=cost(6 << 20),
        name="pair_sums",
    )(slots, k, prior, prior, prior)


def pack_kernel(u_ref, low_ref, high_ref):
    members = u_ref.shape[0] // 64
    for m in range(members):
        for r in range(2):
            for l in range(8):
                at = m * 64 + l * 8
                low_ref[m, r, l : l + 1, :] = u_ref[at + r : at + r + 1, :]
                high_ref[m, r, l : l + 1, :] = u_ref[at + 7 - r : at + 8 - r, :]


def pack(flat, first, count):
    width = flat.shape[1]
    block = 4
    out = pl.BlockSpec((block, 2, 8, width), lambda i: (i, 0, 0, 0))
    return pl.pallas_call(
        pack_kernel,
        grid=(count // block,),
        in_specs=[pl.BlockSpec((block * 64, width), lambda i: (first // block + i, 0))],
        out_specs=[out, out],
        out_shape=[shape(count, 2, 8, width)] * 2,
        compiler_params=pltpu.CompilerParams(vmem_limit_bytes=32 << 20),
        cost_estimate=cost(count * 3 * 128 << 10),
        name="pack_edges",
    )(flat)


def step_kernel(u_ref, before_ref, after_ref, first_ref, last_ref, k_ref, kb_ref, ka_ref, *rest):
    out_ref, one_ref = rest[-2:]
    levels = 8

    def edge(near, far, inner, k):
        zero = jnp.zeros((1, near.shape[1]), F32)
        total = rows_sum(near, zero, zero) + lanes_sum(near) + far + inner
        return near + k * (total - 6.0 * near)

    b0, a0 = before_ref[0, 0], after_ref[0, 0]
    b1 = edge(b0, before_ref[0, 1], first_ref[0, 0], kb_ref[...])
    a1 = edge(a0, after_ref[0, 1], last_ref[0, 0], ka_ref[...])

    def sweep(src, dst, before, after):
        for l in range(levels):
            v = src[l * 8 : l * 8 + 8, :]
            total = rows_sum(v, before[l : l + 1, :], after[l : l + 1, :]) + lanes_sum(v)
            if l > 0:
                total = total + src[l * 8 - 8 : l * 8, :]
            if l < levels - 1:
                total = total + src[l * 8 + 8 : l * 8 + 16, :]
            dst[l * 8 : l * 8 + 8, :] = v + k_ref[l] * (total - 6.0 * v)

    sweep(u_ref, one_ref, b0, a0)
    sweep(one_ref, out_ref, b1, a1)


def two_steps(flat, before, after, low, high, k, kb, ka, done, first):
    count, _, levels, width = before.shape
    rows = 64
    edge = pl.BlockSpec((1, 2, levels, width), lambda i: (i, 0, 0, 0))
    inner = pl.BlockSpec((1, 1, levels, width), lambda i: (i, 0, 0, 0))
    small = pl.BlockSpec((levels, width), lambda i: (0, 0))
    place = pl.BlockSpec((rows, width), lambda i: (first + i, 0))
    operands = [flat, before, after, low, high, k, kb, ka]
    specs = [place, edge, edge, inner, inner, pl.BlockSpec((levels, 8, width), lambda i: (0, 0, 0)), small, small]
    aliases = {}
    if done is not None:
        operands.append(done)
        specs.append(pl.BlockSpec(memory_space=pl.ANY))
        aliases = {8: 0}
    return pl.pallas_call(
        step_kernel,
        grid=(count,),
        in_specs=specs,
        out_specs=place,
        out_shape=shape(*flat.shape),
        scratch_shapes=[pltpu.VMEM((rows, width), F32)],
        input_output_aliases=aliases,
        compiler_params=pltpu.CompilerParams(vmem_limit_bytes=32 << 20),
        cost_estimate=cost(count * 640 << 10),
        name="two_steps",
    )(*operands)


def surface_kernel(p_ref, before_ref, after_ref, low_ref, high_ref, k_ref, out_ref):
    rank = p_ref.shape[1] // 8
    width = p_ref.shape[2]
    levels = k_ref.shape[0]
    zero = jnp.zeros((1, width), F32)

    def edge(ref, own_ref):
        low, near, far = (ref[i * rank : (i + 1) * rank, :] for i in range(3))
        k = ref[3 * rank + levels - 1 : 3 * rank + levels, :]
        inner = own_ref[rank : 2 * rank, :]
        return near + k * (low + far + inner + lanes_sum(near) - 6.0 * near)

    b1, a1 = edge(before_ref, low_ref), edge(after_ref, high_ref)
    k6, k7 = k_ref[levels - 2], k_ref[levels - 1]
    piece = out_ref.shape[2]
    for s in range(rank):
        at = pl.ds(s * 8, 8)
        u5, u6, u7 = (p_ref[i, at, :] for i in range(3))

        def row(ref, part):
            return ref[part * rank + s : part * rank + s + 1, :]

        t6 = rows_sum(u6, row(before_ref, 0), row(after_ref, 0)) + lanes_sum(u6) + u5 + u7
        t7 = rows_sum(u7, row(before_ref, 1), row(after_ref, 1)) + lanes_sum(u7) + u6
        v6 = u6 + k6 * (t6 - 6.0 * u6)
        v7 = u7 + k7 * (t7 - 6.0 * u7)
        total = rows_sum(v7, b1[s : s + 1, :], a1[s : s + 1, :]) + lanes_sum(v7) + v6
        w7 = v7 + k7 * (total - 6.0 * v7)
        for g in range(width // piece):
            out_ref[g, s * 8 : s * 8 + 8, :] = w7[:, g * piece : (g + 1) * piece]


def surface(sums, before, after, low, high, k, groups):
    levels, rank, rows, width = sums.shape
    return pl.pallas_call(
        surface_kernel,
        in_specs=[VMEM] * 6,
        out_specs=VMEM,
        out_shape=shape(groups, rank * rows, width // groups),
        compiler_params=pltpu.CompilerParams(vmem_limit_bytes=32 << 20),
        cost_estimate=cost(4 << 20),
        name="surface_steps",
    )(sums.reshape(levels, rank * rows, width), before, after, low, high, k)


def sensor_kernel(at_ref, cell_ref, value_ref, var_ref, out_ref):
    width, columns = 1024, out_ref.shape[1]
    rows = out_ref.shape[0] // 2
    chunks, span = cell_ref.shape
    weight = 1.0 / var_ref[...]
    local = cell_ref[...] - at_ref[0] * (rows * width)
    x = local // width
    y = local - x * width - at_ref[1] * columns
    left, right = [], []
    row = lax.broadcasted_iota(jnp.int32, (rows, span), 0)
    column = lax.broadcasted_iota(jnp.int32, (columns, span), 0)
    weighted = weight * value_ref[...]
    for c in range(chunks):
        hit = x[c : c + 1, :] == row
        left.append(
            jnp.concatenate(
                [jnp.where(hit, weight[c : c + 1, :], 0.0), jnp.where(hit, weighted[c : c + 1, :], 0.0)], 0
            )
        )
        right.append(jnp.where(y[c : c + 1, :] == column, 1.0, 0.0))
    out_ref[...] = lax.dot_general(
        jnp.concatenate(left, 1),
        jnp.concatenate(right, 1),
        (((1,), (1,)), ((), ())),
        precision=HI,
        preferred_element_type=F32,
    )


def sensors(place, cells, values, var, columns):
    return pl.pallas_call(
        sensor_kernel,
        in_specs=[SMEM, VMEM, VMEM, VMEM],
        out_specs=VMEM,
        out_shape=shape(16, columns),
        compiler_params=pltpu.CompilerParams(vmem_limit_bytes=32 << 20),
        cost_estimate=cost(4 << 20),
        name="sensor_sums",
    )(place, *(a.reshape(-1, 128) for a in (cells, values, var)))


def gram_kernel(place_ref, obs_ref, own_ref, r1_ref, r2_ref, r3_ref, sums_ref, s_ref, mean_ref, raw_ref):
    chip, core = place_ref[1] // 2, place_ref[1] % 2
    for d, ref in ((0, own_ref), (1, r1_ref), (2, r2_ref), (3, r3_ref)):
        for slot in range(2):
            group = jnp.bitwise_xor(chip, d) * 2 + jnp.bitwise_xor(core, slot)
            raw_ref[pl.ds(pl.multiple_of(group * 128, 128), 128), :] = ref[slot]
    total = None
    sketches = raw_ref.shape[0] // 8
    member_total = 2 * sketches
    for x in range(0, 8, 2):
        both, means, weights, values = [], [], [], []
        for i in (x, x + 1):
            raw = raw_ref[pl.ds(i, sketches, stride=8), :]
            mean = jnp.sum(raw, axis=0, keepdims=True) * (1.0 / member_total)
            dev = raw - 2.0 * mean
            s_ref[:, i * 128 : (i + 1) * 128] = dev
            mean_ref[i : i + 1, :] = mean
            both.append(dev)
            w = obs_ref[i : i + 1, :]
            weights.append(w)
            values.append(obs_ref[8 + i : 9 + i, :] - mean * w)
        dev = jnp.concatenate(both, 1)
        w = jnp.concatenate(weights, 1)
        z = jnp.broadcast_to(jnp.concatenate(values, 1), (8, dev.shape[1]))
        left = jnp.concatenate([dev, dev * w, z], 0)
        part = lax.dot_general(left, dev, (((1,), (1,)), ((), ())), precision=HI, preferred_element_type=F32)
        total = part if total is None else total + part
    gram, weighted, rhs = total[:sketches], total[sketches : 2 * sketches], total[2 * sketches :]
    row = lax.broadcasted_iota(jnp.int32, gram.shape, 0)
    lane = lax.broadcasted_iota(jnp.int32, gram.shape, 1)
    sums_ref[0:sketches, :] = jnp.where(lane > row, gram, weighted)
    sums_ref[sketches : sketches + 8, :] = jnp.broadcast_to(
        jnp.sum(jnp.where(lane == row, gram, 0.0), axis=0, keepdims=True), (8, 128)
    )
    sums_ref[sketches + 8 : sketches + 16, :] = rhs


def gram(place, obs, own, r1, r2, r3):
    return pl.pallas_call(
        gram_kernel,
        in_specs=[SMEM] + [VMEM] * 5,
        out_specs=[VMEM] * 3,
        out_shape=[shape(144, 128), shape(128, 1024), shape(8, 128)],
        scratch_shapes=[pltpu.VMEM((1024, 128), F32)],
        compiler_params=pltpu.CompilerParams(vmem_limit_bytes=32 << 20),
        cost_estimate=cost(4 << 20),
        name="gram_sums",
    )(place, obs, own, r1, r2, r3)


def dot(a, b, ca=1, cb=0):
    return lax.dot_general(a, b, (((ca,), (cb,)), ((), ())), precision=HI, preferred_element_type=F32)


def analysis_kernel(sums_ref, m_ref, s_ref, mean_ref, out_ref):
    n = 128
    rank = m_ref.shape[2]
    packed = sums_ref[0:n, :]
    row = lax.broadcasted_iota(jnp.int32, (n, n), 0)
    lane = lax.broadcasted_iota(jnp.int32, (n, n), 1)
    upper = jnp.where(lane > row, packed, 0.0)
    lower = jnp.where(lane < row, packed, 0.0)
    g = upper + upper.T + jnp.where(lane == row, sums_ref[n : n + 1, :], 0.0)
    h = lower + lower.T + jnp.where(lane == row, packed, 0.0)
    q = sums_ref[n + 8 : n + 9, :]

    def mixer(level, blocks):
        mt = m_ref[level].T
        rows = []
        for p in range(blocks):
            parts = [jnp.zeros((rank, 2 * rank), F32)] * blocks
            parts[p] = mt
            rows.append(jnp.concatenate(parts, 1) if blocks > 1 else mt)
        return jnp.concatenate(rows, 0) if blocks > 1 else rows[0]

    def eliminate(c, extra, blocks):
        wide = c.shape[1]
        both = jnp.concatenate([c, extra], 1)
        width = both.shape[1]
        sub = lax.broadcasted_iota(jnp.int32, (rank, width), 0)
        parts = [both[b * rank : (b + 1) * rank, :] for b in range(blocks)]
        for j in range(rank - 1):
            for b in range(blocks):
                v = parts[b]
                at = b * rank + j
                column = jnp.broadcast_to(v[:, at : at + 1], v.shape)
                factor = jnp.where(sub > j, column / column[j : j + 1, :], 0.0)
                parts[b] = v - factor * v[j : j + 1, :]
        both = jnp.concatenate(parts, 0) if blocks > 1 else parts[0]
        return both[:, :wide], both[:, wide:]

    def eye(k):
        return jnp.where(
            lax.broadcasted_iota(jnp.int32, (k, k), 0) == lax.broadcasted_iota(jnp.int32, (k, k), 1), 1.0, 0.0
        ).astype(F32)

    blocks = n // rank
    c = g
    w = None
    for level in range(m_ref.shape[0]):
        tc, t = eliminate(c, eye(c.shape[0]), blocks)
        blocks //= 2
        mix = mixer(level, blocks)
        x = dot(mix, t)
        c = dot(dot(mix, tc), x, 1, 1)
        w = x if w is None else dot(x, w)
    h3 = dot(dot(w, h), w, 1, 1)
    q3 = jnp.sum(w * q, axis=1, keepdims=True)
    u, t3 = eliminate(c, eye(rank), 1)
    system = 255.0 * eye(rank) + dot(dot(t3, h3), t3, 1, 1)
    rhs = jnp.sum(t3 * dot(jnp.broadcast_to(q, (8, n)), w, 1, 1)[0:1, :], axis=1, keepdims=True)
    v = jnp.concatenate([system, jnp.broadcast_to(rhs, (rank, rank))], 1)
    sub = lax.broadcasted_iota(jnp.int32, v.shape, 0)
    for j in range(rank):
        column = jnp.broadcast_to(v[:, j : j + 1], v.shape)
        factor = jnp.where(sub != j, column / column[j : j + 1, :], 0.0)
        v = v - factor * v[j : j + 1, :]
    diagonal = jnp.sum(jnp.where(eye(rank) > 0.5, v[:, :rank], 0.0), axis=1, keepdims=True)
    coef = v[:, rank : rank + 1] / diagonal
    basis_map = dot(t3, w)
    weights = jnp.sum(coef * basis_map, axis=0, keepdims=True)
    increment = dot(jnp.broadcast_to(weights, (8, n)), s_ref[...])
    for i in range(8):
        out_ref[i : i + 1, :] = mean_ref[i : i + 1, :] + increment[0:1, i * 128 : (i + 1) * 128]


def analysis(sums, merge, s, mean):
    return pl.pallas_call(
        analysis_kernel,
        in_specs=[VMEM] * 4,
        out_specs=VMEM,
        out_shape=shape(8, 128),
        compiler_params=pltpu.CompilerParams(vmem_limit_bytes=32 << 20),
        cost_estimate=cost(16 << 20),
        name="analysis",
    )(sums, merge, s, mean)


def to_next(v):
    size = lax.axis_size("tile")
    return lax.ppermute(v, "tile", [(i, i + 1) for i in range(size - 1)])


def to_previous(v):
    size = lax.axis_size("tile")
    return lax.ppermute(v, "tile", [(i + 1, i) for i in range(size - 1)])


def across(v, axis, bits):
    return lax.ppermute(v, axis, [(i, i ^ bits) for i in range(lax.axis_size(axis))])


def local(prior, k, slots, merge, cells, values, var):
    members, levels, rows, width = prior.shape
    rank = merge.shape[2]
    groups = lax.axis_size("grp")
    tile, group = lax.axis_index("tile"), lax.axis_index("grp")
    chip, core = group // 2, group % 2
    place = jnp.stack([tile, group]).astype(jnp.int32)
    flat = prior.reshape(members * levels * rows, width)

    sums, low, high = pair_sums(prior, slots, k, rank)
    before = to_next(high)
    after = to_previous(low)
    kb, ka = before[3 * rank :], after[3 * rank :]

    arrived = []
    first = 0
    for count in CHUNKS:
        lo, hi = pack(flat, first, count)
        arrived.append((first, to_next(hi), to_previous(lo), lo, hi))
        first += count

    pieces = surface(sums, before, after, low, high, k, groups).reshape(groups // 2, 2, rank * rows, width // groups)
    obs = sensors(place, cells, values, var, width // groups)

    mine = lax.dynamic_index_in_dim(pieces, core, 1, False)
    other = lax.dynamic_index_in_dim(pieces, 1 - core, 1, False)
    pairs = jnp.stack([mine, across(other, "grp", 1)], 1)

    def pair_for(bits):
        return lax.dynamic_index_in_dim(pairs, chip ^ bits, 0, False)

    own = pair_for(0)
    r1, r3, r2 = (across(pair_for(bits), "grp", 2 * bits) for bits in (1, 3, 2))
    part, sketches, mean = gram(place, obs, own, r1, r2, r3)

    half = part.reshape(2, -1, part.shape[1])
    total = lax.dynamic_index_in_dim(half, core, 0, False) + across(
        lax.dynamic_index_in_dim(half, 1 - core, 0, False), "grp", 1
    )
    for axis, bits in (("grp", 2), ("grp", 6), ("tile", 4), ("tile", 12), ("tile", 1), ("tile", 3)):
        total = total + across(total, axis, bits)
    second = across(total, "grp", 1)
    both = jnp.where(core == 0, jnp.concatenate([total, second], 0), jnp.concatenate([second, total], 0))

    posterior = analysis(both, merge, sketches, mean)

    out = None
    for first, b, a, lo, hi in arrived:
        out = two_steps(flat, b, a, lo, hi, k, kb, ka, out, first)
    return out.reshape(prior.shape), posterior


def solution(mesh):
    in_specs = (P("grp", None, "tile", None), P(None, "tile", None), P("grp"), P(), P(), P(), P())
    out_specs = (P("grp", None, "tile", None), P("tile", "grp"))
    return jax.shard_map(local, mesh=mesh, in_specs=in_specs, out_specs=out_specs, check_vma=False)
```

time: 502 us -> 148 us (0.29)
  the two profiles are of different devices: /device:TPU:1 before, /device:TPU:57 now
where the time goes in v1:
time: 148 us; the launch traced here: 146 us
  starting transfers between devices  53.3 us (36%)
  Pallas kernels  48.2 us (33%)
  waiting for transfers between devices  21.9 us (15%)
  local copies, waits for them, and re-layouts  20.6 us (14%)
    pallas_call x4, Pallas kernels, two_steps(): pl.pallas_call(step_kernel, grid=(count,), in_specs=specs, out_specs=plac...  24.7 us
    ppermute x5, starting transfers between devices, to_previous(): return lax.ppermute(v, 'tile', [(i + 1, i) for i in range(size - 1)])  23.9 us
    unnamed x33, local copies, waits for them, and re-layouts  19 us
    ppermute x12, waiting for transfers between devices, across(): lax.ppermute(v, axis, [(i, i ^ bits) for i in range(lax.axis_size(axis))])  18 us
    ppermute x12, starting transfers between devices, across(): lax.ppermute(v, axis, [(i, i ^ bits) for i in range(lax.axis_size(axis))])  17.6 us
    pallas_call x1, Pallas kernels, analysis(): pl.pallas_call(analysis_kernel, in_specs=[VMEM] * 4, out_specs=VMEM, out_...  11.9 us
    ppermute x5, starting transfers between devices, to_next(): return lax.ppermute(v, 'tile', [(i, i + 1) for i in range(size - 1)])  11.8 us
    pallas_call x4, Pallas kernels, pack(): pl.pallas_call(pack_kernel, grid=(count // block,), in_specs=[pl.BlockSpe...  3.57 us
  transfers between devices with their start and end apart: 22, of which 9 were waited for; matrix products, arithmetic and copies ran while one was open for 2% of the time, Pallas kernels for 22%

profile of v1, /device:TPU:57, one launch (start us, length us, event | category | flops | bytes accessed | tf_op | source)
XLA Modules:
  0.0 145.9 jit_solution(18126333025801505338)
XLA Ops:
  0.6 3.4 %copy-done = f32[32,8,8,1024]{3,2,1,0:T(8,128)S(1)} copy-done((f32[32,8,8,1024]{3,2,1,0:T(8,128)S(1)}, f32[32,8,8,1024]{3,2,1,0:T(8,128)}, u32[]{:S(2)}) %copy-start) | copy-done | bytes 8388632
  7.2 3.1 %collective-permute-start.2 = (f32[56,1024]{1,0:T(8,128)S(1)}, f32[56,1024]{1,0:T(8,128)S(1)}, u32[]{:S(2)}, u32[]{:S(2)}) collective-permute-start(f32[56,1024]{1,0:T(8,128)S(1)} %get-tuple-element.18.high_ref), channel_id=1, source_target_pairs={{0,1},{1,2},{2,3},{3,4},{4,5},{5,6},{6,7},{7,8},{8,9},{9,10},{10,1... | collective-permute-start | bytes 688136 | tf_op jit(solution)/shard_map/ppermute | solution.py:400
  10.3 4.3 %collective-permute-start.3 = (f32[56,1024]{1,0:T(8,128)S(1)}, f32[56,1024]{1,0:T(8,128)S(1)}, u32[]{:S(2)}, u32[]{:S(2)}) collective-permute-start(f32[56,1024]{1,0:T(8,128)S(1)} %get-tuple-element.19.low_ref), channel_id=1, source_target_pairs={{1,0},{2,1},{3,2},{4,3},{5,4},{6,5},{7,6},{8,7},{9,8},{10,9},{11,1... | collective-permute-start | bytes 688136 | tf_op jit(solution)/shard_map/ppermute | solution.py:405
  14.6 3.0 %collective-permute-done.2.before_ref = f32[56,1024]{1,0:T(8,128)S(1)} collective-permute-done((f32[56,1024]{1,0:T(8,128)S(1)}, f32[56,1024]{1,0:T(8,128)S(1)}, u32[]{:S(2)}, u32[]{:S(2)}) %collective-permute-start.2) | collective-permute-done | bytes 229408 | tf_op jit(solution)/shard_map/ppermute | solution.py:400
  25.5 2.7 %collective-permute-start.13 = (f32[2,128,128]{2,1,0:T(8,128)}, f32[2,128,128]{2,1,0:T(8,128)}, u32[]{:S(2)}, u32[]{:S(2)}) collective-permute-start(f32[2,128,128]{2,1,0:T(8,128)} %get-tuple-element.30), channel_id=1, source_target_pairs={{0,96},{16,112},{32,64},{48,80},{64,32},{80,48},{96,0},{112,16},{1... | collective-permute-start | bytes 393224 | tf_op jit(solution)/shard_map/ppermute | solution.py:409
  28.3 3.4 %copy-done.1 = f32[32,8,8,1024]{3,2,1,0:T(8,128)S(1)} copy-done((f32[32,8,8,1024]{3,2,1,0:T(8,128)S(1)}, f32[32,8,8,1024]{3,2,1,0:T(8,128)}, u32[]{:S(2)}) %copy-start.1) | copy-done | bytes 8388632
  31.9 3.0 %collective-permute-start.8 = (f32[8,2,8,1024]{3,2,1,0:T(8,128)S(1)}, f32[8,2,8,1024]{3,2,1,0:T(8,128)S(1)}, u32[]{:S(2)}, u32[]{:S(2)}) collective-permute-start(f32[8,2,8,1024]{3,2,1,0:T(8,128)S(1)} %get-tuple-element.24.last_ref), channel_id=1, source_target_pairs={{0,1},{1,2},{2,3},{3,4},{4,5},{5,6},{6,7},{7,8},{8,9},{9,10},{10,1... | collective-permute-start | bytes 1572872 | tf_op jit(solution)/shard_map/ppermute | solution.py:400
  34.9 5.2 %collective-permute-start.9 = (f32[8,2,8,1024]{3,2,1,0:T(8,128)S(1)}, f32[8,2,8,1024]{3,2,1,0:T(8,128)S(1)}, u32[]{:S(2)}, u32[]{:S(2)}) collective-permute-start(f32[8,2,8,1024]{3,2,1,0:T(8,128)S(1)} %get-tuple-element.25.first_ref), channel_id=1, source_target_pairs={{1,0},{2,1},{3,2},{4,3},{5,4},{6,5},{7,6},{8,7},{9,8},{10,9},{11,1... | collective-permute-start | bytes 1572872 | tf_op jit(solution)/shard_map/ppermute | solution.py:405
  51.7 3.1 %collective-permute-done.15 = f32[72,128]{1,0:T(8,128)S(1)} collective-permute-done((f32[72,128]{1,0:T(8,128)S(1)}, f32[72,128]{1,0:T(8,128)S(1)}, u32[]{:S(2)}, u32[]{:S(2)}) %collective-permute-start.15) | collective-permute-done | bytes 36896 | tf_op jit(solution)/shard_map/ppermute | solution.py:409
  54.8 4.3 %collective-permute-done.16 = f32[72,128]{1,0:T(8,128)S(1)} collective-permute-done((f32[72,128]{1,0:T(8,128)S(1)}, f32[72,128]{1,0:T(8,128)S(1)}, u32[]{:S(2)}, u32[]{:S(2)}) %collective-permute-start.16) | collective-permute-done | bytes 36896 | tf_op jit(solution)/shard_map/ppermute | solution.py:409
  59.1 4.2 %collective-permute-done.17 = f32[72,128]{1,0:T(8,128)S(1)} collective-permute-done((f32[72,128]{1,0:T(8,128)S(1)}, f32[72,128]{1,0:T(8,128)S(1)}, u32[]{:S(2)}, u32[]{:S(2)}) %collective-permute-start.17) | collective-permute-done | bytes 36896 | tf_op jit(solution)/shard_map/ppermute | solution.py:409
  66.3 2.6 %collective-permute-done.19 = f32[72,128]{1,0:T(8,128)S(1)} collective-permute-done((f32[72,128]{1,0:T(8,128)S(1)}, f32[72,128]{1,0:T(8,128)S(1)}, u32[]{:S(2)}, u32[]{:S(2)}) %collective-permute-start.19) | collective-permute-done | bytes 36896 | tf_op jit(solution)/shard_map/ppermute | solution.py:409
  68.9 2.9 %collective-permute-start.20 = (f32[72,128]{1,0:T(8,128)S(1)}, f32[72,128]{1,0:T(8,128)S(1)}, u32[]{:S(2)}, u32[]{:S(2)}) collective-permute-start(f32[72,128]{1,0:T(8,128)S(1)} %add.62), channel_id=1, source_target_pairs={{0,3},{1,2},{2,1},{3,0},{4,7},{5,6},{6,5},{7,4},{8,11},{9,10},{10,... | collective-permute-start | bytes 110600 | tf_op jit(solution)/shard_map/ppermute | solution.py:409
  71.8 3.5 %collective-permute-start.7 = (f32[8,2,8,1024]{3,2,1,0:T(8,128)S(1)}, f32[8,2,8,1024]{3,2,1,0:T(8,128)S(1)}, u32[]{:S(2)}, u32[]{:S(2)}) collective-permute-start(f32[8,2,8,1024]{3,2,1,0:T(8,128)S(1)} %get-tuple-element.23.first_ref), channel_id=1, source_target_pairs={{1,0},{2,1},{3,2},{4,3},{5,4},{6,5},{7,6},{8,7},{9,8},{10,9},{11,1... | collective-permute-start | bytes 1572872 | tf_op jit(solution)/shard_map/ppermute | solution.py:405
  75.4 3.4 %copy-done.2 = f32[32,8,8,1024]{3,2,1,0:T(8,128)S(1)} copy-done((f32[32,8,8,1024]{3,2,1,0:T(8,128)S(1)}, f32[32,8,8,1024]{3,2,1,0:T(8,128)}, u32[]{:S(2)}) %copy-start.2) | copy-done | bytes 8388632
  82.9 5.5 %collective-permute-start.5 = (f32[8,2,8,1024]{3,2,1,0:T(8,128)}, f32[8,2,8,1024]{3,2,1,0:T(8,128)}, u32[]{:S(2)}, u32[]{:S(2)}) collective-permute-start(f32[8,2,8,1024]{3,2,1,0:T(8,128)} %get-tuple-element.21.first_ref), channel_id=1, source_target_pairs={{1,0},{2,1},{3,2},{4,3},{5,4},{6,5},{7,6},{8,7},{9,8},{10,9},{11,1... | collective-permute-start | bytes 1572872 | tf_op jit(solution)/shard_map/ppermute | solution.py:405
  91.2 5.5 %collective-permute-start.1 = (f32[8,2,8,1024]{3,2,1,0:T(8,128)}, f32[8,2,8,1024]{3,2,1,0:T(8,128)}, u32[]{:S(2)}, u32[]{:S(2)}) collective-permute-start(f32[8,2,8,1024]{3,2,1,0:T(8,128)} %get-tuple-element.17.first_ref), channel_id=1, source_target_pairs={{1,0},{2,1},{3,2},{4,3},{5,4},{6,5},{7,6},{8,7},{9,8},{10,9},{11,1... | collective-permute-start | bytes 1572872 | tf_op jit(solution)/shard_map/ppermute | solution.py:405
  97.5 6.1 %collective-permute-start.21 = (f32[72,128]{1,0:T(8,128)S(1)}, f32[72,128]{1,0:T(8,128)S(1)}, u32[]{:S(2)}, u32[]{:S(2)}) collective-permute-start(f32[72,128]{1,0:T(8,128)S(1)} %add.63), channel_id=1, source_target_pairs={{0,16},{16,0},{32,48},{48,32},{64,80},{80,64},{96,112},{112,96},{1... | collective-permute-start | bytes 110600 | tf_op jit(solution)/shard_map/ppermute | solution.py:409
  105.9 3.4 %copy-done.3 = f32[32,8,8,1024]{3,2,1,0:T(8,128)S(1)} copy-done((f32[32,8,8,1024]{3,2,1,0:T(8,128)S(1)}, f32[32,8,8,1024]{3,2,1,0:T(8,128)}, u32[]{:S(2)}) %copy-start.3) | copy-done | bytes 8388632
  109.3 4.8 %two_steps.4.rest_0_ = f32[2048,1024]{1,0:T(8,128)} custom-call(f32[2048,1024]{1,0:T(8,128)S(1)} %bitcast.29, f32[8,2,8,1024]{3,2,1,0:T(8,128)S(1)} %collective-permute-done.8.before_ref, f32[8,2,8,1024]{3,2,1,0:T(8,128)S(1)} %collective-permute-done.9.after_ref, f32[8,2,8,1024]{3,2,1,0:T(8,128)S(1)} %get-tuple-element.25.first_ref, ...), custom_call_target="tpu_custom_call" | custom-call | bytes 5242880 | tf_op jit(solution)/shard_map/two_steps/pallas_call | solution.py:160
  114.1 6.2 %two_steps.5.rest_0_ = f32[2048,1024]{1,0:T(8,128)} custom-call(f32[2048,1024]{1,0:T(8,128)S(1)} %bitcast.30, f32[8,2,8,1024]{3,2,1,0:T(8,128)S(1)} %copy-done.7, f32[8,2,8,1024]{3,2,1,0:T(8,128)S(1)} %copy-done.9, f32[8,2,8,1024]{3,2,1,0:T(8,128)S(1)} %get-tuple-element.23.first_ref, ...), custom_call_target="tpu_custom_call", output_to_operand_aliasing={{}: (8, {})} | custom-call | bytes 5242880 | tf_op jit(solution)/shard_map/two_steps/pallas_call | solution.py:160
  120.3 6.8 %two_steps.6.rest_0_ = f32[2048,1024]{1,0:T(8,128)} custom-call(f32[2048,1024]{1,0:T(8,128)S(1)} %bitcast.31, f32[8,2,8,1024]{3,2,1,0:T(8,128)} %collective-permute-done.4.before_ref, f32[8,2,8,1024]{3,2,1,0:T(8,128)} %collective-permute-done.5.after_ref, f32[8,2,8,1024]{3,2,1,0:T(8,128)} %get-tuple-element.21.first_ref, ...), custom_call_target="tpu_custom_call", output_to_operand_aliasing={{}: (8, {})} | custom-call | bytes 5242880 | tf_op jit(solution)/shard_map/two_steps/pallas_call | solution.py:160
  127.2 6.8 %two_steps.7 = f32[2048,1024]{1,0:T(8,128)} custom-call(f32[2048,1024]{1,0:T(8,128)S(1)} %bitcast.32, f32[8,2,8,1024]{3,2,1,0:T(8,128)} %collective-permute-done.before_ref, f32[8,2,8,1024]{3,2,1,0:T(8,128)} %collective-permute-done.1.after_ref, f32[8,2,8,1024]{3,2,1,0:T(8,128)} %get-tuple-element.17.first_ref, ...), custom_call_target="tpu_custom_call", output_to_operand_aliasing={{}: (8, {})} | custom-call | bytes 5242880 | tf_op jit(solution)/shard_map/two_steps/pallas_call | solution.py:160
  134.0 11.9 %analysis.1 = f32[8,128]{1,0:T(8,128)} custom-call(f32[144,128]{1,0:T(8,128)S(1)} %maximum_select_fusion.sums_ref, f32[3,32,16]{2,1,0:T(8,128)S(1)} %copy.12.m_ref, f32[128,1024]{1,0:T(8,128)S(1)} %get-tuple-element.28.s_ref, f32[8,128]{1,0:T(8,128)S(1)} %get-tuple-element.29.mean_ref), custom_call_target="tpu_custom_call" | custom-call | bytes 16777216 | tf_op jit(solution)/shard_map/analysis/pallas_call | solution.py:387
  (80 shorter events, 35.9 us)
Async XLA Ops:
  7.2 10.5 %collective-permute-start.2 = (f32[56,1024]{1,0:T(8,128)S(1)}, f32[56,1024]{1,0:T(8,128)S(1)}, u32[]{:S(2)}, u32[]{:S(2)}) collective-permute-start(f32[56,1024]{1,0:T(8,128)S(1)} %get-tuple-element.18.high_ref), channel_id=1, source_target_pairs={{0,1},{1,2},{2,3},{3,4},{4,5},{5,6},{6,7},{7,8},{8,9},{9,10},{10,1... | collective-permute-start | bytes 688136 | tf_op jit(solution)/shard_map/ppermute | solution.py:400
  10.3 8.2 %collective-permute-start.3 = (f32[56,1024]{1,0:T(8,128)S(1)}, f32[56,1024]{1,0:T(8,128)S(1)}, u32[]{:S(2)}, u32[]{:S(2)}) collective-permute-start(f32[56,1024]{1,0:T(8,128)S(1)} %get-tuple-element.19.low_ref), channel_id=1, source_target_pairs={{1,0},{2,1},{3,2},{4,3},{5,4},{6,5},{7,6},{8,7},{9,8},{10,9},{11,1... | collective-permute-start | bytes 688136 | tf_op jit(solution)/shard_map/ppermute | solution.py:405
  17.6 17.3 %copy-start.10 = (f32[56,1024]{1,0:T(8,128)}, f32[56,1024]{1,0:T(8,128)S(1)}, u32[]{:S(2)}) copy-start(f32[56,1024]{1,0:T(8,128)S(1)} %collective-permute-done.2.before_ref) | copy-start | bytes 688132
  18.5 16.4 %copy-start.11 = (f32[56,1024]{1,0:T(8,128)}, f32[56,1024]{1,0:T(8,128)S(1)}, u32[]{:S(2)}) copy-start(f32[56,1024]{1,0:T(8,128)S(1)} %collective-permute-done.3.after_ref) | copy-start | bytes 688132
  20.5 3.1 %collective-permute-start.10 = (f32[4,128,128]{2,1,0:T(8,128)S(1)}, f32[4,128,128]{2,1,0:T(8,128)S(1)}, u32[]{:S(2)}, u32[]{:S(2)}) collective-permute-start(f32[4,128,128]{2,1,0:T(8,128)S(1)} %get-tuple-element.34), channel_id=1, source_target_pairs={{0,16},{16,0},{32,48},{48,32},{64,80},{80,64},{96,112},{112,96},{1... | collective-permute-start | bytes 786440 | tf_op jit(solution)/shard_map/ppermute | solution.py:409
  24.4 20.6 %collective-permute-start.11 = (f32[2,128,128]{2,1,0:T(8,128)}, f32[2,128,128]{2,1,0:T(8,128)}, u32[]{:S(2)}, u32[]{:S(2)}) collective-permute-start(f32[2,128,128]{2,1,0:T(8,128)} %get-tuple-element.32), channel_id=1, source_target_pairs={{0,32},{16,48},{32,0},{48,16},{64,96},{80,112},{96,64},{112,80},{1... | collective-permute-start | bytes 393224 | tf_op jit(solution)/shard_map/ppermute | solution.py:409
  24.9 22.1 %collective-permute-start.12 = (f32[2,128,128]{2,1,0:T(8,128)}, f32[2,128,128]{2,1,0:T(8,128)}, u32[]{:S(2)}, u32[]{:S(2)}) collective-permute-start(f32[2,128,128]{2,1,0:T(8,128)} %get-tuple-element.33), channel_id=1, source_target_pairs={{0,64},{16,80},{32,96},{48,112},{64,0},{80,16},{96,32},{112,48},{1... | collective-permute-start | bytes 393224 | tf_op jit(solution)/shard_map/ppermute | solution.py:409
  25.5 21.4 %collective-permute-start.13 = (f32[2,128,128]{2,1,0:T(8,128)}, f32[2,128,128]{2,1,0:T(8,128)}, u32[]{:S(2)}, u32[]{:S(2)}) collective-permute-start(f32[2,128,128]{2,1,0:T(8,128)} %get-tuple-element.30), channel_id=1, source_target_pairs={{0,96},{16,112},{32,64},{48,80},{64,32},{80,48},{96,0},{112,16},{1... | collective-permute-start | bytes 393224 | tf_op jit(solution)/shard_map/ppermute | solution.py:409
  31.9 49.0 %collective-permute-start.8 = (f32[8,2,8,1024]{3,2,1,0:T(8,128)S(1)}, f32[8,2,8,1024]{3,2,1,0:T(8,128)S(1)}, u32[]{:S(2)}, u32[]{:S(2)}) collective-permute-start(f32[8,2,8,1024]{3,2,1,0:T(8,128)S(1)} %get-tuple-element.24.last_ref), channel_id=1, source_target_pairs={{0,1},{1,2},{2,3},{3,4},{4,5},{5,6},{6,7},{7,8},{8,9},{9,10},{10,1... | collective-permute-start | bytes 1572872 | tf_op jit(solution)/shard_map/ppermute | solution.py:400
  34.9 48.0 %collective-permute-start.9 = (f32[8,2,8,1024]{3,2,1,0:T(8,128)S(1)}, f32[8,2,8,1024]{3,2,1,0:T(8,128)S(1)}, u32[]{:S(2)}, u32[]{:S(2)}) collective-permute-start(f32[8,2,8,1024]{3,2,1,0:T(8,128)S(1)} %get-tuple-element.25.first_ref), channel_id=1, source_target_pairs={{1,0},{2,1},{3,2},{4,3},{5,4},{6,5},{7,6},{8,7},{9,8},{10,9},{11,1... | collective-permute-start | bytes 1572872 | tf_op jit(solution)/shard_map/ppermute | solution.py:405
  45.0 43.4 %collective-permute-start.6 = (f32[8,2,8,1024]{3,2,1,0:T(8,128)}, f32[8,2,8,1024]{3,2,1,0:T(8,128)S(1)}, u32[]{:S(2)}, u32[]{:S(2)}) collective-permute-start(f32[8,2,8,1024]{3,2,1,0:T(8,128)} %get-tuple-element.22.last_ref), channel_id=1, source_target_pairs={{0,1},{1,2},{2,3},{3,4},{4,5},{5,6},{6,7},{7,8},{8,9},{9,10},{10,1... | collective-permute-start | bytes 1572872 | tf_op jit(solution)/shard_map/ppermute | solution.py:400
  49.2 2.4 %collective-permute-start.14 = (f32[72,128]{1,0:T(8,128)S(1)}, f32[72,128]{1,0:T(8,128)S(1)}, u32[]{:S(2)}, u32[]{:S(2)}) collective-permute-start(f32[72,128]{1,0:T(8,128)S(1)} %dynamic-slice_bitcast_fusion.1), channel_id=1, source_target_pairs={{0,16},{16,0},{32,48},{48,32},{64,80},{80,64},{96,112},{112,96},{1... | collective-permute-start | bytes 110600 | tf_op jit(solution)/shard_map/ppermute | solution.py:409
  51.6 3.1 %collective-permute-start.15 = (f32[72,128]{1,0:T(8,128)S(1)}, f32[72,128]{1,0:T(8,128)S(1)}, u32[]{:S(2)}, u32[]{:S(2)}) collective-permute-start(f32[72,128]{1,0:T(8,128)S(1)} %bitcast_add_fusion), channel_id=1, source_target_pairs={{0,32},{16,48},{32,0},{48,16},{64,96},{80,112},{96,64},{112,80},{1... | collective-permute-start | bytes 110600 | tf_op jit(solution)/shard_map/ppermute | solution.py:409
  54.8 4.3 %collective-permute-start.16 = (f32[72,128]{1,0:T(8,128)S(1)}, f32[72,128]{1,0:T(8,128)S(1)}, u32[]{:S(2)}, u32[]{:S(2)}) collective-permute-start(f32[72,128]{1,0:T(8,128)S(1)} %add.58), channel_id=1, source_target_pairs={{0,96},{16,112},{32,64},{48,80},{64,32},{80,48},{96,0},{112,16},{1... | collective-permute-start | bytes 110600 | tf_op jit(solution)/shard_map/ppermute | solution.py:409
  59.1 4.2 %collective-permute-start.17 = (f32[72,128]{1,0:T(8,128)S(1)}, f32[72,128]{1,0:T(8,128)S(1)}, u32[]{:S(2)}, u32[]{:S(2)}) collective-permute-start(f32[72,128]{1,0:T(8,128)S(1)} %add.59), channel_id=1, source_target_pairs={{0,4},{1,5},{2,6},{3,7},{4,0},{5,1},{6,2},{7,3},{8,12},{9,13},{10,... | collective-permute-start | bytes 110600 | tf_op jit(solution)/shard_map/ppermute | solution.py:409
  63.3 2.8 %collective-permute-start.18 = (f32[72,128]{1,0:T(8,128)S(1)}, f32[72,128]{1,0:T(8,128)S(1)}, u32[]{:S(2)}, u32[]{:S(2)}) collective-permute-start(f32[72,128]{1,0:T(8,128)S(1)} %add.60), channel_id=1, source_target_pairs={{0,12},{1,13},{2,14},{3,15},{4,8},{5,9},{6,10},{7,11},{8,4},{9,5},... | collective-permute-start | bytes 110600 | tf_op jit(solution)/shard_map/ppermute | solution.py:409
  66.1 2.8 %collective-permute-start.19 = (f32[72,128]{1,0:T(8,128)S(1)}, f32[72,128]{1,0:T(8,128)S(1)}, u32[]{:S(2)}, u32[]{:S(2)}) collective-permute-start(f32[72,128]{1,0:T(8,128)S(1)} %add.61), channel_id=1, source_target_pairs={{0,1},{1,0},{2,3},{3,2},{4,5},{5,4},{6,7},{7,6},{8,9},{9,8},{10,11... | collective-permute-start | bytes 110600 | tf_op jit(solution)/shard_map/ppermute | solution.py:409
  68.9 22.2 %collective-permute-start.20 = (f32[72,128]{1,0:T(8,128)S(1)}, f32[72,128]{1,0:T(8,128)S(1)}, u32[]{:S(2)}, u32[]{:S(2)}) collective-permute-start(f32[72,128]{1,0:T(8,128)S(1)} %add.62), channel_id=1, source_target_pairs={{0,3},{1,2},{2,1},{3,0},{4,7},{5,6},{6,5},{7,4},{8,11},{9,10},{10,... | collective-permute-start | bytes 110600 | tf_op jit(solution)/shard_map/ppermute | solution.py:409
  71.8 24.8 %collective-permute-start.7 = (f32[8,2,8,1024]{3,2,1,0:T(8,128)S(1)}, f32[8,2,8,1024]{3,2,1,0:T(8,128)S(1)}, u32[]{:S(2)}, u32[]{:S(2)}) collective-permute-start(f32[8,2,8,1024]{3,2,1,0:T(8,128)S(1)} %get-tuple-element.23.first_ref), channel_id=1, source_target_pairs={{1,0},{2,1},{3,2},{4,3},{5,4},{6,5},{7,6},{8,7},{9,8},{10,9},{11,1... | collective-permute-start | bytes 1572872 | tf_op jit(solution)/shard_map/ppermute | solution.py:405
  81.0 39.4 %collective-permute-start.4 = (f32[8,2,8,1024]{3,2,1,0:T(8,128)}, f32[8,2,8,1024]{3,2,1,0:T(8,128)}, u32[]{:S(2)}, u32[]{:S(2)}) collective-permute-start(f32[8,2,8,1024]{3,2,1,0:T(8,128)} %get-tuple-element.20.last_ref), channel_id=1, source_target_pairs={{0,1},{1,2},{2,3},{3,4},{4,5},{5,6},{6,7},{7,8},{8,9},{9,10},{10,1... | collective-permute-start | bytes 1572872 | tf_op jit(solution)/shard_map/ppermute | solution.py:400
  82.9 37.4 %collective-permute-start.5 = (f32[8,2,8,1024]{3,2,1,0:T(8,128)}, f32[8,2,8,1024]{3,2,1,0:T(8,128)}, u32[]{:S(2)}, u32[]{:S(2)}) collective-permute-start(f32[8,2,8,1024]{3,2,1,0:T(8,128)} %get-tuple-element.21.first_ref), channel_id=1, source_target_pairs={{1,0},{2,1},{3,2},{4,3},{5,4},{6,5},{7,6},{8,7},{9,8},{10,9},{11,1... | collective-permute-start | bytes 1572872 | tf_op jit(solution)/shard_map/ppermute | solution.py:405
  89.2 37.9 %collective-permute-start = (f32[8,2,8,1024]{3,2,1,0:T(8,128)}, f32[8,2,8,1024]{3,2,1,0:T(8,128)}, u32[]{:S(2)}, u32[]{:S(2)}) collective-permute-start(f32[8,2,8,1024]{3,2,1,0:T(8,128)} %get-tuple-element.16.last_ref), channel_id=1, source_target_pairs={{0,1},{1,2},{2,3},{3,4},{4,5},{5,6},{6,7},{7,8},{8,9},{9,10},{10,1... | collective-permute-start | bytes 1572872 | tf_op jit(solution)/shard_map/ppermute | solution.py:400
  91.2 36.0 %collective-permute-start.1 = (f32[8,2,8,1024]{3,2,1,0:T(8,128)}, f32[8,2,8,1024]{3,2,1,0:T(8,128)}, u32[]{:S(2)}, u32[]{:S(2)}) collective-permute-start(f32[8,2,8,1024]{3,2,1,0:T(8,128)} %get-tuple-element.17.first_ref), channel_id=1, source_target_pairs={{1,0},{2,1},{3,2},{4,3},{5,4},{6,5},{7,6},{8,7},{9,8},{10,9},{11,1... | collective-permute-start | bytes 1572872 | tf_op jit(solution)/shard_map/ppermute | solution.py:405
  97.5 36.5 %collective-permute-start.21 = (f32[72,128]{1,0:T(8,128)S(1)}, f32[72,128]{1,0:T(8,128)S(1)}, u32[]{:S(2)}, u32[]{:S(2)}) collective-permute-start(f32[72,128]{1,0:T(8,128)S(1)} %add.63), channel_id=1, source_target_pairs={{0,16},{16,0},{32,48},{48,32},{64,80},{80,64},{96,112},{112,96},{1... | collective-permute-start | bytes 110600 | tf_op jit(solution)/shard_map/ppermute | solution.py:409
  (14 other events, 50.4 us)

commit v2 on v1

v2 whole, which is shorter than its diff:
```python
import functools

import jax
import jax.numpy as jnp
from jax import lax
from jax.experimental import pallas as pl
from jax.experimental.pallas import tpu as pltpu
from jax.sharding import PartitionSpec as P

HI = lax.Precision.HIGHEST
VMEM = pl.BlockSpec(memory_space=pltpu.VMEM)
SMEM = pl.BlockSpec(memory_space=pltpu.SMEM)
ANY = pl.BlockSpec(memory_space=pl.ANY)
HBM = pl.BlockSpec(memory_space=pltpu.HBM)
ROWS = 8
LIMIT = 16 << 20
LARGE = 105 << 19
CHUNKS = (2, 2)
F32 = jnp.float32


def shape(*dims):
    return jax.ShapeDtypeStruct(dims, F32)


def cost(nbytes, flops=0):
    return pl.CostEstimate(flops=flops, bytes_accessed=nbytes, transcendentals=0)


def params(limit=LIMIT):
    return pltpu.CompilerParams(vmem_limit_bytes=limit)


def lanes_sum(v):
    tiles = [v[:, t : t + 128] for t in range(0, v.shape[1], 128)]
    lane = lax.broadcasted_iota(jnp.int32, tiles[0].shape, 1)
    first, last = lane == 0, lane == 127
    ups = [jnp.zeros_like(tiles[0])] + [pltpu.roll(t, 1, 1) for t in tiles]
    downs = [pltpu.roll(t, 127, 1) for t in tiles] + [jnp.zeros_like(tiles[0])]
    out = [
        jnp.where(first, ups[t], ups[t + 1]) + jnp.where(last, downs[t + 1], downs[t])
        for t in range(len(tiles))
    ]
    return jnp.concatenate(out, 1)


def pair_kernel(slot_ref, k_ref, u_ref, sum_ref, low_ref, high_ref, pair_ref, seen_ref, order_ref, sem, k_sem):
    members, levels = u_ref.shape[:2]
    rank = sum_ref.shape[2]
    at = pl.ds(3 * rank, levels)
    turned = [
        pltpu.make_async_copy(k_ref.at[:, 0, :], low_ref.at[at], k_sem.at[0]),
        pltpu.make_async_copy(k_ref.at[:, ROWS - 1, :], high_ref.at[at], k_sem.at[1]),
    ]
    for copy in turned:
        copy.start()
    for s in range(rank):
        seen_ref[s] = 0

    def place(m, carry):
        s = slot_ref[m]
        which = jnp.minimum(seen_ref[s], 1)
        order_ref[2 * s + which] = m
        seen_ref[s] = which + 1
        return carry

    lax.fori_loop(0, members, place, 0)
    copies = [
        pltpu.make_async_copy(
            u_ref.at[order_ref[2 * s + i], pl.ds(levels - 3, 3)], pair_ref.at[i, :, :, s, :], sem.at[i, s]
        )
        for s in range(rank)
        for i in range(2)
    ]
    for copy in copies:
        copy.start()
    for copy in turned + copies:
        copy.wait()
    for l in range(3):
        for x in range(ROWS):
            sum_ref[l, x] = pair_ref[0, l, x] + pair_ref[1, l, x]
    for part, (level, x) in enumerate(((1, 0), (2, 0), (2, 1))):
        at = pl.ds(part * rank, rank)
        low_ref[at, :] = sum_ref[level, x]
        high_ref[at, :] = sum_ref[level, ROWS - 1 - x]


def pair_sums(prior, slots, k, rank):
    members, levels, rows, width = prior.shape
    edge = 3 * rank + levels
    return pl.pallas_call(
        pair_kernel,
        in_specs=[SMEM, HBM, HBM],
        out_specs=[VMEM] * 3,
        out_shape=[
            shape(3, rows, rank, width),
            shape(edge, width),
            shape(edge, width),
        ],
        scratch_shapes=[
            pltpu.VMEM((2, 3, rows, rank, width), F32),
            pltpu.SMEM((rank,), jnp.int32),
            pltpu.SMEM((members,), jnp.int32),
            pltpu.SemaphoreType.DMA((2, rank)),
            pltpu.SemaphoreType.DMA((2,)),
        ],
        compiler_params=params(54 << 20),
        cost_estimate=cost(6 << 20),
        name="pair_sums",
    )(slots, k, prior)


def pack_kernel(first, u_ref, *rest):
    low_ref, high_ref, sem = rest[-3:]
    groups, depth, _, span, _ = low_ref.shape
    copies = []
    for g in range(groups):
        for m in range(span):
            for r in range(depth):
                for side, (ref, x) in enumerate(((low_ref, r), (high_ref, ROWS - 1 - r))):
                    copies.append(
                        pltpu.make_async_copy(
                            u_ref.at[first + g * span + m, :, x, :], ref.at[g, r, :, m, :], sem.at[g, m, r, side]
                        )
                    )
    for copy in copies:
        copy.start()
    for copy in copies:
        copy.wait()


def pack(prior, first, groups, *tokens):
    levels, width = prior.shape[1], prior.shape[3]
    return pl.pallas_call(
        functools.partial(pack_kernel, first),
        in_specs=[HBM] + [ANY] * len(tokens),
        out_specs=[VMEM] * 2,
        out_shape=[shape(groups, 2, levels, 8, width)] * 2,
        scratch_shapes=[pltpu.SemaphoreType.DMA((groups, 8, 2, 2))],
        compiler_params=params(LARGE),
        cost_estimate=cost(groups << 21),
        name="pack_edges",
    )(prior, *tokens)


def step_kernel(first, u_ref, before_ref, after_ref, k_ref, kb_ref, ka_ref, *rest):
    out_ref, token_ref, u, v, w, in_sem, edge_sem, out_sem = rest[-8:]
    token_ref[...] = jnp.zeros_like(token_ref)
    levels, span, width = u_ref.shape[1], u.shape[3], u.shape[4]
    groups = before_ref.shape[0]
    part = levels // 4

    def fetch(g, p):
        slot = g % 2
        at, to = pl.ds(p * part, part), pl.ds(p * part + 1, part)
        copies = [
            pltpu.make_async_copy(
                u_ref.at[first + g * span + m, at], u.at[slot, to, pl.ds(2, ROWS), m, :], in_sem.at[slot, p, m]
            )
            for m in range(span)
        ]
        for r in range(2):
            for side, (ref, x) in enumerate(((before_ref, 1 - r), (after_ref, ROWS + 2 + r))):
                copies.append(
                    pltpu.make_async_copy(ref.at[g, r, at], u.at[slot, to, x], edge_sem.at[slot, p, r, side])
                )
        return copies

    def store(g, p):
        slot, at = g % 2, pl.ds(p * part, part)
        return [
            pltpu.make_async_copy(
                w.at[slot, at, :, m, :], out_ref.at[first + g * span + m, at], out_sem.at[slot, p, m]
            )
            for m in range(span)
        ]

    parts = levels // part
    for p in range(parts):
        for copy in fetch(0, p):
            copy.start()
    zero = jnp.zeros((span, width), F32)
    for l in (0, levels + 1):
        for x in range(ROWS + 4):
            for slot in range(u.shape[0]):
                u[slot, l, x] = zero
        for x in range(ROWS + 2):
            v[l, x] = zero
    tile = (span, 128)
    lane = lax.broadcasted_iota(jnp.int32, tile, 1)
    left, right = lane == 0, lane == 127

    def tiles(ref, l, x):
        return [ref[l, x, :, t : t + 128] for t in range(0, width, 128)]

    def one_step(src, l, x, rows, k):
        blank = jnp.zeros(tile, F32)
        before, here, after = rows
        ups = [blank] + [pltpu.roll(h, 1, 1) for h in here]
        downs = [pltpu.roll(h, 127, 1) for h in here] + [blank]
        out = []
        for t, h in enumerate(here):
            cut = pl.ds(t * 128, 128)
            total = (before[t] + after[t]) + (src[l - 1, x, :, cut] + src[l + 1, x, :, cut])
            total += jnp.where(left, ups[t], ups[t + 1]) + jnp.where(right, downs[t + 1], downs[t])
            out.append(h + k[:, t * 128 : t * 128 + 128] * (total - 6.0 * h))
        return out

    for g in range(groups):
        slot = g % 2
        if g + 1 < groups:
            for p in range(parts):
                for copy in fetch(g + 1, p):
                    copy.start()
        if g >= 2:
            for p in range(parts):
                for copy in store(g - 2, p):
                    copy.wait()

        def first_step(l):
            rows = [tiles(u.at[slot], l + 1, x) for x in range(2)]
            for x in range(-1, ROWS + 1):
                rows = rows[-2:] + [tiles(u.at[slot], l + 1, x + 3)]
                if x < 0:
                    k = kb_ref[l : l + 1, :]
                elif x == ROWS:
                    k = ka_ref[l : l + 1, :]
                else:
                    k = k_ref[l, x : x + 1, :]
                for t, tile_out in enumerate(one_step(u.at[slot], l + 1, x + 2, rows, k)):
                    v[l + 1, x + 1, :, t * 128 : t * 128 + 128] = tile_out

        def second_step(l):
            rows = [tiles(v, l + 1, x) for x in range(2)]
            for x in range(ROWS):
                rows = rows[-2:] + [tiles(v, l + 1, x + 2)]
                for t, tile_out in enumerate(one_step(v, l + 1, x + 1, rows, k_ref[l, x : x + 1, :])):
                    w[slot, l, x, :, t * 128 : t * 128 + 128] = tile_out

        for copy in fetch(g, 0):
            copy.wait()
        first_step(0)
        done = 0
        for p in range(parts):
            if p + 1 < parts:
                for copy in fetch(g, p + 1):
                    copy.wait()
            top = (p + 1) * part if p + 1 < parts else levels - 1
            for l in range(done + 1, top + 1):
                first_step(l)
                second_step(l - 1)
            done = top
            if p + 1 < parts:
                for copy in store(g, p):
                    copy.start()
        second_step(levels - 1)
        for copy in store(g, parts - 1):
            copy.start()
    for g in range(max(groups - 2, 0), groups):
        for p in range(parts):
            for copy in store(g, p):
                copy.wait()


def two_steps(prior, before, after, k, kb, ka, done, first, *tokens):
    members, levels, rows, width = prior.shape
    slots = min(before.shape[0], 2)
    operands = [prior, before, after, k, kb, ka]
    specs = [HBM] + [ANY] * 2 + [VMEM] * 3
    aliases = {}
    if done is not None:
        operands.append(done)
        specs.append(HBM)
        aliases = {6: 0}
    return pl.pallas_call(
        functools.partial(step_kernel, first),
        in_specs=specs + [ANY] * len(tokens),
        out_specs=[HBM, VMEM],
        out_shape=[shape(*prior.shape), shape(8, 128)],
        scratch_shapes=[
            pltpu.VMEM((slots, levels + 2, rows + 4, 8, width), F32),
            pltpu.VMEM((levels + 2, rows + 2, 8, width), F32),
            pltpu.VMEM((slots, levels, rows, 8, width), F32),
            pltpu.SemaphoreType.DMA((slots, 4, 8)),
            pltpu.SemaphoreType.DMA((slots, 4, 2, 2)),
            pltpu.SemaphoreType.DMA((slots, 4, 8)),
        ],
        input_output_aliases=aliases,
        compiler_params=params(LARGE),
        cost_estimate=cost(before.shape[0] << 23),
        name="two_steps",
    )(*operands, *tokens)


def surface_kernel(p_ref, before_ref, after_ref, k_ref, *rest):
    out_ref = rest[-1]
    rank = p_ref.shape[2]
    top = before_ref.shape[0] - 1

    def edge(ref, x):
        low, near, far = (ref[i * rank : (i + 1) * rank, :] for i in range(3))
        k = ref[top : top + 1, :]
        return near + k * (low + far + p_ref[2, x] + lanes_sum(near) - 6.0 * near)

    v6, v7 = [], [edge(before_ref, 0)]
    for x in range(ROWS):
        u6, u7 = p_ref[1, x], p_ref[2, x]

        def beside(level, part):
            before = p_ref[level, x - 1] if x > 0 else before_ref[part * rank : (part + 1) * rank, :]
            after = p_ref[level, x + 1] if x < ROWS - 1 else after_ref[part * rank : (part + 1) * rank, :]
            return before + after

        v6.append(u6 + k_ref[0, x : x + 1, :] * (beside(1, 0) + lanes_sum(u6) + p_ref[0, x] + u7 - 6.0 * u6))
        v7.append(u7 + k_ref[1, x : x + 1, :] * (beside(2, 1) + lanes_sum(u7) + u6 - 6.0 * u7))
    v7.append(edge(after_ref, ROWS - 1))
    piece = out_ref.shape[3]
    for x in range(ROWS):
        here = v7[x + 1]
        total = v7[x] + v7[x + 2] + lanes_sum(here) + v6[x]
        out = here + k_ref[1, x : x + 1, :] * (total - 6.0 * here)
        for g in range(out_ref.shape[0]):
            out_ref[g, x] = out[:, g * piece : (g + 1) * piece]


def surface(sums, before, after, k, groups, *tokens):
    _, rows, rank, width = sums.shape
    levels = k.shape[0]
    edge = pl.BlockSpec(before.shape, lambda i: (0, 0))
    return pl.pallas_call(
        surface_kernel,
        grid=(1,),
        in_specs=[
            pl.BlockSpec(sums.shape, lambda i: (0, 0, 0, 0)),
            edge,
            edge,
            pl.BlockSpec((2, rows, width), lambda i: (levels // 2 - 1, 0, 0)),
        ]
        + [ANY] * len(tokens),
        out_specs=pl.BlockSpec((groups, rows, rank, width // groups), lambda i: (0, 0, 0, 0)),
        out_shape=shape(groups, rows, rank, width // groups),
        compiler_params=params(),
        cost_estimate=cost(4 << 20),
        name="surface_steps",
    )(sums, before, after, k, *tokens)


def sensor_kernel(at_ref, cell_ref, value_ref, var_ref, m_ref, *rest):
    rank = m_ref.shape[2]
    out_ref, *mix_refs = rest[-1 - m_ref.shape[0] :]
    for level, ref in enumerate(mix_refs):
        ref[...] = jnp.zeros_like(ref)
        turned = m_ref[level].T
        for p in range(ref.shape[0] // rank):
            ref[p * rank : (p + 1) * rank, 2 * p * rank : 2 * (p + 1) * rank] = turned
    width, columns = 1024, out_ref.shape[1]
    rows = out_ref.shape[0] // 2
    chunks, span = cell_ref.shape
    weight = 1.0 / var_ref[...]
    local = cell_ref[...] - at_ref[0] * (rows * width)
    x = local // width
    y = local - x * width - at_ref[1] * columns
    left, right = [], []
    row = lax.broadcasted_iota(jnp.int32, (rows, span), 0)
    column = lax.broadcasted_iota(jnp.int32, (columns, span), 0)
    weighted = weight * value_ref[...]
    for c in range(chunks):
        hit = x[c : c + 1, :] == row
        left.append(
            jnp.concatenate(
                [jnp.where(hit, weight[c : c + 1, :], 0.0), jnp.where(hit, weighted[c : c + 1, :], 0.0)], 0
            )
        )
        right.append(jnp.where(y[c : c + 1, :] == column, 1.0, 0.0))
    out_ref[...] = lax.dot_general(
        jnp.concatenate(left, 1),
        jnp.concatenate(right, 1),
        (((1,), (1,)), ((), ())),
        precision=HI,
        preferred_element_type=F32,
    )


def sensors(place, cells, values, var, merge, columns, *tokens):
    rank = merge.shape[2]
    mixers = [shape(rank << i, 2 * rank << i) for i in range(merge.shape[0])][::-1]
    return pl.pallas_call(
        sensor_kernel,
        in_specs=[SMEM] + [VMEM] * 4 + [ANY] * len(tokens),
        out_specs=[VMEM] * (1 + len(mixers)),
        out_shape=[shape(16, columns)] + mixers,
        compiler_params=params(),
        cost_estimate=cost(4 << 20),
        name="sensor_sums",
    )(place, *(a.reshape(-1, 128) for a in (cells, values, var)), merge, *tokens)


def gram_kernel(place_ref, obs_ref, own_ref, r1_ref, r2_ref, r3_ref, *rest):
    sums_ref, s_ref, mean_ref, raw_ref = rest[-4:]
    chip, core = place_ref[1] // 2, place_ref[1] % 2
    for d, ref in ((0, own_ref), (1, r1_ref), (2, r2_ref), (3, r3_ref)):
        for slot in range(2):
            group = jnp.bitwise_xor(chip, d) * 2 + jnp.bitwise_xor(core, slot)
            rank = ref.shape[2]
            at = pl.ds(pl.multiple_of(group * rank, rank), rank)
            for x in range(ROWS):
                raw_ref[x, at, :] = ref[slot, x]
    total = None
    sketches = raw_ref.shape[1]
    member_total = 2 * sketches
    for x in range(0, 8, 2):
        both, means, weights, values = [], [], [], []
        for i in (x, x + 1):
            raw = raw_ref[i]
            mean = jnp.sum(raw, axis=0, keepdims=True) * (1.0 / member_total)
            dev = raw - 2.0 * mean
            s_ref[:, i * 128 : (i + 1) * 128] = dev
            mean_ref[i : i + 1, :] = mean
            both.append(dev)
            w = obs_ref[i : i + 1, :]
            weights.append(w)
            values.append(obs_ref[8 + i : 9 + i, :] - mean * w)
        dev = jnp.concatenate(both, 1)
        w = jnp.concatenate(weights, 1)
        z = jnp.broadcast_to(jnp.concatenate(values, 1), (8, dev.shape[1]))
        left = jnp.concatenate([dev, dev * w, z], 0)
        part = lax.dot_general(left, dev, (((1,), (1,)), ((), ())), precision=HI, preferred_element_type=F32)
        total = part if total is None else total + part
    gram, weighted, rhs = total[:sketches], total[sketches : 2 * sketches], total[2 * sketches :]
    row = lax.broadcasted_iota(jnp.int32, gram.shape, 0)
    lane = lax.broadcasted_iota(jnp.int32, gram.shape, 1)
    sums_ref[0:sketches, :] = jnp.where(lane > row, gram, weighted)
    sums_ref[sketches : sketches + 8, :] = jnp.broadcast_to(
        jnp.sum(jnp.where(lane == row, gram, 0.0), axis=0, keepdims=True), (8, 128)
    )
    sums_ref[sketches + 8 : sketches + 16, :] = rhs


def gram(place, obs, own, r1, r2, r3, *tokens):
    return pl.pallas_call(
        gram_kernel,
        in_specs=[SMEM] + [VMEM] * 5 + [ANY] * len(tokens),
        out_specs=[VMEM] * 3,
        out_shape=[shape(144, 128), shape(128, 1024), shape(8, 128)],
        scratch_shapes=[pltpu.VMEM((8, 128, 128), F32)],
        compiler_params=params(),
        cost_estimate=cost(4 << 20),
        name="gram_sums",
    )(place, obs, own, r1, r2, r3, *tokens)


def dot(a, b, ca=1, cb=0):
    return lax.dot_general(a, b, (((ca,), (cb,)), ((), ())), precision=HI, preferred_element_type=F32)


def analysis_kernel(sums_ref, mix0_ref, mix1_ref, mix2_ref, s_ref, mean_ref, out_ref):
    n = 128
    mixers = (mix0_ref, mix1_ref, mix2_ref)
    rank = mix2_ref.shape[0]
    packed = sums_ref[0:n, :]
    row = lax.broadcasted_iota(jnp.int32, (n, n), 0)
    lane = lax.broadcasted_iota(jnp.int32, (n, n), 1)
    upper = jnp.where(lane > row, packed, 0.0)
    lower = jnp.where(lane < row, packed, 0.0)
    g = upper + upper.T + jnp.where(lane == row, sums_ref[n : n + 1, :], 0.0)
    h = lower + lower.T + jnp.where(lane == row, packed, 0.0)
    q = sums_ref[n + 8 : n + 9, :]

    block = (rank, n)
    sub = lax.broadcasted_iota(jnp.int32, block, 0)
    at = lax.broadcasted_iota(jnp.int32, block, 1)
    unit = jnp.where(at % rank == sub, 1.0, 0.0)

    def eliminate(d, extra, visit=None):
        columns = [jnp.take_along_axis(d, at // rank * rank + j, axis=1) for j in range(rank)]
        for j in range(rank):
            c = columns[j]
            inverse = 1.0 / c[j : j + 1, :]
            if visit is not None:
                visit(j, inverse, extra)
            if j == rank - 1:
                break
            factor = jnp.where(sub > j, c * inverse, 0.0)
            for k in range(j + 1, rank):
                columns[k] = columns[k] - factor * c[k : k + 1, :]
            extra = [e - factor * e[j : j + 1, :] for e in extra]
        return extra

    def widened(v):
        if v.shape[1] == n:
            return v
        return jnp.concatenate([v, jnp.zeros((rank, n - v.shape[1]), F32)], 1) + jnp.where(
            at >= v.shape[1], unit, 0.0
        )

    c = g
    w = None
    for mix_ref in mixers:
        size = c.shape[0]
        d = jnp.zeros((rank, size), F32)
        for b in range(size // rank):
            d = d + jnp.where(at[:, :size] // rank == b, c[b * rank : (b + 1) * rank, :], 0.0)
        (t,) = eliminate(widened(d), [unit])
        t = jnp.concatenate([t[:, :size]] * (size // rank), 0)
        t = jnp.where(row[:size, :size] // rank == lane[:size, :size] // rank, t, 0.0)
        x = dot(mix_ref[...], t)
        c = dot(dot(x, c), x, 1, 1)
        w = x if w is None else dot(x, w)
    h3 = dot(dot(w, h), w, 1, 1)
    (t3,) = eliminate(widened(c), [unit])
    t3 = t3[:, :rank]
    basis_map = dot(t3, w)
    eye = unit[:, :rank]
    system = 255.0 * eye + dot(dot(t3, h3), t3, 1, 1)
    rhs = jnp.broadcast_to(jnp.sum(basis_map * q, axis=1, keepdims=True), block)
    found = []

    def visit(j, inverse, extra):
        y, v = extra
        found.append((y[j : j + 1, :] * inverse[:, 0:1]) * v[j : j + 1, :])

    eliminate(jnp.concatenate([system] * (n // rank), 1), [rhs, basis_map], visit)
    weights = found[0]
    for part in found[1:]:
        weights = weights + part
    increment = dot(jnp.broadcast_to(weights, (8, n)), s_ref[...])
    for i in range(8):
        out_ref[i : i + 1, :] = mean_ref[i : i + 1, :] + increment[0:1, i * 128 : (i + 1) * 128]


def analysis(sums, mixers, s, mean):
    return pl.pallas_call(
        analysis_kernel,
        in_specs=[VMEM] * 6,
        out_specs=VMEM,
        out_shape=shape(8, 128),
        compiler_params=params(),
        cost_estimate=cost(16 << 20),
        name="analysis",
    )(sums, *mixers, s, mean)


def add_kernel(a_ref, b_ref, c_ref, d_ref, *rest):
    rest[-1][...] = (a_ref[...] + b_ref[...]) + (c_ref[...] + d_ref[...])


def add_up(a, b, c, d, *tokens):
    return pl.pallas_call(
        add_kernel,
        in_specs=[VMEM] * 4 + [ANY] * len(tokens),
        out_specs=VMEM,
        out_shape=shape(*a.shape),
        compiler_params=params(),
        cost_estimate=cost(1 << 18),
        name="add_up",
    )(a, b, c, d, *tokens)


def to_next(v):
    size = lax.axis_size("tile")
    return lax.ppermute(v, "tile", [(i, i + 1) for i in range(size - 1)])


def to_previous(v):
    size = lax.axis_size("tile")
    return lax.ppermute(v, "tile", [(i + 1, i) for i in range(size - 1)])


def across(v, axis, bits):
    return lax.ppermute(v, axis, [(i, i ^ bits) for i in range(lax.axis_size(axis))])


def local(prior, k, slots, merge, cells, values, var):
    members, levels, rows, width = prior.shape
    rank = merge.shape[2]
    groups = lax.axis_size("grp")
    tile, group = lax.axis_index("tile"), lax.axis_index("grp")
    chip, core = group // 2, group % 2
    place = jnp.stack([tile, group]).astype(jnp.int32)
    sums, low, high = pair_sums(prior, slots, k, rank)
    before = to_next(high)
    after = to_previous(low)
    kb, ka = before[3 * rank :], after[3 * rank :]

    lo, hi = pack(prior, 0, CHUNKS[0], low)
    arrived_a = to_next(hi), to_previous(lo)
    obs, *mixers = sensors(place, cells, values, var, merge, width // groups, lo)
    pieces = surface(sums, before, after, k, groups, obs)
    pieces = pieces.reshape(groups // 2, 2, rows, rank, width // groups)

    mine = lax.dynamic_index_in_dim(pieces, core, 1, False)
    other = lax.dynamic_index_in_dim(pieces, 1 - core, 1, False)
    pairs = jnp.stack([mine, across(other, "grp", 1)], 1)

    def pair_for(bits):
        return lax.dynamic_index_in_dim(pairs, chip ^ bits, 0, False)

    own = pair_for(0)
    r1, r3, r2 = (across(pair_for(bits), "grp", 2 * bits) for bits in (1, 3, 2))
    lo, hi = pack(prior, 8 * CHUNKS[0], CHUNKS[1], own)
    part, sketches, mean = gram(place, obs, own, r1, r2, r3, lo)
    lo, hi, part = lax.optimization_barrier((lo, hi, part))

    half = part.reshape(2, -1, part.shape[1])
    total = lax.dynamic_index_in_dim(half, core, 0, False) + across(
        lax.dynamic_index_in_dim(half, 1 - core, 0, False), "grp", 1
    )

    def others(v, axis, near):
        return [across(v, axis, near * bits) for bits in (1, 2, 3)]

    arrived_b = to_next(hi), to_previous(lo)
    parts = others(total, "grp", 2)
    out, done = two_steps(prior, *arrived_a, k, kb, ka, None, 0, part)
    total = add_up(total, *parts, done)
    total = add_up(total, *others(total, "tile", 4), *arrived_b)
    parts = others(total, "tile", 1)
    out, done = two_steps(prior, *arrived_b, k, kb, ka, out, 8 * CHUNKS[0], total)
    total = add_up(total, *parts, done)
    second = across(total, "grp", 1)
    both = jnp.where(core == 0, jnp.concatenate([total, second], 0), jnp.concatenate([second, total], 0))
    posterior = analysis(both, mixers, sketches, mean)
    return out, posterior


def solution(mesh):
    in_specs = (P("grp", None, "tile", None), P(None, "tile", None), P("grp"), P(), P(), P(), P())
    out_specs = (P("grp", None, "tile", None), P("tile", "grp"))
    return jax.shard_map(local, mesh=mesh, in_specs=in_specs, out_specs=out_specs, check_vma=False)
```

time: 148 us -> 105 us (0.71)
  the two profiles are of different devices: /device:TPU:57 before, /device:TPU:1 now
where the time goes in v2:
time: 105 us; the launch traced here: 104 us
  starting transfers between devices  40.9 us (39%)
  Pallas kernels  39.2 us (37%)
  waiting for transfers between devices  21.1 us (20%)
  local copies, waits for them, and re-layouts  1.76 us (2%)
    ppermute x15, starting transfers between devices, across(): lax.ppermute(v, axis, [(i, i ^ bits) for i in range(lax.axis_size(axis))])  25.7 us
    pallas_call x2, Pallas kernels, two_steps(): pl.pallas_call(functools.partial(step_kernel, first), in_specs=specs + [A...  18.6 us
    ppermute x15, waiting for transfers between devices, across(): lax.ppermute(v, axis, [(i, i ^ bits) for i in range(lax.axis_size(axis))])  14.2 us
    ppermute x3, starting transfers between devices, to_next(): return lax.ppermute(v, 'tile', [(i, i + 1) for i in range(size - 1)])  11.3 us
    pallas_call x2, Pallas kernels, pack(): pl.pallas_call(functools.partial(pack_kernel, first), in_specs=[HBM] + [A...  6.03 us
    pallas_call x1, Pallas kernels, pair_sums(): pl.pallas_call(pair_kernel, in_specs=[SMEM, HBM, HBM], out_specs=[VMEM] *...  4.94 us
    ppermute x3, waiting for transfers between devices, to_next(): return lax.ppermute(v, 'tile', [(i, i + 1) for i in range(size - 1)])  4.6 us
    pallas_call x1, Pallas kernels, analysis(): pl.pallas_call(analysis_kernel, in_specs=[VMEM] * 6, out_specs=VMEM, out_...  4.19 us
  transfers between devices with their start and end apart: 21, of which 8 were waited for; matrix products, arithmetic and copies ran while one was open for 0% of the time, Pallas kernels for 28%

profile of v2, /device:TPU:1, one launch (start us, length us, event | category | flops | bytes accessed | tf_op | source)
XLA Modules:
  0.0 104.0 jit_solution(7045443850522869855)
XLA Ops:
  0.7 4.9 %pair_sums.1 = (f32[3,8,16,1024]{3,2,1,0:T(8,128)}, f32[56,1024]{1,0:T(8,128)}, f32[56,1024]{1,0:T(8,128)}) custom-call(s32[32]{0:T(128)} %slot_ref.1, f32[8,8,1024]{2,1,0:T(8,128)} %k_ref.7, f32[32,8,8,1024]{3,2,1,0:T(8,128)} %u_ref.9), custom_call_target="tpu_custom_call" | custom-call | bytes 6291456 | tf_op jit(solution)/shard_map/pair_sums/pallas_call | solution.py:91
  5.6 4.1 %collective-permute-start = (f32[56,1024]{1,0:T(8,128)}, f32[56,1024]{1,0:T(8,128)S(1)}, u32[]{:S(2)}, u32[]{:S(2)}) collective-permute-start(f32[56,1024]{1,0:T(8,128)} %get-tuple-element.24), channel_id=1, source_target_pairs={{0,1},{1,2},{2,3},{3,4},{4,5},{5,6},{6,7},{7,8},{8,9},{9,10},{10,1... | collective-permute-start | bytes 688136 | tf_op jit(solution)/shard_map/ppermute | solution.py:561
  9.7 1.3 %collective-permute-start.1 = (f32[56,1024]{1,0:T(8,128)}, f32[56,1024]{1,0:T(8,128)S(1)}, u32[]{:S(2)}, u32[]{:S(2)}) collective-permute-start(f32[56,1024]{1,0:T(8,128)} %get-tuple-element.25.rest_0_), channel_id=1, source_target_pairs={{1,0},{2,1},{3,2},{4,3},{5,4},{6,5},{7,6},{8,7},{9,8},{10,9},{11,1... | collective-permute-start | bytes 688136 | tf_op jit(solution)/shard_map/ppermute | solution.py:566
  12.0 3.0 %pack_edges.2 = (f32[2,2,8,8,1024]{4,3,2,1,0:T(8,128)S(1)}, f32[2,2,8,8,1024]{4,3,2,1,0:T(8,128)}) custom-call(f32[32,8,8,1024]{3,2,1,0:T(8,128)} %u_ref.9, f32[56,1024]{1,0:T(8,128)S(1)} %copy-done.3), custom_call_target="tpu_custom_call" | custom-call | bytes 4194304 | tf_op jit(solution)/shard_map/pack_edges/pallas_call | solution.py:134
  15.2 2.4 %sensor_sums.1 = (f32[16,128]{1,0:T(8,128)S(1)}, f32[64,128]{1,0:T(8,128)S(1)}, f32[32,64]{1,0:T(8,128)S(1)}, f32[16,32]{1,0:T(8,128)S(1)}) custom-call(s32[2]{0:T(128)S(1)} %pad_add_fusion.at_ref.place_ref, s32[32,128]{1,0:T(8,128)S(1)} %bitcast.25, f32[32,128]{1,0:T(8,128)S(1)} %bitcast.26, f32[32,128]{1,0:T(8,128)S(1)} %bitcast.27, ...), custom_call_target="tpu_custom_call" | custom-call | bytes 4194304 | tf_op jit(solution)/shard_map/sensor_sums/pallas_call | solution.py:387
  19.3 1.9 %collective-permute-start.2 = (f32[4,8,16,128]{3,2,1,0:T(8,128)S(1)}, f32[4,8,16,128]{3,2,1,0:T(8,128)S(1)}, u32[]{:S(2)}, u32[]{:S(2)}) collective-permute-start(f32[4,8,16,128]{3,2,1,0:T(8,128)S(1)} %get-tuple-element.48), channel_id=1, source_target_pairs={{0,16},{16,0},{32,48},{48,32},{64,80},{80,64},{96,112},{112,96},{1... | collective-permute-start | bytes 786440 | tf_op jit(solution)/shard_map/ppermute | solution.py:570
  22.5 2.8 %collective-permute-start.5 = (f32[2,8,16,128]{3,2,1,0:T(8,128)S(1)}, f32[2,8,16,128]{3,2,1,0:T(8,128)S(1)}, u32[]{:S(2)}, u32[]{:S(2)}) collective-permute-start(f32[2,8,16,128]{3,2,1,0:T(8,128)S(1)} %get-tuple-element.44), channel_id=1, source_target_pairs={{0,96},{16,112},{32,64},{48,80},{64,32},{80,48},{96,0},{112,16},{1... | collective-permute-start | bytes 393224 | tf_op jit(solution)/shard_map/ppermute | solution.py:570
  26.6 3.2 %collective-permute-start.8 = (f32[2,2,8,8,1024]{4,3,2,1,0:T(8,128)}, f32[2,2,8,8,1024]{4,3,2,1,0:T(8,128)S(1)}, u32[]{:S(2)}, u32[]{:S(2)}) collective-permute-start(f32[2,2,8,8,1024]{4,3,2,1,0:T(8,128)} %get-tuple-element.33), channel_id=1, source_target_pairs={{0,1},{1,2},{2,3},{3,4},{4,5},{5,6},{6,7},{7,8},{8,9},{9,10},{10,1... | collective-permute-start | bytes 3145736 | tf_op jit(solution)/shard_map/ppermute | solution.py:561
  29.7 1.3 %collective-permute-start.9 = (f32[2,2,8,8,1024]{4,3,2,1,0:T(8,128)S(1)}, f32[2,2,8,8,1024]{4,3,2,1,0:T(8,128)S(1)}, u32[]{:S(2)}, u32[]{:S(2)}) collective-permute-start(f32[2,2,8,8,1024]{4,3,2,1,0:T(8,128)S(1)} %get-tuple-element.26.rest_0_), channel_id=1, source_target_pairs={{1,0},{2,1},{3,2},{4,3},{5,4},{6,5},{7,6},{8,7},{9,8},{10,9},{11,1... | collective-permute-start | bytes 3145736 | tf_op jit(solution)/shard_map/ppermute | solution.py:566
  31.0 3.0 %pack_edges.3 = (f32[2,2,8,8,1024]{4,3,2,1,0:T(8,128)S(1)}, f32[2,2,8,8,1024]{4,3,2,1,0:T(8,128)}) custom-call(f32[32,8,8,1024]{3,2,1,0:T(8,128)} %u_ref.9, f32[2,8,16,128]{3,2,1,0:T(8,128)S(1)} %get-tuple-element.45.rest_0_.own_ref), custom_call_target="tpu_custom_call" | custom-call | bytes 4194304 | tf_op jit(solution)/shard_map/pack_edges/pallas_call | solution.py:134
  34.1 1.7 %gram_sums.1 = (f32[144,128]{1,0:T(8,128)S(1)}, f32[128,1024]{1,0:T(8,128)S(1)}, f32[8,128]{1,0:T(8,128)S(1)}) custom-call(s32[2]{0:T(128)S(1)} %pad_add_fusion.at_ref.place_ref, f32[16,128]{1,0:T(8,128)S(1)} %get-tuple-element.27.rest_0_.obs_ref, f32[2,8,16,128]{3,2,1,0:T(8,128)S(1)} %get-tuple-element.45.rest_0_.own_ref, ...), custom_call_target="tpu_custom_call" | custom-call | bytes 4194304 | tf_op jit(solution)/shard_map/gram_sums/pallas_call | solution.py:440
  35.8 4.1 %collective-permute-start.6 = (f32[2,2,8,8,1024]{4,3,2,1,0:T(8,128)}, f32[2,2,8,8,1024]{4,3,2,1,0:T(8,128)S(1)}, u32[]{:S(2)}, u32[]{:S(2)}) collective-permute-start(f32[2,2,8,8,1024]{4,3,2,1,0:T(8,128)} %get-tuple-element.31), channel_id=1, source_target_pairs={{0,1},{1,2},{2,3},{3,4},{4,5},{5,6},{6,7},{7,8},{8,9},{9,10},{10,1... | collective-permute-start | bytes 3145736 | tf_op jit(solution)/shard_map/ppermute | solution.py:561
  39.9 1.3 %collective-permute-start.7 = (f32[2,2,8,8,1024]{4,3,2,1,0:T(8,128)S(1)}, f32[2,2,8,8,1024]{4,3,2,1,0:T(8,128)S(1)}, u32[]{:S(2)}, u32[]{:S(2)}) collective-permute-start(f32[2,2,8,8,1024]{4,3,2,1,0:T(8,128)S(1)} %get-tuple-element.32.rest_0_), channel_id=1, source_target_pairs={{1,0},{2,1},{3,2},{4,3},{5,4},{6,5},{7,6},{8,7},{9,8},{10,9},{11,1... | collective-permute-start | bytes 3145736 | tf_op jit(solution)/shard_map/ppermute | solution.py:566
  41.2 2.0 %collective-permute-start.10 = (f32[72,128]{1,0:T(8,128)S(1)}, f32[72,128]{1,0:T(8,128)S(1)}, u32[]{:S(2)}, u32[]{:S(2)}) collective-permute-start(f32[72,128]{1,0:T(8,128)S(1)} %dynamic-slice_bitcast_fusion.1), channel_id=1, source_target_pairs={{0,16},{16,0},{32,48},{48,32},{64,80},{80,64},{96,112},{112,96},{1... | collective-permute-start | bytes 110600 | tf_op jit(solution)/shard_map/ppermute | solution.py:570
  44.0 2.7 %collective-permute-start.13 = (f32[72,128]{1,0:T(8,128)S(1)}, f32[72,128]{1,0:T(8,128)S(1)}, u32[]{:S(2)}, u32[]{:S(2)}) collective-permute-start(f32[72,128]{1,0:T(8,128)S(1)} %bitcast_add_fusion.a_ref), channel_id=1, source_target_pairs={{0,96},{16,112},{32,64},{48,80},{64,32},{80,48},{96,0},{112,16},{1... | collective-permute-start | bytes 110600 | tf_op jit(solution)/shard_map/ppermute | solution.py:570
  46.8 4.6 %collective-permute-done.8.before_ref = f32[2,2,8,8,1024]{4,3,2,1,0:T(8,128)S(1)} collective-permute-done((f32[2,2,8,8,1024]{4,3,2,1,0:T(8,128)}, f32[2,2,8,8,1024]{4,3,2,1,0:T(8,128)S(1)}, u32[]{:S(2)}, u32[]{:S(2)}) %collective-permute-start.8) | collective-permute-done | bytes 1048608 | tf_op jit(solution)/shard_map/ppermute | solution.py:561
  51.4 1.7 %collective-permute-start.12 = (f32[72,128]{1,0:T(8,128)S(1)}, f32[72,128]{1,0:T(8,128)S(1)}, u32[]{:S(2)}, u32[]{:S(2)}) collective-permute-start(f32[72,128]{1,0:T(8,128)S(1)} %bitcast_add_fusion.a_ref), channel_id=1, source_target_pairs={{0,64},{16,80},{32,96},{48,112},{64,0},{80,16},{96,32},{112,48},{1... | collective-permute-start | bytes 110600 | tf_op jit(solution)/shard_map/ppermute | solution.py:570
  53.1 1.9 %collective-permute-done.9.after_ref = f32[2,2,8,8,1024]{4,3,2,1,0:T(8,128)S(1)} collective-permute-done((f32[2,2,8,8,1024]{4,3,2,1,0:T(8,128)S(1)}, f32[2,2,8,8,1024]{4,3,2,1,0:T(8,128)S(1)}, u32[]{:S(2)}, u32[]{:S(2)}) %collective-permute-start.9) | collective-permute-done | bytes 1048608 | tf_op jit(solution)/shard_map/ppermute | solution.py:566
  55.9 9.3 %two_steps.2 = (f32[32,8,8,1024]{3,2,1,0:T(8,128)}, f32[8,128]{1,0:T(8,128)S(1)}) custom-call(f32[32,8,8,1024]{3,2,1,0:T(8,128)} %u_ref.9, f32[2,2,8,8,1024]{4,3,2,1,0:T(8,128)S(1)} %collective-permute-done.8.before_ref, f32[2,2,8,8,1024]{4,3,2,1,0:T(8,128)} %copy-done.7, f32[8,8,1024]{2,1,0:T(8,128)S(1)} %copy-done, f32[8,1024]{1,0:T(8,128)S(1)} %slice.8.kb_ref, ...), custom_call_target="tpu_custom_call" | custom-call | bytes 16777216 | tf_op jit(solution)/shard_map/two_steps/pallas_call | solution.py:275
  65.3 7.3 %collective-permute-start.16 = (f32[72,128]{1,0:T(8,128)S(1)}, f32[72,128]{1,0:T(8,128)S(1)}, u32[]{:S(2)}, u32[]{:S(2)}) collective-permute-start(f32[72,128]{1,0:T(8,128)S(1)} %add_up.3.a_ref), channel_id=1, source_target_pairs={{0,12},{1,13},{2,14},{3,15},{4,8},{5,9},{6,10},{7,11},{8,4},{9,5},... | collective-permute-start | bytes 110600 | tf_op jit(solution)/shard_map/ppermute | solution.py:570
  74.0 10.6 %collective-permute-done.15.c_ref = f32[72,128]{1,0:T(8,128)S(1)} collective-permute-done((f32[72,128]{1,0:T(8,128)S(1)}, f32[72,128]{1,0:T(8,128)S(1)}, u32[]{:S(2)}, u32[]{:S(2)}) %collective-permute-start.15) | collective-permute-done | bytes 36896 | tf_op jit(solution)/shard_map/ppermute | solution.py:570
  84.6 3.1 %collective-permute-start.19 = (f32[72,128]{1,0:T(8,128)S(1)}, f32[72,128]{1,0:T(8,128)S(1)}, u32[]{:S(2)}, u32[]{:S(2)}) collective-permute-start(f32[72,128]{1,0:T(8,128)S(1)} %add_up.4.rest_1_.a_ref), channel_id=1, source_target_pairs={{0,3},{1,2},{2,1},{3,0},{4,7},{5,6},{6,5},{7,4},{8,11},{9,10},{10,... | collective-permute-start | bytes 110600 | tf_op jit(solution)/shard_map/ppermute | solution.py:570
  88.4 9.3 %two_steps.3 = (f32[32,8,8,1024]{3,2,1,0:T(8,128)}, f32[8,128]{1,0:T(8,128)S(1)}) custom-call(f32[32,8,8,1024]{3,2,1,0:T(8,128)} %u_ref.9, f32[2,2,8,8,1024]{4,3,2,1,0:T(8,128)S(1)} %collective-permute-done.6.rest_0_.before_ref, f32[2,2,8,8,1024]{4,3,2,1,0:T(8,128)} %copy-done.1, f32[8,8,1024]{2,1,0:T(8,128)S(1)} %copy-done, ...), custom_call_target="tpu_custom_call", output_to_operand_aliasing={{0}: (6, {})} | custom-call | bytes 16777216 | tf_op jit(solution)/shard_map/two_steps/pallas_call | solution.py:275
  99.8 4.2 %analysis.1 = f32[8,128]{1,0:T(8,128)} custom-call(f32[144,128]{1,0:T(8,128)S(1)} %maximum_select_fusion.sums_ref, f32[64,128]{1,0:T(8,128)S(1)} %get-tuple-element.39.mix0_ref, f32[32,64]{1,0:T(8,128)S(1)} %get-tuple-element.40.mix1_ref, f32[16,32]{1,0:T(8,128)S(1)} %get-tuple-element.41.mix2_ref, f32[128,1024]{1,0:T(8,128)S(1)} %get-tuple-element.42.s_ref, ...), custom_call_target="tpu_custom_call" | custom-call | bytes 16777216 | tf_op jit(solution)/shard_map/analysis/pallas_call | solution.py:532
  (57 shorter events, 11.3 us)
Async XLA Ops:
  0.6 17.4 %copy-start = (f32[8,8,1024]{2,1,0:T(8,128)S(1)}, f32[8,8,1024]{2,1,0:T(8,128)}, u32[]{:S(2)}) copy-start(f32[8,8,1024]{2,1,0:T(8,128)} %k_ref.7) | copy-start | bytes 786436
  0.7 14.5 %copy-start.6 = (f32[4096]{0:T(1024)S(1)}, f32[4096]{0:T(1024)}, u32[]{:S(2)}) copy-start(f32[4096]{0:T(1024)} %param.13) | copy-start | bytes 49156
  0.7 14.5 %copy-start.5 = (f32[4096]{0:T(1024)S(1)}, f32[4096]{0:T(1024)}, u32[]{:S(2)}) copy-start(f32[4096]{0:T(1024)} %param.12) | copy-start | bytes 49156
  5.6 11.9 %collective-permute-start = (f32[56,1024]{1,0:T(8,128)}, f32[56,1024]{1,0:T(8,128)S(1)}, u32[]{:S(2)}, u32[]{:S(2)}) collective-permute-start(f32[56,1024]{1,0:T(8,128)} %get-tuple-element.24), channel_id=1, source_target_pairs={{0,1},{1,2},{2,3},{3,4},{4,5},{5,6},{6,7},{7,8},{8,9},{9,10},{10,1... | collective-permute-start | bytes 688136 | tf_op jit(solution)/shard_map/ppermute | solution.py:561
  9.7 8.3 %collective-permute-start.1 = (f32[56,1024]{1,0:T(8,128)}, f32[56,1024]{1,0:T(8,128)S(1)}, u32[]{:S(2)}, u32[]{:S(2)}) collective-permute-start(f32[56,1024]{1,0:T(8,128)} %get-tuple-element.25.rest_0_), channel_id=1, source_target_pairs={{1,0},{2,1},{3,2},{4,3},{5,4},{6,5},{7,6},{8,7},{9,8},{10,9},{11,1... | collective-permute-start | bytes 688136 | tf_op jit(solution)/shard_map/ppermute | solution.py:566
  19.3 3.1 %collective-permute-start.2 = (f32[4,8,16,128]{3,2,1,0:T(8,128)S(1)}, f32[4,8,16,128]{3,2,1,0:T(8,128)S(1)}, u32[]{:S(2)}, u32[]{:S(2)}) collective-permute-start(f32[4,8,16,128]{3,2,1,0:T(8,128)S(1)} %get-tuple-element.48), channel_id=1, source_target_pairs={{0,16},{16,0},{32,48},{48,32},{64,80},{80,64},{96,112},{112,96},{1... | collective-permute-start | bytes 786440 | tf_op jit(solution)/shard_map/ppermute | solution.py:570
  22.5 11.6 %collective-permute-start.5 = (f32[2,8,16,128]{3,2,1,0:T(8,128)S(1)}, f32[2,8,16,128]{3,2,1,0:T(8,128)S(1)}, u32[]{:S(2)}, u32[]{:S(2)}) collective-permute-start(f32[2,8,16,128]{3,2,1,0:T(8,128)S(1)} %get-tuple-element.44), channel_id=1, source_target_pairs={{0,96},{16,112},{32,64},{48,80},{64,32},{80,48},{96,0},{112,16},{1... | collective-permute-start | bytes 393224 | tf_op jit(solution)/shard_map/ppermute | solution.py:570
  25.3 8.8 %collective-permute-start.3 = (f32[2,8,16,128]{3,2,1,0:T(8,128)S(1)}, f32[2,8,16,128]{3,2,1,0:T(8,128)S(1)}, u32[]{:S(2)}, u32[]{:S(2)}) collective-permute-start(f32[2,8,16,128]{3,2,1,0:T(8,128)S(1)} %get-tuple-element.46), channel_id=1, source_target_pairs={{0,32},{16,48},{32,0},{48,16},{64,96},{80,112},{96,64},{112,80},{1... | collective-permute-start | bytes 393224 | tf_op jit(solution)/shard_map/ppermute | solution.py:570
  25.3 8.8 %collective-permute-start.4 = (f32[2,8,16,128]{3,2,1,0:T(8,128)S(1)}, f32[2,8,16,128]{3,2,1,0:T(8,128)S(1)}, u32[]{:S(2)}, u32[]{:S(2)}) collective-permute-start(f32[2,8,16,128]{3,2,1,0:T(8,128)S(1)} %get-tuple-element.47), channel_id=1, source_target_pairs={{0,64},{16,80},{32,96},{48,112},{64,0},{80,16},{96,32},{112,48},{1... | collective-permute-start | bytes 393224 | tf_op jit(solution)/shard_map/ppermute | solution.py:570
  26.6 24.8 %collective-permute-start.8 = (f32[2,2,8,8,1024]{4,3,2,1,0:T(8,128)}, f32[2,2,8,8,1024]{4,3,2,1,0:T(8,128)S(1)}, u32[]{:S(2)}, u32[]{:S(2)}) collective-permute-start(f32[2,2,8,8,1024]{4,3,2,1,0:T(8,128)} %get-tuple-element.33), channel_id=1, source_target_pairs={{0,1},{1,2},{2,3},{3,4},{4,5},{5,6},{6,7},{7,8},{8,9},{9,10},{10,1... | collective-permute-start | bytes 3145736 | tf_op jit(solution)/shard_map/ppermute | solution.py:561
  29.7 25.2 %collective-permute-start.9 = (f32[2,2,8,8,1024]{4,3,2,1,0:T(8,128)S(1)}, f32[2,2,8,8,1024]{4,3,2,1,0:T(8,128)S(1)}, u32[]{:S(2)}, u32[]{:S(2)}) collective-permute-start(f32[2,2,8,8,1024]{4,3,2,1,0:T(8,128)S(1)} %get-tuple-element.26.rest_0_), channel_id=1, source_target_pairs={{1,0},{2,1},{3,2},{4,3},{5,4},{6,5},{7,6},{8,7},{9,8},{10,9},{11,1... | collective-permute-start | bytes 3145736 | tf_op jit(solution)/shard_map/ppermute | solution.py:566
  35.8 48.8 %collective-permute-start.6 = (f32[2,2,8,8,1024]{4,3,2,1,0:T(8,128)}, f32[2,2,8,8,1024]{4,3,2,1,0:T(8,128)S(1)}, u32[]{:S(2)}, u32[]{:S(2)}) collective-permute-start(f32[2,2,8,8,1024]{4,3,2,1,0:T(8,128)} %get-tuple-element.31), channel_id=1, source_target_pairs={{0,1},{1,2},{2,3},{3,4},{4,5},{5,6},{6,7},{7,8},{8,9},{9,10},{10,1... | collective-permute-start | bytes 3145736 | tf_op jit(solution)/shard_map/ppermute | solution.py:561
  39.9 44.7 %collective-permute-start.7 = (f32[2,2,8,8,1024]{4,3,2,1,0:T(8,128)S(1)}, f32[2,2,8,8,1024]{4,3,2,1,0:T(8,128)S(1)}, u32[]{:S(2)}, u32[]{:S(2)}) collective-permute-start(f32[2,2,8,8,1024]{4,3,2,1,0:T(8,128)S(1)} %get-tuple-element.32.rest_0_), channel_id=1, source_target_pairs={{1,0},{2,1},{3,2},{4,3},{5,4},{6,5},{7,6},{8,7},{9,8},{10,9},{11,1... | collective-permute-start | bytes 3145736 | tf_op jit(solution)/shard_map/ppermute | solution.py:566
  41.2 2.8 %collective-permute-start.10 = (f32[72,128]{1,0:T(8,128)S(1)}, f32[72,128]{1,0:T(8,128)S(1)}, u32[]{:S(2)}, u32[]{:S(2)}) collective-permute-start(f32[72,128]{1,0:T(8,128)S(1)} %dynamic-slice_bitcast_fusion.1), channel_id=1, source_target_pairs={{0,16},{16,0},{32,48},{48,32},{64,80},{80,64},{96,112},{112,96},{1... | collective-permute-start | bytes 110600 | tf_op jit(solution)/shard_map/ppermute | solution.py:570
  44.0 21.2 %collective-permute-start.13 = (f32[72,128]{1,0:T(8,128)S(1)}, f32[72,128]{1,0:T(8,128)S(1)}, u32[]{:S(2)}, u32[]{:S(2)}) collective-permute-start(f32[72,128]{1,0:T(8,128)S(1)} %bitcast_add_fusion.a_ref), channel_id=1, source_target_pairs={{0,96},{16,112},{32,64},{48,80},{64,32},{80,48},{96,0},{112,16},{1... | collective-permute-start | bytes 110600 | tf_op jit(solution)/shard_map/ppermute | solution.py:570
  51.4 13.9 %collective-permute-start.12 = (f32[72,128]{1,0:T(8,128)S(1)}, f32[72,128]{1,0:T(8,128)S(1)}, u32[]{:S(2)}, u32[]{:S(2)}) collective-permute-start(f32[72,128]{1,0:T(8,128)S(1)} %bitcast_add_fusion.a_ref), channel_id=1, source_target_pairs={{0,64},{16,80},{32,96},{48,112},{64,0},{80,16},{96,32},{112,48},{1... | collective-permute-start | bytes 110600 | tf_op jit(solution)/shard_map/ppermute | solution.py:570
  54.9 10.3 %collective-permute-start.11 = (f32[72,128]{1,0:T(8,128)S(1)}, f32[72,128]{1,0:T(8,128)S(1)}, u32[]{:S(2)}, u32[]{:S(2)}) collective-permute-start(f32[72,128]{1,0:T(8,128)S(1)} %bitcast_add_fusion.a_ref), channel_id=1, source_target_pairs={{0,32},{16,48},{32,0},{48,16},{64,96},{80,112},{96,64},{112,80},{1... | collective-permute-start | bytes 110600 | tf_op jit(solution)/shard_map/ppermute | solution.py:570
  65.3 8.7 %collective-permute-start.16 = (f32[72,128]{1,0:T(8,128)S(1)}, f32[72,128]{1,0:T(8,128)S(1)}, u32[]{:S(2)}, u32[]{:S(2)}) collective-permute-start(f32[72,128]{1,0:T(8,128)S(1)} %add_up.3.a_ref), channel_id=1, source_target_pairs={{0,12},{1,13},{2,14},{3,15},{4,8},{5,9},{6,10},{7,11},{8,4},{9,5},... | collective-permute-start | bytes 110600 | tf_op jit(solution)/shard_map/ppermute | solution.py:570
  72.6 11.9 %collective-permute-start.15 = (f32[72,128]{1,0:T(8,128)S(1)}, f32[72,128]{1,0:T(8,128)S(1)}, u32[]{:S(2)}, u32[]{:S(2)}) collective-permute-start(f32[72,128]{1,0:T(8,128)S(1)} %add_up.3.a_ref), channel_id=1, source_target_pairs={{0,8},{1,9},{2,10},{3,11},{4,12},{5,13},{6,14},{7,15},{8,0},{9,1},... | collective-permute-start | bytes 110600 | tf_op jit(solution)/shard_map/ppermute | solution.py:570
  72.6 11.9 %collective-permute-start.14 = (f32[72,128]{1,0:T(8,128)S(1)}, f32[72,128]{1,0:T(8,128)S(1)}, u32[]{:S(2)}, u32[]{:S(2)}) collective-permute-start(f32[72,128]{1,0:T(8,128)S(1)} %add_up.3.a_ref), channel_id=1, source_target_pairs={{0,4},{1,5},{2,6},{3,7},{4,0},{5,1},{6,2},{7,3},{8,12},{9,13},{10,... | collective-permute-start | bytes 110600 | tf_op jit(solution)/shard_map/ppermute | solution.py:570
  84.6 13.1 %collective-permute-start.19 = (f32[72,128]{1,0:T(8,128)S(1)}, f32[72,128]{1,0:T(8,128)S(1)}, u32[]{:S(2)}, u32[]{:S(2)}) collective-permute-start(f32[72,128]{1,0:T(8,128)S(1)} %add_up.4.rest_1_.a_ref), channel_id=1, source_target_pairs={{0,3},{1,2},{2,1},{3,0},{4,7},{5,6},{6,5},{7,4},{8,11},{9,10},{10,... | collective-permute-start | bytes 110600 | tf_op jit(solution)/shard_map/ppermute | solution.py:570
  87.7 10.0 %collective-permute-start.18 = (f32[72,128]{1,0:T(8,128)S(1)}, f32[72,128]{1,0:T(8,128)S(1)}, u32[]{:S(2)}, u32[]{:S(2)}) collective-permute-start(f32[72,128]{1,0:T(8,128)S(1)} %add_up.4.rest_1_.a_ref), channel_id=1, source_target_pairs={{0,2},{1,3},{2,0},{3,1},{4,6},{5,7},{6,4},{7,5},{8,10},{9,11},{10,... | collective-permute-start | bytes 110600 | tf_op jit(solution)/shard_map/ppermute | solution.py:570
  87.7 10.0 %collective-permute-start.17 = (f32[72,128]{1,0:T(8,128)S(1)}, f32[72,128]{1,0:T(8,128)S(1)}, u32[]{:S(2)}, u32[]{:S(2)}) collective-permute-start(f32[72,128]{1,0:T(8,128)S(1)} %add_up.4.rest_1_.a_ref), channel_id=1, source_target_pairs={{0,1},{1,0},{2,3},{3,2},{4,5},{5,4},{6,7},{7,6},{8,9},{9,8},{10,11... | collective-permute-start | bytes 110600 | tf_op jit(solution)/shard_map/ppermute | solution.py:570
  97.8 2.0 %collective-permute-start.20 = (f32[72,128]{1,0:T(8,128)S(1)}, f32[72,128]{1,0:T(8,128)S(1)}, u32[]{:S(2)}, u32[]{:S(2)}) collective-permute-start(f32[72,128]{1,0:T(8,128)S(1)} %add_up.5), channel_id=1, source_target_pairs={{0,16},{16,0},{32,48},{48,32},{64,80},{80,64},{96,112},{112,96},{1... | collective-permute-start | bytes 110600 | tf_op jit(solution)/shard_map/ppermute | solution.py:570
  (6 other events, 47.0 us)

commit v3 on v2

--- a/solution.py
+++ b/solution.py
@@ -15,7 +15,7 @@
 ROWS = 8
 LIMIT = 16 << 20
 LARGE = 105 << 19
-CHUNKS = (2, 2)
+CHUNKS = (1, 2, 1)
 F32 = jnp.float32
 
 
@@ -24,7 +24,7 @@
 
 
 def cost(nbytes, flops=0):
-    return pl.CostEstimate(flops=flops, bytes_accessed=nbytes, transcendentals=0)
+    return pl.CostEstimate(flops=flops, bytes_accessed=nbytes >> 10, transcendentals=0)
 
 
 def params(limit=LIMIT):
@@ -148,6 +148,7 @@
     token_ref[...] = jnp.zeros_like(token_ref)
     levels, span, width = u_ref.shape[1], u.shape[3], u.shape[4]
     groups = before_ref.shape[0]
+    skip = kb_ref.shape[0] - levels
     part = levels // 4
 
     def fetch(g, p):
@@ -222,9 +223,9 @@
             for x in range(-1, ROWS + 1):
                 rows = rows[-2:] + [tiles(u.at[slot], l + 1, x + 3)]
                 if x < 0:
-                    k = kb_ref[l : l + 1, :]
+                    k = kb_ref[skip + l : skip + l + 1, :]
                 elif x == ROWS:
-                    k = ka_ref[l : l + 1, :]
+                    k = ka_ref[skip + l : skip + l + 1, :]
                 else:
                     k = k_ref[l, x : x + 1, :]
                 for t, tile_out in enumerate(one_step(u.at[slot], l + 1, x + 2, rows, k)):
@@ -580,7 +581,6 @@
     sums, low, high = pair_sums(prior, slots, k, rank)
     before = to_next(high)
     after = to_previous(low)
-    kb, ka = before[3 * rank :], after[3 * rank :]
 
     lo, hi = pack(prior, 0, CHUNKS[0], low)
     arrived_a = to_next(hi), to_previous(lo)
@@ -598,6 +598,7 @@
     own = pair_for(0)
     r1, r3, r2 = (across(pair_for(bits), "grp", 2 * bits) for bits in (1, 3, 2))
     lo, hi = pack(prior, 8 * CHUNKS[0], CHUNKS[1], own)
+    r1, r2, r3, *arrived_a = lax.optimization_barrier((r1, r2, r3, *arrived_a))
     part, sketches, mean = gram(place, obs, own, r1, r2, r3, lo)
     lo, hi, part = lax.optimization_barrier((lo, hi, part))
 
@@ -611,11 +612,17 @@
 
     arrived_b = to_next(hi), to_previous(lo)
     parts = others(total, "grp", 2)
-    out, done = two_steps(prior, *arrived_a, k, kb, ka, None, 0, part)
+    lo, hi = pack(prior, 8 * sum(CHUNKS[:2]), CHUNKS[2], part)
+    out, done = two_steps(prior, *arrived_a, k, before, after, None, 0, lo)
     total = add_up(total, *parts, done)
-    total = add_up(total, *others(total, "tile", 4), *arrived_b)
+    lo, hi, total = lax.optimization_barrier((lo, hi, total))
+    arrived_c = to_next(hi), to_previous(lo)
+    out, done = two_steps(prior, *arrived_b, k, before, after, out, 8 * CHUNKS[0], total)
+    total, done = lax.optimization_barrier((total, done))
+    total = add_up(total, *others(total, "tile", 4))
+    total, *arrived_c = lax.optimization_barrier((total, *arrived_c))
     parts = others(total, "tile", 1)
-    out, done = two_steps(prior, *arrived_b, k, kb, ka, out, 8 * CHUNKS[0], total)
+    out, done = two_steps(prior, *arrived_c, k, before, after, out, 8 * sum(CHUNKS[:2]), total)
     total = add_up(total, *parts, done)
     second = across(total, "grp", 1)
     both = jnp.where(core == 0, jnp.concatenate([total, second], 0), jnp.concatenate([second, total], 0))

time: 105 us -> 126 us (1.20)
  starting transfers between devices: 40.9 us -> 65.5 us
  waiting for transfers between devices: 21.1 us -> 11 us
  Pallas kernels: 39.2 us -> 43.8 us
  local copies, waits for them, and re-layouts: 1.76 us -> 3.24 us
    ppermute x15, starting transfers between devices: 25.7 us -> 43.6 us  [across(): lax.ppermute(v, axis, [(i, i ^ bits) for i in range(lax.axis_size(axis))])]
    ppermute x3 -> x4, starting transfers between devices: 11.3 us -> 16.8 us  [to_next(): return lax.ppermute(v, 'tile', [(i, i + 1) for i in range(size - 1)])]
    ppermute x3 -> x4, waiting for transfers between devices: 4.6 us -> 0.01 us  [to_next(): return lax.ppermute(v, 'tile', [(i, i + 1) for i in range(size - 1)])]
    pallas_call x2 -> x3, Pallas kernels: 18.6 us -> 22.7 us  [two_steps(): pl.pallas_call(functools.partial(step_kernel, first), in_specs=specs + [A...]
    ppermute x15, waiting for transfers between devices: 14.2 us -> 10.9 us  [across(): lax.ppermute(v, axis, [(i, i ^ bits) for i in range(lax.axis_size(axis))])]
    ppermute x3 -> x4, waiting for transfers between devices: 2.33 us -> 0.02 us  [to_previous(): return lax.ppermute(v, 'tile', [(i + 1, i) for i in range(size - 1)])]
    unnamed x19 -> x25, local copies, waits for them, and re-layouts: 1.69 us -> 3.17 us
    ppermute x3 -> x4, starting transfers between devices: 3.88 us -> 5.17 us  [to_previous(): return lax.ppermute(v, 'tile', [(i + 1, i) for i in range(size - 1)])]
  transfers between devices with their start and end apart: 21 -> 23, of which waited for: 8 -> 8; matrix products, arithmetic and copies ran while one was open for 0% -> 0% of each run, Pallas kernels for 28% -> 26%
where the time goes in v3:
time: 126 us; the launch traced here: 125 us
  starting transfers between devices  65.5 us (52%)
  Pallas kernels  43.8 us (35%)
  waiting for transfers between devices  11 us (9%)
  local copies, waits for them, and re-layouts  3.24 us (3%)
    ppermute x15, starting transfers between devices, across(): lax.ppermute(v, axis, [(i, i ^ bits) for i in range(lax.axis_size(axis))])  43.6 us
    pallas_call x3, Pallas kernels, two_steps(): pl.pallas_call(functools.partial(step_kernel, first), in_specs=specs + [A...  22.7 us
    ppermute x4, starting transfers between devices, to_next(): return lax.ppermute(v, 'tile', [(i, i + 1) for i in range(size - 1)])  16.8 us
    ppermute x15, waiting for transfers between devices, across(): lax.ppermute(v, axis, [(i, i ^ bits) for i in range(lax.axis_size(axis))])  10.9 us
    pallas_call x3, Pallas kernels, pack(): pl.pallas_call(functools.partial(pack_kernel, first), in_specs=[HBM] + [A...  6.72 us
    ppermute x4, starting transfers between devices, to_previous(): return lax.ppermute(v, 'tile', [(i + 1, i) for i in range(size - 1)])  5.17 us
    pallas_call x1, Pallas kernels, pair_sums(): pl.pallas_call(pair_kernel, in_specs=[SMEM, HBM, HBM], out_specs=[VMEM] *...  4.93 us
    pallas_call x1, Pallas kernels, analysis(): pl.pallas_call(analysis_kernel, in_specs=[VMEM] * 6, out_specs=VMEM, out_...  4.19 us
  transfers between devices with their start and end apart: 23, of which 8 were waited for; matrix products, arithmetic and copies ran while one was open for 0% of the time, Pallas kernels for 26%

profile of v3, /device:TPU:1, one launch (start us, length us, event | category | flops | bytes accessed | tf_op | source)
XLA Modules:
  0.0 124.7 jit_solution(11807626223847408580)
XLA Ops:
  0.7 4.9 %pair_sums.1 = (f32[3,8,16,1024]{3,2,1,0:T(8,128)}, f32[56,1024]{1,0:T(8,128)}, f32[56,1024]{1,0:T(8,128)}) custom-call(s32[32]{0:T(128)} %slot_ref.1, f32[8,8,1024]{2,1,0:T(8,128)} %k_ref.9, f32[32,8,8,1024]{3,2,1,0:T(8,128)} %u_ref.13), custom_call_target="tpu_custom_call" | custom-call | bytes 6144 | tf_op jit(solution)/shard_map/pair_sums/pallas_call | solution.py:91
  5.6 4.1 %collective-permute-start = (f32[56,1024]{1,0:T(8,128)}, f32[56,1024]{1,0:T(8,128)S(1)}, u32[]{:S(2)}, u32[]{:S(2)}) collective-permute-start(f32[56,1024]{1,0:T(8,128)} %get-tuple-element.38), channel_id=1, source_target_pairs={{0,1},{1,2},{2,3},{3,4},{4,5},{5,6},{6,7},{7,8},{8,9},{9,10},{10,1... | collective-permute-start | bytes 688136 | tf_op jit(solution)/shard_map/ppermute | solution.py:562
  12.0 2.2 %pack_edges.3 = (f32[1,2,8,8,1024]{4,3,2,1,0:T(8,128)S(1)}, f32[1,2,8,8,1024]{4,3,2,1,0:T(8,128)}) custom-call(f32[32,8,8,1024]{3,2,1,0:T(8,128)} %u_ref.13, f32[56,1024]{1,0:T(8,128)S(1)} %copy-done.4), custom_call_target="tpu_custom_call" | custom-call | bytes 2048 | tf_op jit(solution)/shard_map/pack_edges/pallas_call | solution.py:134
  14.2 4.0 %collective-permute-start.6 = (f32[1,2,8,8,1024]{4,3,2,1,0:T(8,128)}, f32[1,2,8,8,1024]{4,3,2,1,0:T(8,128)S(1)}, u32[]{:S(2)}, u32[]{:S(2)}) collective-permute-start(f32[1,2,8,8,1024]{4,3,2,1,0:T(8,128)} %get-tuple-element.44), channel_id=1, source_target_pairs={{0,1},{1,2},{2,3},{3,4},{4,5},{5,6},{6,7},{7,8},{8,9},{9,10},{10,1... | collective-permute-start | bytes 1572872 | tf_op jit(solution)/shard_map/ppermute | solution.py:562
  19.7 2.4 %sensor_sums.1 = (f32[16,128]{1,0:T(8,128)S(1)}, f32[64,128]{1,0:T(8,128)S(1)}, f32[32,64]{1,0:T(8,128)S(1)}, f32[16,32]{1,0:T(8,128)S(1)}) custom-call(s32[2]{0:T(128)S(1)} %pad_add_fusion.at_ref.place_ref, s32[32,128]{1,0:T(8,128)S(1)} %bitcast.25, f32[32,128]{1,0:T(8,128)S(1)} %bitcast.26, f32[32,128]{1,0:T(8,128)S(1)} %bitcast.27, ...), custom_call_target="tpu_custom_call" | custom-call | bytes 4096 | tf_op jit(solution)/shard_map/sensor_sums/pallas_call | solution.py:388
  23.4 1.6 %collective-permute-start.2 = (f32[4,8,16,128]{3,2,1,0:T(8,128)S(1)}, f32[4,8,16,128]{3,2,1,0:T(8,128)S(1)}, u32[]{:S(2)}, u32[]{:S(2)}) collective-permute-start(f32[4,8,16,128]{3,2,1,0:T(8,128)S(1)} %get-tuple-element.76), channel_id=1, source_target_pairs={{0,16},{16,0},{32,48},{48,32},{64,80},{80,64},{96,112},{112,96},{1... | collective-permute-start | bytes 786440 | tf_op jit(solution)/shard_map/ppermute | solution.py:571
  26.2 2.8 %collective-permute-start.5 = (f32[2,8,16,128]{3,2,1,0:T(8,128)S(1)}, f32[2,8,16,128]{3,2,1,0:T(8,128)S(1)}, u32[]{:S(2)}, u32[]{:S(2)}) collective-permute-start(f32[2,8,16,128]{3,2,1,0:T(8,128)S(1)} %get-tuple-element.72), channel_id=1, source_target_pairs={{0,96},{16,112},{32,64},{48,80},{64,32},{80,48},{96,0},{112,16},{1... | collective-permute-start | bytes 393224 | tf_op jit(solution)/shard_map/ppermute | solution.py:571
  30.3 3.0 %pack_edges.4 = (f32[2,2,8,8,1024]{4,3,2,1,0:T(8,128)S(1)}, f32[2,2,8,8,1024]{4,3,2,1,0:T(8,128)}) custom-call(f32[32,8,8,1024]{3,2,1,0:T(8,128)} %u_ref.13, f32[2,8,16,128]{3,2,1,0:T(8,128)S(1)} %get-tuple-element.73.rest_0_.own_ref), custom_call_target="tpu_custom_call" | custom-call | bytes 4096 | tf_op jit(solution)/shard_map/pack_edges/pallas_call | solution.py:134
  33.5 2.7 %collective-permute-done.4.r2_ref = f32[2,8,16,128]{3,2,1,0:T(8,128)S(1)} collective-permute-done((f32[2,8,16,128]{3,2,1,0:T(8,128)S(1)}, f32[2,8,16,128]{3,2,1,0:T(8,128)S(1)}, u32[]{:S(2)}, u32[]{:S(2)}) %collective-permute-start.4) | collective-permute-done | bytes 131104 | tf_op jit(solution)/shard_map/ppermute | solution.py:571
  36.2 1.7 %gram_sums.1 = (f32[144,128]{1,0:T(8,128)S(1)}, f32[128,1024]{1,0:T(8,128)S(1)}, f32[8,128]{1,0:T(8,128)S(1)}) custom-call(s32[2]{0:T(128)S(1)} %pad_add_fusion.at_ref.place_ref, f32[16,128]{1,0:T(8,128)S(1)} %get-tuple-element.41.rest_0_.obs_ref, f32[2,8,16,128]{3,2,1,0:T(8,128)S(1)} %get-tuple-element.73.rest_0_.own_ref, ...), custom_call_target="tpu_custom_call" | custom-call | bytes 4096 | tf_op jit(solution)/shard_map/gram_sums/pallas_call | solution.py:441
  37.9 4.3 %collective-permute-start.17 = (f32[2,2,8,8,1024]{4,3,2,1,0:T(8,128)}, f32[2,2,8,8,1024]{4,3,2,1,0:T(8,128)S(1)}, u32[]{:S(2)}, u32[]{:S(2)}) collective-permute-start(f32[2,2,8,8,1024]{4,3,2,1,0:T(8,128)} %get-tuple-element.60), channel_id=1, source_target_pairs={{0,1},{1,2},{2,3},{3,4},{4,5},{5,6},{6,7},{7,8},{8,9},{9,10},{10,1... | collective-permute-start | bytes 3145736 | tf_op jit(solution)/shard_map/ppermute | solution.py:562
  43.5 1.7 %collective-permute-start.8 = (f32[72,128]{1,0:T(8,128)S(1)}, f32[72,128]{1,0:T(8,128)S(1)}, u32[]{:S(2)}, u32[]{:S(2)}) collective-permute-start(f32[72,128]{1,0:T(8,128)S(1)} %dynamic-slice_bitcast_fusion.1), channel_id=1, source_target_pairs={{0,16},{16,0},{32,48},{48,32},{64,80},{80,64},{96,112},{112,96},{1... | collective-permute-start | bytes 110600 | tf_op jit(solution)/shard_map/ppermute | solution.py:571
  46.1 2.6 %collective-permute-start.11 = (f32[72,128]{1,0:T(8,128)S(1)}, f32[72,128]{1,0:T(8,128)S(1)}, u32[]{:S(2)}, u32[]{:S(2)}) collective-permute-start(f32[72,128]{1,0:T(8,128)S(1)} %bitcast_add_fusion.a_ref), channel_id=1, source_target_pairs={{0,96},{16,112},{32,64},{48,80},{64,32},{80,48},{96,0},{112,16},{1... | collective-permute-start | bytes 110600 | tf_op jit(solution)/shard_map/ppermute | solution.py:571
  49.4 1.4 %pack_edges.5 = (f32[1,2,8,8,1024]{4,3,2,1,0:T(8,128)S(1)}, f32[1,2,8,8,1024]{4,3,2,1,0:T(8,128)S(1)}) custom-call(f32[32,8,8,1024]{3,2,1,0:T(8,128)} %u_ref.13, f32[144,128]{1,0:T(8,128)S(1)} %get-tuple-element.49.rest_0_), custom_call_target="tpu_custom_call" | custom-call | bytes 2048 | tf_op jit(solution)/shard_map/pack_edges/pallas_call | solution.py:134
  51.6 6.0 %two_steps.3 = (f32[32,8,8,1024]{3,2,1,0:T(8,128)}, f32[8,128]{1,0:T(8,128)S(1)}) custom-call(f32[32,8,8,1024]{3,2,1,0:T(8,128)} %u_ref.13, f32[1,2,8,8,1024]{4,3,2,1,0:T(8,128)S(1)} %collective-permute-done.6.before_ref, f32[1,2,8,8,1024]{4,3,2,1,0:T(8,128)} %collective-permute-done.7.after_ref, f32[8,8,1024]{2,1,0:T(8,128)S(1)} %copy-done, ...), custom_call_target="tpu_custom_call" | custom-call | bytes 8192 | tf_op jit(solution)/shard_map/two_steps/pallas_call | solution.py:276
  57.7 4.3 %collective-permute-start.15 = (f32[1,2,8,8,1024]{4,3,2,1,0:T(8,128)S(1)}, f32[1,2,8,8,1024]{4,3,2,1,0:T(8,128)S(1)}, u32[]{:S(2)}, u32[]{:S(2)}) collective-permute-start(f32[1,2,8,8,1024]{4,3,2,1,0:T(8,128)S(1)} %get-tuple-element.56), channel_id=1, source_target_pairs={{0,1},{1,2},{2,3},{3,4},{4,5},{5,6},{6,7},{7,8},{8,9},{9,10},{10,1... | collective-permute-start | bytes 1572872 | tf_op jit(solution)/shard_map/ppermute | solution.py:562
  63.3 13.2 %collective-permute-start.14 = (f32[72,128]{1,0:T(8,128)S(1)}, f32[72,128]{1,0:T(8,128)S(1)}, u32[]{:S(2)}, u32[]{:S(2)}) collective-permute-start(f32[72,128]{1,0:T(8,128)S(1)} %add_up.3.a_ref.rest_1_), channel_id=1, source_target_pairs={{0,12},{1,13},{2,14},{3,15},{4,8},{5,9},{6,10},{7,11},{8,4},{9,5},... | collective-permute-start | bytes 110600 | tf_op jit(solution)/shard_map/ppermute | solution.py:571
  77.8 10.3 %collective-permute-start.13 = (f32[72,128]{1,0:T(8,128)S(1)}, f32[72,128]{1,0:T(8,128)S(1)}, u32[]{:S(2)}, u32[]{:S(2)}) collective-permute-start(f32[72,128]{1,0:T(8,128)S(1)} %add_up.3.a_ref.rest_1_), channel_id=1, source_target_pairs={{0,8},{1,9},{2,10},{3,11},{4,12},{5,13},{6,14},{7,15},{8,0},{9,1},... | collective-permute-start | bytes 110600 | tf_op jit(solution)/shard_map/ppermute | solution.py:571
  89.8 2.5 %collective-permute-done.12.b_ref = f32[72,128]{1,0:T(8,128)S(1)} collective-permute-done((f32[72,128]{1,0:T(8,128)S(1)}, f32[72,128]{1,0:T(8,128)S(1)}, u32[]{:S(2)}, u32[]{:S(2)}) %collective-permute-start.12) | collective-permute-done | bytes 36896 | tf_op jit(solution)/shard_map/ppermute | solution.py:571
  92.3 5.4 %collective-permute-start.21 = (f32[72,128]{1,0:T(8,128)S(1)}, f32[72,128]{1,0:T(8,128)S(1)}, u32[]{:S(2)}, u32[]{:S(2)}) collective-permute-start(f32[72,128]{1,0:T(8,128)S(1)} %add_up.4.rest_1_.a_ref), channel_id=1, source_target_pairs={{0,3},{1,2},{2,1},{3,0},{4,7},{5,6},{6,5},{7,4},{8,11},{9,10},{10,... | collective-permute-start | bytes 110600 | tf_op jit(solution)/shard_map/ppermute | solution.py:571
  99.7 10.7 %two_steps.4 = (f32[32,8,8,1024]{3,2,1,0:T(8,128)}, f32[8,128]{1,0:T(8,128)}) custom-call(f32[32,8,8,1024]{3,2,1,0:T(8,128)} %u_ref.13, f32[2,2,8,8,1024]{4,3,2,1,0:T(8,128)} %copy-done.8, f32[2,2,8,8,1024]{4,3,2,1,0:T(8,128)} %copy-done.9, f32[8,8,1024]{2,1,0:T(8,128)S(1)} %copy-done, ...), custom_call_target="tpu_custom_call", output_to_operand_aliasing={{0}: (6, {})} | custom-call | bytes 16384 | tf_op jit(solution)/shard_map/two_steps/pallas_call | solution.py:276
  110.4 6.0 %two_steps.5 = (f32[32,8,8,1024]{3,2,1,0:T(8,128)}, f32[8,128]{1,0:T(8,128)S(1)}) custom-call(f32[32,8,8,1024]{3,2,1,0:T(8,128)} %u_ref.13, f32[1,2,8,8,1024]{4,3,2,1,0:T(8,128)S(1)} %collective-permute-done.15.before_ref, f32[1,2,8,8,1024]{4,3,2,1,0:T(8,128)} %copy-done.10, f32[8,8,1024]{2,1,0:T(8,128)S(1)} %copy-done, ...), custom_call_target="tpu_custom_call", output_to_operand_aliasing={{0}: (6, {})} | custom-call | bytes 8192 | tf_op jit(solution)/shard_map/two_steps/pallas_call | solution.py:276
  116.5 3.2 %collective-permute-start.22 = (f32[72,128]{1,0:T(8,128)S(1)}, f32[72,128]{1,0:T(8,128)S(1)}, u32[]{:S(2)}, u32[]{:S(2)}) collective-permute-start(f32[72,128]{1,0:T(8,128)S(1)} %add_up.5), channel_id=1, source_target_pairs={{0,16},{16,0},{32,48},{48,32},{64,80},{80,64},{96,112},{112,96},{1... | collective-permute-start | bytes 110600 | tf_op jit(solution)/shard_map/ppermute | solution.py:571
  120.5 4.2 %analysis.1 = f32[8,128]{1,0:T(8,128)} custom-call(f32[144,128]{1,0:T(8,128)S(1)} %maximum_select_fusion.sums_ref, f32[64,128]{1,0:T(8,128)S(1)} %get-tuple-element.67.mix0_ref, f32[32,64]{1,0:T(8,128)S(1)} %get-tuple-element.68.mix1_ref, f32[16,32]{1,0:T(8,128)S(1)} %get-tuple-element.69.mix2_ref, f32[128,1024]{1,0:T(8,128)S(1)} %get-tuple-element.70.s_ref, ...), custom_call_target="tpu_custom_call" | custom-call | bytes 16384 | tf_op jit(solution)/shard_map/analysis/pallas_call | solution.py:533
  (67 shorter events, 18.4 us)
Async XLA Ops:
  0.6 21.5 %copy-start = (f32[8,8,1024]{2,1,0:T(8,128)S(1)}, f32[8,8,1024]{2,1,0:T(8,128)}, u32[]{:S(2)}) copy-start(f32[8,8,1024]{2,1,0:T(8,128)} %k_ref.9) | copy-start | bytes 786436
  5.6 16.5 %collective-permute-start = (f32[56,1024]{1,0:T(8,128)}, f32[56,1024]{1,0:T(8,128)S(1)}, u32[]{:S(2)}, u32[]{:S(2)}) collective-permute-start(f32[56,1024]{1,0:T(8,128)} %get-tuple-element.38), channel_id=1, source_target_pairs={{0,1},{1,2},{2,3},{3,4},{4,5},{5,6},{6,7},{7,8},{8,9},{9,10},{10,1... | collective-permute-start | bytes 688136 | tf_op jit(solution)/shard_map/ppermute | solution.py:562
  9.7 12.4 %collective-permute-start.1 = (f32[56,1024]{1,0:T(8,128)}, f32[56,1024]{1,0:T(8,128)S(1)}, u32[]{:S(2)}, u32[]{:S(2)}) collective-permute-start(f32[56,1024]{1,0:T(8,128)} %get-tuple-element.39.rest_0_), channel_id=1, source_target_pairs={{1,0},{2,1},{3,2},{4,3},{5,4},{6,5},{7,6},{8,7},{9,8},{10,9},{11,1... | collective-permute-start | bytes 688136 | tf_op jit(solution)/shard_map/ppermute | solution.py:567
  14.2 19.1 %collective-permute-start.6 = (f32[1,2,8,8,1024]{4,3,2,1,0:T(8,128)}, f32[1,2,8,8,1024]{4,3,2,1,0:T(8,128)S(1)}, u32[]{:S(2)}, u32[]{:S(2)}) collective-permute-start(f32[1,2,8,8,1024]{4,3,2,1,0:T(8,128)} %get-tuple-element.44), channel_id=1, source_target_pairs={{0,1},{1,2},{2,3},{3,4},{4,5},{5,6},{6,7},{7,8},{8,9},{9,10},{10,1... | collective-permute-start | bytes 1572872 | tf_op jit(solution)/shard_map/ppermute | solution.py:562
  18.3 15.1 %collective-permute-start.7 = (f32[1,2,8,8,1024]{4,3,2,1,0:T(8,128)S(1)}, f32[1,2,8,8,1024]{4,3,2,1,0:T(8,128)}, u32[]{:S(2)}, u32[]{:S(2)}) collective-permute-start(f32[1,2,8,8,1024]{4,3,2,1,0:T(8,128)S(1)} %get-tuple-element.40.rest_0_), channel_id=1, source_target_pairs={{1,0},{2,1},{3,2},{4,3},{5,4},{6,5},{7,6},{8,7},{9,8},{10,9},{11,1... | collective-permute-start | bytes 1572872 | tf_op jit(solution)/shard_map/ppermute | solution.py:567
  23.4 2.8 %collective-permute-start.2 = (f32[4,8,16,128]{3,2,1,0:T(8,128)S(1)}, f32[4,8,16,128]{3,2,1,0:T(8,128)S(1)}, u32[]{:S(2)}, u32[]{:S(2)}) collective-permute-start(f32[4,8,16,128]{3,2,1,0:T(8,128)S(1)} %get-tuple-element.76), channel_id=1, source_target_pairs={{0,16},{16,0},{32,48},{48,32},{64,80},{80,64},{96,112},{112,96},{1... | collective-permute-start | bytes 786440 | tf_op jit(solution)/shard_map/ppermute | solution.py:571
  26.2 7.2 %collective-permute-start.5 = (f32[2,8,16,128]{3,2,1,0:T(8,128)S(1)}, f32[2,8,16,128]{3,2,1,0:T(8,128)S(1)}, u32[]{:S(2)}, u32[]{:S(2)}) collective-permute-start(f32[2,8,16,128]{3,2,1,0:T(8,128)S(1)} %get-tuple-element.72), channel_id=1, source_target_pairs={{0,96},{16,112},{32,64},{48,80},{64,32},{80,48},{96,0},{112,16},{1... | collective-permute-start | bytes 393224 | tf_op jit(solution)/shard_map/ppermute | solution.py:571
  29.0 4.5 %collective-permute-start.3 = (f32[2,8,16,128]{3,2,1,0:T(8,128)S(1)}, f32[2,8,16,128]{3,2,1,0:T(8,128)S(1)}, u32[]{:S(2)}, u32[]{:S(2)}) collective-permute-start(f32[2,8,16,128]{3,2,1,0:T(8,128)S(1)} %get-tuple-element.74), channel_id=1, source_target_pairs={{0,32},{16,48},{32,0},{48,16},{64,96},{80,112},{96,64},{112,80},{1... | collective-permute-start | bytes 393224 | tf_op jit(solution)/shard_map/ppermute | solution.py:571
  29.0 7.2 %collective-permute-start.4 = (f32[2,8,16,128]{3,2,1,0:T(8,128)S(1)}, f32[2,8,16,128]{3,2,1,0:T(8,128)S(1)}, u32[]{:S(2)}, u32[]{:S(2)}) collective-permute-start(f32[2,8,16,128]{3,2,1,0:T(8,128)S(1)} %get-tuple-element.75), channel_id=1, source_target_pairs={{0,64},{16,80},{32,96},{48,112},{64,0},{80,16},{96,32},{112,48},{1... | collective-permute-start | bytes 393224 | tf_op jit(solution)/shard_map/ppermute | solution.py:571
  37.9 60.5 %collective-permute-start.17 = (f32[2,2,8,8,1024]{4,3,2,1,0:T(8,128)}, f32[2,2,8,8,1024]{4,3,2,1,0:T(8,128)S(1)}, u32[]{:S(2)}, u32[]{:S(2)}) collective-permute-start(f32[2,2,8,8,1024]{4,3,2,1,0:T(8,128)} %get-tuple-element.60), channel_id=1, source_target_pairs={{0,1},{1,2},{2,3},{3,4},{4,5},{5,6},{6,7},{7,8},{8,9},{9,10},{10,1... | collective-permute-start | bytes 3145736 | tf_op jit(solution)/shard_map/ppermute | solution.py:562
  42.2 56.2 %collective-permute-start.18 = (f32[2,2,8,8,1024]{4,3,2,1,0:T(8,128)S(1)}, f32[2,2,8,8,1024]{4,3,2,1,0:T(8,128)S(1)}, u32[]{:S(2)}, u32[]{:S(2)}) collective-permute-start(f32[2,2,8,8,1024]{4,3,2,1,0:T(8,128)S(1)} %get-tuple-element.61.rest_0_), channel_id=1, source_target_pairs={{1,0},{2,1},{3,2},{4,3},{5,4},{6,5},{7,6},{8,7},{9,8},{10,9},{11,1... | collective-permute-start | bytes 3145736 | tf_op jit(solution)/shard_map/ppermute | solution.py:567
  43.5 2.6 %collective-permute-start.8 = (f32[72,128]{1,0:T(8,128)S(1)}, f32[72,128]{1,0:T(8,128)S(1)}, u32[]{:S(2)}, u32[]{:S(2)}) collective-permute-start(f32[72,128]{1,0:T(8,128)S(1)} %dynamic-slice_bitcast_fusion.1), channel_id=1, source_target_pairs={{0,16},{16,0},{32,48},{48,32},{64,80},{80,64},{96,112},{112,96},{1... | collective-permute-start | bytes 110600 | tf_op jit(solution)/shard_map/ppermute | solution.py:571
  46.1 11.5 %collective-permute-start.11 = (f32[72,128]{1,0:T(8,128)S(1)}, f32[72,128]{1,0:T(8,128)S(1)}, u32[]{:S(2)}, u32[]{:S(2)}) collective-permute-start(f32[72,128]{1,0:T(8,128)S(1)} %bitcast_add_fusion.a_ref), channel_id=1, source_target_pairs={{0,96},{16,112},{32,64},{48,80},{64,32},{80,48},{96,0},{112,16},{1... | collective-permute-start | bytes 110600 | tf_op jit(solution)/shard_map/ppermute | solution.py:571
  48.7 9.0 %collective-permute-start.10 = (f32[72,128]{1,0:T(8,128)S(1)}, f32[72,128]{1,0:T(8,128)S(1)}, u32[]{:S(2)}, u32[]{:S(2)}) collective-permute-start(f32[72,128]{1,0:T(8,128)S(1)} %bitcast_add_fusion.a_ref), channel_id=1, source_target_pairs={{0,64},{16,80},{32,96},{48,112},{64,0},{80,16},{96,32},{112,48},{1... | collective-permute-start | bytes 110600 | tf_op jit(solution)/shard_map/ppermute | solution.py:571
  48.7 9.0 %collective-permute-start.9 = (f32[72,128]{1,0:T(8,128)S(1)}, f32[72,128]{1,0:T(8,128)S(1)}, u32[]{:S(2)}, u32[]{:S(2)}) collective-permute-start(f32[72,128]{1,0:T(8,128)S(1)} %bitcast_add_fusion.a_ref), channel_id=1, source_target_pairs={{0,32},{16,48},{32,0},{48,16},{64,96},{80,112},{96,64},{112,80},{1... | collective-permute-start | bytes 110600 | tf_op jit(solution)/shard_map/ppermute | solution.py:571
  57.7 34.6 %collective-permute-start.15 = (f32[1,2,8,8,1024]{4,3,2,1,0:T(8,128)S(1)}, f32[1,2,8,8,1024]{4,3,2,1,0:T(8,128)S(1)}, u32[]{:S(2)}, u32[]{:S(2)}) collective-permute-start(f32[1,2,8,8,1024]{4,3,2,1,0:T(8,128)S(1)} %get-tuple-element.56), channel_id=1, source_target_pairs={{0,1},{1,2},{2,3},{3,4},{4,5},{5,6},{6,7},{7,8},{8,9},{9,10},{10,1... | collective-permute-start | bytes 1572872 | tf_op jit(solution)/shard_map/ppermute | solution.py:562
  62.0 30.3 %collective-permute-start.16 = (f32[1,2,8,8,1024]{4,3,2,1,0:T(8,128)S(1)}, f32[1,2,8,8,1024]{4,3,2,1,0:T(8,128)S(1)}, u32[]{:S(2)}, u32[]{:S(2)}) collective-permute-start(f32[1,2,8,8,1024]{4,3,2,1,0:T(8,128)S(1)} %copy-done.3), channel_id=1, source_target_pairs={{1,0},{2,1},{3,2},{4,3},{5,4},{6,5},{7,6},{8,7},{9,8},{10,9},{11,1... | collective-permute-start | bytes 1572872 | tf_op jit(solution)/shard_map/ppermute | solution.py:567
  63.3 14.5 %collective-permute-start.14 = (f32[72,128]{1,0:T(8,128)S(1)}, f32[72,128]{1,0:T(8,128)S(1)}, u32[]{:S(2)}, u32[]{:S(2)}) collective-permute-start(f32[72,128]{1,0:T(8,128)S(1)} %add_up.3.a_ref.rest_1_), channel_id=1, source_target_pairs={{0,12},{1,13},{2,14},{3,15},{4,8},{5,9},{6,10},{7,11},{8,4},{9,5},... | collective-permute-start | bytes 110600 | tf_op jit(solution)/shard_map/ppermute | solution.py:571
  77.8 11.6 %collective-permute-start.13 = (f32[72,128]{1,0:T(8,128)S(1)}, f32[72,128]{1,0:T(8,128)S(1)}, u32[]{:S(2)}, u32[]{:S(2)}) collective-permute-start(f32[72,128]{1,0:T(8,128)S(1)} %add_up.3.a_ref.rest_1_), channel_id=1, source_target_pairs={{0,8},{1,9},{2,10},{3,11},{4,12},{5,13},{6,14},{7,15},{8,0},{9,1},... | collective-permute-start | bytes 110600 | tf_op jit(solution)/shard_map/ppermute | solution.py:571
  89.4 2.8 %collective-permute-start.12 = (f32[72,128]{1,0:T(8,128)S(1)}, f32[72,128]{1,0:T(8,128)S(1)}, u32[]{:S(2)}, u32[]{:S(2)}) collective-permute-start(f32[72,128]{1,0:T(8,128)S(1)} %add_up.3.a_ref.rest_1_), channel_id=1, source_target_pairs={{0,4},{1,5},{2,6},{3,7},{4,0},{5,1},{6,2},{7,3},{8,12},{9,13},{10,... | collective-permute-start | bytes 110600 | tf_op jit(solution)/shard_map/ppermute | solution.py:571
  92.3 24.1 %collective-permute-start.21 = (f32[72,128]{1,0:T(8,128)S(1)}, f32[72,128]{1,0:T(8,128)S(1)}, u32[]{:S(2)}, u32[]{:S(2)}) collective-permute-start(f32[72,128]{1,0:T(8,128)S(1)} %add_up.4.rest_1_.a_ref), channel_id=1, source_target_pairs={{0,3},{1,2},{2,1},{3,0},{4,7},{5,6},{6,5},{7,4},{8,11},{9,10},{10,... | collective-permute-start | bytes 110600 | tf_op jit(solution)/shard_map/ppermute | solution.py:571
  97.7 18.8 %collective-permute-start.20 = (f32[72,128]{1,0:T(8,128)S(1)}, f32[72,128]{1,0:T(8,128)S(1)}, u32[]{:S(2)}, u32[]{:S(2)}) collective-permute-start(f32[72,128]{1,0:T(8,128)S(1)} %add_up.4.rest_1_.a_ref), channel_id=1, source_target_pairs={{0,2},{1,3},{2,0},{3,1},{4,6},{5,7},{6,4},{7,5},{8,10},{9,11},{10,... | collective-permute-start | bytes 110600 | tf_op jit(solution)/shard_map/ppermute | solution.py:571
  97.7 18.8 %collective-permute-start.19 = (f32[72,128]{1,0:T(8,128)S(1)}, f32[72,128]{1,0:T(8,128)S(1)}, u32[]{:S(2)}, u32[]{:S(2)}) collective-permute-start(f32[72,128]{1,0:T(8,128)S(1)} %add_up.4.rest_1_.a_ref), channel_id=1, source_target_pairs={{0,1},{1,0},{2,3},{3,2},{4,5},{5,4},{6,7},{7,6},{8,9},{9,8},{10,11... | collective-permute-start | bytes 110600 | tf_op jit(solution)/shard_map/ppermute | solution.py:571
  116.5 4.0 %collective-permute-start.22 = (f32[72,128]{1,0:T(8,128)S(1)}, f32[72,128]{1,0:T(8,128)S(1)}, u32[]{:S(2)}, u32[]{:S(2)}) collective-permute-start(f32[72,128]{1,0:T(8,128)S(1)} %add_up.5), channel_id=1, source_target_pairs={{0,16},{16,0},{32,48},{48,32},{64,80},{80,64},{96,112},{112,96},{1... | collective-permute-start | bytes 110600 | tf_op jit(solution)/shard_map/ppermute | solution.py:571
  (11 other events, 125.3 us)

commit v4 on v3

--- a/solution.py
+++ b/solution.py
@@ -614,11 +614,10 @@
     parts = others(total, "grp", 2)
     lo, hi = pack(prior, 8 * sum(CHUNKS[:2]), CHUNKS[2], part)
     out, done = two_steps(prior, *arrived_a, k, before, after, None, 0, lo)
+    lo, hi, done = lax.optimization_barrier((lo, hi, done))
+    arrived_c = to_next(hi), to_previous(lo)
+    out, done = two_steps(prior, *arrived_b, k, before, after, out, 8 * CHUNKS[0], done)
     total = add_up(total, *parts, done)
-    lo, hi, total = lax.optimization_barrier((lo, hi, total))
-    arrived_c = to_next(hi), to_previous(lo)
-    out, done = two_steps(prior, *arrived_b, k, before, after, out, 8 * CHUNKS[0], total)
-    total, done = lax.optimization_barrier((total, done))
     total = add_up(total, *others(total, "tile", 4))
     total, *arrived_c = lax.optimization_barrier((total, *arrived_c))
     parts = others(total, "tile", 1)

time: 126 us -> 116 us (0.921)
  starting transfers between devices: 65.5 us -> 47.6 us
  waiting for transfers between devices: 11 us -> 19.9 us
    ppermute x15, starting transfers between devices: 43.6 us -> 25.6 us  [across(): lax.ppermute(v, axis, [(i, i ^ bits) for i in range(lax.axis_size(axis))])]
    ppermute x4, waiting for transfers between devices: 0.02 us -> 4.21 us  [to_previous(): return lax.ppermute(v, 'tile', [(i + 1, i) for i in range(size - 1)])]
    ppermute x4, waiting for transfers between devices: 0.01 us -> 3.22 us  [to_next(): return lax.ppermute(v, 'tile', [(i, i + 1) for i in range(size - 1)])]
    ppermute x15, waiting for transfers between devices: 10.9 us -> 12.4 us  [across(): lax.ppermute(v, axis, [(i, i ^ bits) for i in range(lax.axis_size(axis))])]
  transfers between devices with their start and end apart: 23 -> 23, of which waited for: 8 -> 9; matrix products, arithmetic and copies ran while one was open for 0% -> 0% of each run, Pallas kernels for 26% -> 28%
where the time goes in v4:
time: 116 us; the launch traced here: 115 us
  starting transfers between devices  47.6 us (41%)
  Pallas kernels  43.2 us (37%)
  waiting for transfers between devices  19.9 us (17%)
  local copies, waits for them, and re-layouts  2.88 us (2%)
    ppermute x15, starting transfers between devices, across(): lax.ppermute(v, axis, [(i, i ^ bits) for i in range(lax.axis_size(axis))])  25.6 us
    pallas_call x3, Pallas kernels, two_steps(): pl.pallas_call(functools.partial(step_kernel, first), in_specs=specs + [A...  22.1 us
    ppermute x4, starting transfers between devices, to_next(): return lax.ppermute(v, 'tile', [(i, i + 1) for i in range(size - 1)])  16.8 us
    ppermute x15, waiting for transfers between devices, across(): lax.ppermute(v, axis, [(i, i ^ bits) for i in range(lax.axis_size(axis))])  12.4 us
    pallas_call x3, Pallas kernels, pack(): pl.pallas_call(functools.partial(pack_kernel, first), in_specs=[HBM] + [A...  6.73 us
    ppermute x4, starting transfers between devices, to_previous(): return lax.ppermute(v, 'tile', [(i + 1, i) for i in range(size - 1)])  5.3 us
    pallas_call x1, Pallas kernels, pair_sums(): pl.pallas_call(pair_kernel, in_specs=[SMEM, HBM, HBM], out_specs=[VMEM] *...  4.93 us
    ppermute x4, waiting for transfers between devices, to_previous(): return lax.ppermute(v, 'tile', [(i + 1, i) for i in range(size - 1)])  4.21 us
  transfers between devices with their start and end apart: 23, of which 9 were waited for; matrix products, arithmetic and copies ran while one was open for 0% of the time, Pallas kernels for 28%

profile of v4, /device:TPU:1, one launch (start us, length us, event | category | flops | bytes accessed | tf_op | source)
XLA Modules:
  0.0 114.7 jit_solution(5469651306500655291)
XLA Ops:
  0.7 4.9 %pair_sums.1 = (f32[3,8,16,1024]{3,2,1,0:T(8,128)}, f32[56,1024]{1,0:T(8,128)}, f32[56,1024]{1,0:T(8,128)}) custom-call(s32[32]{0:T(128)} %slot_ref.1, f32[8,8,1024]{2,1,0:T(8,128)} %k_ref.9, f32[32,8,8,1024]{3,2,1,0:T(8,128)} %u_ref.13), custom_call_target="tpu_custom_call" | custom-call | bytes 6144 | tf_op jit(solution)/shard_map/pair_sums/pallas_call | solution.py:91
  7.1 4.6 %collective-permute-start = (f32[56,1024]{1,0:T(8,128)}, f32[56,1024]{1,0:T(8,128)S(1)}, u32[]{:S(2)}, u32[]{:S(2)}) collective-permute-start(f32[56,1024]{1,0:T(8,128)} %get-tuple-element.39), channel_id=1, source_target_pairs={{0,1},{1,2},{2,3},{3,4},{4,5},{5,6},{6,7},{7,8},{8,9},{9,10},{10,1... | collective-permute-start | bytes 688136 | tf_op jit(solution)/shard_map/ppermute | solution.py:562
  12.6 2.2 %pack_edges.3 = (f32[1,2,8,8,1024]{4,3,2,1,0:T(8,128)S(1)}, f32[1,2,8,8,1024]{4,3,2,1,0:T(8,128)}) custom-call(f32[32,8,8,1024]{3,2,1,0:T(8,128)} %u_ref.13, f32[56,1024]{1,0:T(8,128)S(1)} %copy-done.4), custom_call_target="tpu_custom_call" | custom-call | bytes 2048 | tf_op jit(solution)/shard_map/pack_edges/pallas_call | solution.py:134
  16.1 4.0 %collective-permute-start.6 = (f32[1,2,8,8,1024]{4,3,2,1,0:T(8,128)}, f32[1,2,8,8,1024]{4,3,2,1,0:T(8,128)S(1)}, u32[]{:S(2)}, u32[]{:S(2)}) collective-permute-start(f32[1,2,8,8,1024]{4,3,2,1,0:T(8,128)} %get-tuple-element.45), channel_id=1, source_target_pairs={{0,1},{1,2},{2,3},{3,4},{4,5},{5,6},{6,7},{7,8},{8,9},{9,10},{10,1... | collective-permute-start | bytes 1572872 | tf_op jit(solution)/shard_map/ppermute | solution.py:562
  20.4 2.4 %sensor_sums.1 = (f32[16,128]{1,0:T(8,128)S(1)}, f32[64,128]{1,0:T(8,128)S(1)}, f32[32,64]{1,0:T(8,128)S(1)}, f32[16,32]{1,0:T(8,128)S(1)}) custom-call(s32[2]{0:T(128)S(1)} %pad_add_fusion.at_ref.place_ref, s32[32,128]{1,0:T(8,128)S(1)} %bitcast.25, f32[32,128]{1,0:T(8,128)S(1)} %bitcast.26, f32[32,128]{1,0:T(8,128)S(1)} %bitcast.27, ...), custom_call_target="tpu_custom_call" | custom-call | bytes 4096 | tf_op jit(solution)/shard_map/sensor_sums/pallas_call | solution.py:388
  24.0 2.0 %collective-permute-start.2 = (f32[4,8,16,128]{3,2,1,0:T(8,128)S(1)}, f32[4,8,16,128]{3,2,1,0:T(8,128)S(1)}, u32[]{:S(2)}, u32[]{:S(2)}) collective-permute-start(f32[4,8,16,128]{3,2,1,0:T(8,128)S(1)} %get-tuple-element.78), channel_id=1, source_target_pairs={{0,16},{16,0},{32,48},{48,32},{64,80},{80,64},{96,112},{112,96},{1... | collective-permute-start | bytes 786440 | tf_op jit(solution)/shard_map/ppermute | solution.py:571
  28.7 2.6 %collective-permute-start.4 = (f32[2,8,16,128]{3,2,1,0:T(8,128)S(1)}, f32[2,8,16,128]{3,2,1,0:T(8,128)S(1)}, u32[]{:S(2)}, u32[]{:S(2)}) collective-permute-start(f32[2,8,16,128]{3,2,1,0:T(8,128)S(1)} %get-tuple-element.77), channel_id=1, source_target_pairs={{0,64},{16,80},{32,96},{48,112},{64,0},{80,16},{96,32},{112,48},{1... | collective-permute-start | bytes 393224 | tf_op jit(solution)/shard_map/ppermute | solution.py:571
  31.3 3.0 %pack_edges.4 = (f32[2,2,8,8,1024]{4,3,2,1,0:T(8,128)S(1)}, f32[2,2,8,8,1024]{4,3,2,1,0:T(8,128)}) custom-call(f32[32,8,8,1024]{3,2,1,0:T(8,128)} %u_ref.13, f32[2,8,16,128]{3,2,1,0:T(8,128)S(1)} %get-tuple-element.75.rest_0_.own_ref), custom_call_target="tpu_custom_call" | custom-call | bytes 4096 | tf_op jit(solution)/shard_map/pack_edges/pallas_call | solution.py:134
  34.4 3.0 %collective-permute-done.4.r2_ref = f32[2,8,16,128]{3,2,1,0:T(8,128)S(1)} collective-permute-done((f32[2,8,16,128]{3,2,1,0:T(8,128)S(1)}, f32[2,8,16,128]{3,2,1,0:T(8,128)S(1)}, u32[]{:S(2)}, u32[]{:S(2)}) %collective-permute-start.4) | collective-permute-done | bytes 131104 | tf_op jit(solution)/shard_map/ppermute | solution.py:571
  37.4 2.5 %collective-permute-done.5.r3_ref = f32[2,8,16,128]{3,2,1,0:T(8,128)S(1)} collective-permute-done((f32[2,8,16,128]{3,2,1,0:T(8,128)S(1)}, f32[2,8,16,128]{3,2,1,0:T(8,128)S(1)}, u32[]{:S(2)}, u32[]{:S(2)}) %collective-permute-start.5) | collective-permute-done | bytes 131104 | tf_op jit(solution)/shard_map/ppermute | solution.py:571
  41.6 3.1 %collective-permute-start.12 = (f32[2,2,8,8,1024]{4,3,2,1,0:T(8,128)}, f32[2,2,8,8,1024]{4,3,2,1,0:T(8,128)S(1)}, u32[]{:S(2)}, u32[]{:S(2)}) collective-permute-start(f32[2,2,8,8,1024]{4,3,2,1,0:T(8,128)} %get-tuple-element.51), channel_id=1, source_target_pairs={{0,1},{1,2},{2,3},{3,4},{4,5},{5,6},{6,7},{7,8},{8,9},{9,10},{10,1... | collective-permute-start | bytes 3145736 | tf_op jit(solution)/shard_map/ppermute | solution.py:562
  48.3 6.0 %two_steps.3 = (f32[32,8,8,1024]{3,2,1,0:T(8,128)}, f32[8,128]{1,0:T(8,128)S(1)}) custom-call(f32[32,8,8,1024]{3,2,1,0:T(8,128)} %u_ref.13, f32[1,2,8,8,1024]{4,3,2,1,0:T(8,128)S(1)} %collective-permute-done.6.before_ref, f32[1,2,8,8,1024]{4,3,2,1,0:T(8,128)} %collective-permute-done.7.after_ref, f32[8,8,1024]{2,1,0:T(8,128)S(1)} %copy-done, ...), custom_call_target="tpu_custom_call" | custom-call | bytes 8192 | tf_op jit(solution)/shard_map/two_steps/pallas_call | solution.py:276
  54.3 5.0 %collective-permute-start.17 = (f32[1,2,8,8,1024]{4,3,2,1,0:T(8,128)S(1)}, f32[1,2,8,8,1024]{4,3,2,1,0:T(8,128)S(1)}, u32[]{:S(2)}, u32[]{:S(2)}) collective-permute-start(f32[1,2,8,8,1024]{4,3,2,1,0:T(8,128)S(1)} %get-tuple-element.61), channel_id=1, source_target_pairs={{0,1},{1,2},{2,3},{3,4},{4,5},{5,6},{6,7},{7,8},{8,9},{9,10},{10,1... | collective-permute-start | bytes 1572872 | tf_op jit(solution)/shard_map/ppermute | solution.py:562
  63.2 3.2 %collective-permute-done.12.before_ref = f32[2,2,8,8,1024]{4,3,2,1,0:T(8,128)S(1)} collective-permute-done((f32[2,2,8,8,1024]{4,3,2,1,0:T(8,128)}, f32[2,2,8,8,1024]{4,3,2,1,0:T(8,128)S(1)}, u32[]{:S(2)}, u32[]{:S(2)}) %collective-permute-start.12) | collective-permute-done | bytes 1048608 | tf_op jit(solution)/shard_map/ppermute | solution.py:562
  67.0 4.2 %collective-permute-done.13.after_ref = f32[2,2,8,8,1024]{4,3,2,1,0:T(8,128)S(1)} collective-permute-done((f32[2,2,8,8,1024]{4,3,2,1,0:T(8,128)S(1)}, f32[2,2,8,8,1024]{4,3,2,1,0:T(8,128)S(1)}, u32[]{:S(2)}, u32[]{:S(2)}) %collective-permute-start.13) | collective-permute-done | bytes 1048608 | tf_op jit(solution)/shard_map/ppermute | solution.py:567
  72.2 10.1 %two_steps.4 = (f32[32,8,8,1024]{3,2,1,0:T(8,128)}, f32[8,128]{1,0:T(8,128)S(1)}) custom-call(f32[32,8,8,1024]{3,2,1,0:T(8,128)} %u_ref.13, f32[2,2,8,8,1024]{4,3,2,1,0:T(8,128)} %copy-done.8, f32[2,2,8,8,1024]{4,3,2,1,0:T(8,128)} %copy-done.9, f32[8,8,1024]{2,1,0:T(8,128)S(1)} %copy-done, ...), custom_call_target="tpu_custom_call", output_to_operand_aliasing={{0}: (6, {})} | custom-call | bytes 16384 | tf_op jit(solution)/shard_map/two_steps/pallas_call | solution.py:276
  82.4 3.5 %collective-permute-start.14 = (f32[72,128]{1,0:T(8,128)S(1)}, f32[72,128]{1,0:T(8,128)S(1)}, u32[]{:S(2)}, u32[]{:S(2)}) collective-permute-start(f32[72,128]{1,0:T(8,128)S(1)} %add_up.3.a_ref), channel_id=1, source_target_pairs={{0,4},{1,5},{2,6},{3,7},{4,0},{5,1},{6,2},{7,3},{8,12},{9,13},{10,... | collective-permute-start | bytes 110600 | tf_op jit(solution)/shard_map/ppermute | solution.py:571
  85.9 3.6 %collective-permute-start.15 = (f32[72,128]{1,0:T(8,128)S(1)}, f32[72,128]{1,0:T(8,128)S(1)}, u32[]{:S(2)}, u32[]{:S(2)}) collective-permute-start(f32[72,128]{1,0:T(8,128)S(1)} %add_up.3.a_ref), channel_id=1, source_target_pairs={{0,8},{1,9},{2,10},{3,11},{4,12},{5,13},{6,14},{7,15},{8,0},{9,1},... | collective-permute-start | bytes 110600 | tf_op jit(solution)/shard_map/ppermute | solution.py:571
  89.5 1.7 %collective-permute-done.15.c_ref = f32[72,128]{1,0:T(8,128)S(1)} collective-permute-done((f32[72,128]{1,0:T(8,128)S(1)}, f32[72,128]{1,0:T(8,128)S(1)}, u32[]{:S(2)}, u32[]{:S(2)}) %collective-permute-start.15) | collective-permute-done | bytes 36896 | tf_op jit(solution)/shard_map/ppermute | solution.py:571
  91.2 2.3 %collective-permute-done.16.d_ref = f32[72,128]{1,0:T(8,128)S(1)} collective-permute-done((f32[72,128]{1,0:T(8,128)S(1)}, f32[72,128]{1,0:T(8,128)S(1)}, u32[]{:S(2)}, u32[]{:S(2)}) %collective-permute-start.16) | collective-permute-done | bytes 36896 | tf_op jit(solution)/shard_map/ppermute | solution.py:571
  94.2 3.9 %collective-permute-start.20 = (f32[72,128]{1,0:T(8,128)S(1)}, f32[72,128]{1,0:T(8,128)S(1)}, u32[]{:S(2)}, u32[]{:S(2)}) collective-permute-start(f32[72,128]{1,0:T(8,128)S(1)} %add_up.4.rest_1_.a_ref), channel_id=1, source_target_pairs={{0,2},{1,3},{2,0},{3,1},{4,6},{5,7},{6,4},{7,5},{8,10},{9,11},{10,... | collective-permute-start | bytes 110600 | tf_op jit(solution)/shard_map/ppermute | solution.py:571
  98.1 6.0 %two_steps.5 = (f32[32,8,8,1024]{3,2,1,0:T(8,128)}, f32[8,128]{1,0:T(8,128)S(1)}) custom-call(f32[32,8,8,1024]{3,2,1,0:T(8,128)} %u_ref.13, f32[1,2,8,8,1024]{4,3,2,1,0:T(8,128)S(1)} %collective-permute-done.17.before_ref, f32[1,2,8,8,1024]{4,3,2,1,0:T(8,128)} %copy-done.10, f32[8,8,1024]{2,1,0:T(8,128)S(1)} %copy-done, ...), custom_call_target="tpu_custom_call", output_to_operand_aliasing={{0}: (6, {})} | custom-call | bytes 8192 | tf_op jit(solution)/shard_map/two_steps/pallas_call | solution.py:276
  104.1 5.6 %collective-permute-start.22 = (f32[72,128]{1,0:T(8,128)S(1)}, f32[72,128]{1,0:T(8,128)S(1)}, u32[]{:S(2)}, u32[]{:S(2)}) collective-permute-start(f32[72,128]{1,0:T(8,128)S(1)} %add_up.5), channel_id=1, source_target_pairs={{0,16},{16,0},{32,48},{48,32},{64,80},{80,64},{96,112},{112,96},{1... | collective-permute-start | bytes 110600 | tf_op jit(solution)/shard_map/ppermute | solution.py:571
  110.5 4.2 %analysis.1 = f32[8,128]{1,0:T(8,128)} custom-call(f32[144,128]{1,0:T(8,128)S(1)} %maximum_select_fusion.sums_ref, f32[64,128]{1,0:T(8,128)S(1)} %get-tuple-element.69.mix0_ref, f32[32,64]{1,0:T(8,128)S(1)} %get-tuple-element.70.mix1_ref, f32[16,32]{1,0:T(8,128)S(1)} %get-tuple-element.71.mix2_ref, f32[128,1024]{1,0:T(8,128)S(1)} %get-tuple-element.72.s_ref, ...), custom_call_target="tpu_custom_call" | custom-call | bytes 16384 | tf_op jit(solution)/shard_map/analysis/pallas_call | solution.py:533
  (67 shorter events, 19.9 us)
Async XLA Ops:
  0.6 22.1 %copy-start = (f32[8,8,1024]{2,1,0:T(8,128)S(1)}, f32[8,8,1024]{2,1,0:T(8,128)}, u32[]{:S(2)}) copy-start(f32[8,8,1024]{2,1,0:T(8,128)} %k_ref.9) | copy-start | bytes 786436
  5.6 17.1 %collective-permute-start.1 = (f32[56,1024]{1,0:T(8,128)}, f32[56,1024]{1,0:T(8,128)S(1)}, u32[]{:S(2)}, u32[]{:S(2)}) collective-permute-start(f32[56,1024]{1,0:T(8,128)} %get-tuple-element.40.rest_0_), channel_id=1, source_target_pairs={{1,0},{2,1},{3,2},{4,3},{5,4},{6,5},{7,6},{8,7},{9,8},{10,9},{11,1... | collective-permute-start | bytes 688136 | tf_op jit(solution)/shard_map/ppermute | solution.py:567
  7.1 15.7 %collective-permute-start = (f32[56,1024]{1,0:T(8,128)}, f32[56,1024]{1,0:T(8,128)S(1)}, u32[]{:S(2)}, u32[]{:S(2)}) collective-permute-start(f32[56,1024]{1,0:T(8,128)} %get-tuple-element.39), channel_id=1, source_target_pairs={{0,1},{1,2},{2,3},{3,4},{4,5},{5,6},{6,7},{7,8},{8,9},{9,10},{10,1... | collective-permute-start | bytes 688136 | tf_op jit(solution)/shard_map/ppermute | solution.py:562
  14.8 19.5 %collective-permute-start.7 = (f32[1,2,8,8,1024]{4,3,2,1,0:T(8,128)S(1)}, f32[1,2,8,8,1024]{4,3,2,1,0:T(8,128)}, u32[]{:S(2)}, u32[]{:S(2)}) collective-permute-start(f32[1,2,8,8,1024]{4,3,2,1,0:T(8,128)S(1)} %get-tuple-element.41.rest_0_), channel_id=1, source_target_pairs={{1,0},{2,1},{3,2},{4,3},{5,4},{6,5},{7,6},{8,7},{9,8},{10,9},{11,1... | collective-permute-start | bytes 1572872 | tf_op jit(solution)/shard_map/ppermute | solution.py:567
  16.1 18.2 %collective-permute-start.6 = (f32[1,2,8,8,1024]{4,3,2,1,0:T(8,128)}, f32[1,2,8,8,1024]{4,3,2,1,0:T(8,128)S(1)}, u32[]{:S(2)}, u32[]{:S(2)}) collective-permute-start(f32[1,2,8,8,1024]{4,3,2,1,0:T(8,128)} %get-tuple-element.45), channel_id=1, source_target_pairs={{0,1},{1,2},{2,3},{3,4},{4,5},{5,6},{6,7},{7,8},{8,9},{9,10},{10,1... | collective-permute-start | bytes 1572872 | tf_op jit(solution)/shard_map/ppermute | solution.py:562
  24.0 3.2 %collective-permute-start.2 = (f32[4,8,16,128]{3,2,1,0:T(8,128)S(1)}, f32[4,8,16,128]{3,2,1,0:T(8,128)S(1)}, u32[]{:S(2)}, u32[]{:S(2)}) collective-permute-start(f32[4,8,16,128]{3,2,1,0:T(8,128)S(1)} %get-tuple-element.78), channel_id=1, source_target_pairs={{0,16},{16,0},{32,48},{48,32},{64,80},{80,64},{96,112},{112,96},{1... | collective-permute-start | bytes 786440 | tf_op jit(solution)/shard_map/ppermute | solution.py:571
  27.2 7.2 %collective-permute-start.3 = (f32[2,8,16,128]{3,2,1,0:T(8,128)S(1)}, f32[2,8,16,128]{3,2,1,0:T(8,128)S(1)}, u32[]{:S(2)}, u32[]{:S(2)}) collective-permute-start(f32[2,8,16,128]{3,2,1,0:T(8,128)S(1)} %get-tuple-element.76), channel_id=1, source_target_pairs={{0,32},{16,48},{32,0},{48,16},{64,96},{80,112},{96,64},{112,80},{1... | collective-permute-start | bytes 393224 | tf_op jit(solution)/shard_map/ppermute | solution.py:571
  28.7 8.7 %collective-permute-start.4 = (f32[2,8,16,128]{3,2,1,0:T(8,128)S(1)}, f32[2,8,16,128]{3,2,1,0:T(8,128)S(1)}, u32[]{:S(2)}, u32[]{:S(2)}) collective-permute-start(f32[2,8,16,128]{3,2,1,0:T(8,128)S(1)} %get-tuple-element.77), channel_id=1, source_target_pairs={{0,64},{16,80},{32,96},{48,112},{64,0},{80,16},{96,32},{112,48},{1... | collective-permute-start | bytes 393224 | tf_op jit(solution)/shard_map/ppermute | solution.py:571
  31.3 8.6 %collective-permute-start.5 = (f32[2,8,16,128]{3,2,1,0:T(8,128)S(1)}, f32[2,8,16,128]{3,2,1,0:T(8,128)S(1)}, u32[]{:S(2)}, u32[]{:S(2)}) collective-permute-start(f32[2,8,16,128]{3,2,1,0:T(8,128)S(1)} %get-tuple-element.74), channel_id=1, source_target_pairs={{0,96},{16,112},{32,64},{48,80},{64,32},{80,48},{96,0},{112,16},{1... | collective-permute-start | bytes 393224 | tf_op jit(solution)/shard_map/ppermute | solution.py:571
  41.6 24.8 %collective-permute-start.12 = (f32[2,2,8,8,1024]{4,3,2,1,0:T(8,128)}, f32[2,2,8,8,1024]{4,3,2,1,0:T(8,128)S(1)}, u32[]{:S(2)}, u32[]{:S(2)}) collective-permute-start(f32[2,2,8,8,1024]{4,3,2,1,0:T(8,128)} %get-tuple-element.51), channel_id=1, source_target_pairs={{0,1},{1,2},{2,3},{3,4},{4,5},{5,6},{6,7},{7,8},{8,9},{9,10},{10,1... | collective-permute-start | bytes 3145736 | tf_op jit(solution)/shard_map/ppermute | solution.py:562
  44.7 26.5 %collective-permute-start.13 = (f32[2,2,8,8,1024]{4,3,2,1,0:T(8,128)S(1)}, f32[2,2,8,8,1024]{4,3,2,1,0:T(8,128)S(1)}, u32[]{:S(2)}, u32[]{:S(2)}) collective-permute-start(f32[2,2,8,8,1024]{4,3,2,1,0:T(8,128)S(1)} %get-tuple-element.52.rest_0_), channel_id=1, source_target_pairs={{1,0},{2,1},{3,2},{4,3},{5,4},{6,5},{7,6},{8,7},{9,8},{10,9},{11,1... | collective-permute-start | bytes 3145736 | tf_op jit(solution)/shard_map/ppermute | solution.py:567
  54.3 39.2 %collective-permute-start.17 = (f32[1,2,8,8,1024]{4,3,2,1,0:T(8,128)S(1)}, f32[1,2,8,8,1024]{4,3,2,1,0:T(8,128)S(1)}, u32[]{:S(2)}, u32[]{:S(2)}) collective-permute-start(f32[1,2,8,8,1024]{4,3,2,1,0:T(8,128)S(1)} %get-tuple-element.61), channel_id=1, source_target_pairs={{0,1},{1,2},{2,3},{3,4},{4,5},{5,6},{6,7},{7,8},{8,9},{9,10},{10,1... | collective-permute-start | bytes 1572872 | tf_op jit(solution)/shard_map/ppermute | solution.py:562
  59.3 34.2 %collective-permute-start.18 = (f32[1,2,8,8,1024]{4,3,2,1,0:T(8,128)S(1)}, f32[1,2,8,8,1024]{4,3,2,1,0:T(8,128)S(1)}, u32[]{:S(2)}, u32[]{:S(2)}) collective-permute-start(f32[1,2,8,8,1024]{4,3,2,1,0:T(8,128)S(1)} %copy-done.3), channel_id=1, source_target_pairs={{1,0},{2,1},{3,2},{4,3},{5,4},{6,5},{7,6},{8,7},{9,8},{10,9},{11,1... | collective-permute-start | bytes 1572872 | tf_op jit(solution)/shard_map/ppermute | solution.py:567
  60.7 2.5 %collective-permute-start.8 = (f32[72,128]{1,0:T(8,128)S(1)}, f32[72,128]{1,0:T(8,128)S(1)}, u32[]{:S(2)}, u32[]{:S(2)}) collective-permute-start(f32[72,128]{1,0:T(8,128)S(1)} %dynamic-slice_bitcast_fusion.1), channel_id=1, source_target_pairs={{0,16},{16,0},{32,48},{48,32},{64,80},{80,64},{96,112},{112,96},{1... | collective-permute-start | bytes 110600 | tf_op jit(solution)/shard_map/ppermute | solution.py:571
  63.2 19.2 %collective-permute-start.10 = (f32[72,128]{1,0:T(8,128)S(1)}, f32[72,128]{1,0:T(8,128)S(1)}, u32[]{:S(2)}, u32[]{:S(2)}) collective-permute-start(f32[72,128]{1,0:T(8,128)S(1)} %bitcast_add_fusion.a_ref), channel_id=1, source_target_pairs={{0,64},{16,80},{32,96},{48,112},{64,0},{80,16},{96,32},{112,48},{1... | collective-permute-start | bytes 110600 | tf_op jit(solution)/shard_map/ppermute | solution.py:571
  66.4 16.0 %collective-permute-start.11 = (f32[72,128]{1,0:T(8,128)S(1)}, f32[72,128]{1,0:T(8,128)S(1)}, u32[]{:S(2)}, u32[]{:S(2)}) collective-permute-start(f32[72,128]{1,0:T(8,128)S(1)} %bitcast_add_fusion.a_ref), channel_id=1, source_target_pairs={{0,96},{16,112},{32,64},{48,80},{64,32},{80,48},{96,0},{112,16},{1... | collective-permute-start | bytes 110600 | tf_op jit(solution)/shard_map/ppermute | solution.py:571
  71.3 11.1 %collective-permute-start.9 = (f32[72,128]{1,0:T(8,128)S(1)}, f32[72,128]{1,0:T(8,128)S(1)}, u32[]{:S(2)}, u32[]{:S(2)}) collective-permute-start(f32[72,128]{1,0:T(8,128)S(1)} %bitcast_add_fusion.a_ref), channel_id=1, source_target_pairs={{0,32},{16,48},{32,0},{48,16},{64,96},{80,112},{96,64},{112,80},{1... | collective-permute-start | bytes 110600 | tf_op jit(solution)/shard_map/ppermute | solution.py:571
  82.4 7.1 %collective-permute-start.14 = (f32[72,128]{1,0:T(8,128)S(1)}, f32[72,128]{1,0:T(8,128)S(1)}, u32[]{:S(2)}, u32[]{:S(2)}) collective-permute-start(f32[72,128]{1,0:T(8,128)S(1)} %add_up.3.a_ref), channel_id=1, source_target_pairs={{0,4},{1,5},{2,6},{3,7},{4,0},{5,1},{6,2},{7,3},{8,12},{9,13},{10,... | collective-permute-start | bytes 110600 | tf_op jit(solution)/shard_map/ppermute | solution.py:571
  85.9 5.3 %collective-permute-start.15 = (f32[72,128]{1,0:T(8,128)S(1)}, f32[72,128]{1,0:T(8,128)S(1)}, u32[]{:S(2)}, u32[]{:S(2)}) collective-permute-start(f32[72,128]{1,0:T(8,128)S(1)} %add_up.3.a_ref), channel_id=1, source_target_pairs={{0,8},{1,9},{2,10},{3,11},{4,12},{5,13},{6,14},{7,15},{8,0},{9,1},... | collective-permute-start | bytes 110600 | tf_op jit(solution)/shard_map/ppermute | solution.py:571
  89.5 4.0 %collective-permute-start.16 = (f32[72,128]{1,0:T(8,128)S(1)}, f32[72,128]{1,0:T(8,128)S(1)}, u32[]{:S(2)}, u32[]{:S(2)}) collective-permute-start(f32[72,128]{1,0:T(8,128)S(1)} %add_up.3.a_ref), channel_id=1, source_target_pairs={{0,12},{1,13},{2,14},{3,15},{4,8},{5,9},{6,10},{7,11},{8,4},{9,5},... | collective-permute-start | bytes 110600 | tf_op jit(solution)/shard_map/ppermute | solution.py:571
  93.6 10.5 %collective-permute-start.19 = (f32[72,128]{1,0:T(8,128)S(1)}, f32[72,128]{1,0:T(8,128)S(1)}, u32[]{:S(2)}, u32[]{:S(2)}) collective-permute-start(f32[72,128]{1,0:T(8,128)S(1)} %add_up.4.rest_1_.a_ref), channel_id=1, source_target_pairs={{0,1},{1,0},{2,3},{3,2},{4,5},{5,4},{6,7},{7,6},{8,9},{9,8},{10,11... | collective-permute-start | bytes 110600 | tf_op jit(solution)/shard_map/ppermute | solution.py:571
  94.2 9.9 %collective-permute-start.20 = (f32[72,128]{1,0:T(8,128)S(1)}, f32[72,128]{1,0:T(8,128)S(1)}, u32[]{:S(2)}, u32[]{:S(2)}) collective-permute-start(f32[72,128]{1,0:T(8,128)S(1)} %add_up.4.rest_1_.a_ref), channel_id=1, source_target_pairs={{0,2},{1,3},{2,0},{3,1},{4,6},{5,7},{6,4},{7,5},{8,10},{9,11},{10,... | collective-permute-start | bytes 110600 | tf_op jit(solution)/shard_map/ppermute | solution.py:571
  98.1 6.0 %collective-permute-start.21 = (f32[72,128]{1,0:T(8,128)S(1)}, f32[72,128]{1,0:T(8,128)S(1)}, u32[]{:S(2)}, u32[]{:S(2)}) collective-permute-start(f32[72,128]{1,0:T(8,128)S(1)} %add_up.4.rest_1_.a_ref), channel_id=1, source_target_pairs={{0,3},{1,2},{2,1},{3,0},{4,7},{5,6},{6,5},{7,4},{8,11},{9,10},{10,... | collective-permute-start | bytes 110600 | tf_op jit(solution)/shard_map/ppermute | solution.py:571
  104.1 6.4 %collective-permute-start.22 = (f32[72,128]{1,0:T(8,128)S(1)}, f32[72,128]{1,0:T(8,128)S(1)}, u32[]{:S(2)}, u32[]{:S(2)}) collective-permute-start(f32[72,128]{1,0:T(8,128)S(1)} %add_up.5), channel_id=1, source_target_pairs={{0,16},{16,0},{32,48},{48,32},{64,80},{80,64},{96,112},{112,96},{1... | collective-permute-start | bytes 110600 | tf_op jit(solution)/shard_map/ppermute | solution.py:571
  (11 other events, 118.9 us)

commit v5 on v2

--- a/solution.py
+++ b/solution.py
@@ -15,7 +15,7 @@
 ROWS = 8
 LIMIT = 16 << 20
 LARGE = 105 << 19
-CHUNKS = (2, 2)
+CHUNKS = (1, 3)
 F32 = jnp.float32
 
 
@@ -597,9 +597,9 @@
 
     own = pair_for(0)
     r1, r3, r2 = (across(pair_for(bits), "grp", 2 * bits) for bits in (1, 3, 2))
-    lo, hi = pack(prior, 8 * CHUNKS[0], CHUNKS[1], own)
+    lo, hi = pack(prior, 8 * CHUNKS[0], CHUNKS[1], r1)
+    r1, r2, r3, *arrived_a = lax.optimization_barrier((r1, r2, r3, *arrived_a))
     part, sketches, mean = gram(place, obs, own, r1, r2, r3, lo)
-    lo, hi, part = lax.optimization_barrier((lo, hi, part))
 
     half = part.reshape(2, -1, part.shape[1])
     total = lax.dynamic_index_in_dim(half, core, 0, False) + across(

time: 105 us -> 140 us (1.33)
  waiting for transfers between devices: 21.1 us -> 48.4 us
  starting transfers between devices: 40.9 us -> 46.1 us
  local copies, waits for them, and re-layouts: 1.76 us -> 4.14 us
    ppermute x3, waiting for transfers between devices: 4.6 us -> 34.2 us  [to_next(): return lax.ppermute(v, 'tile', [(i, i + 1) for i in range(size - 1)])]
    ppermute x15, starting transfers between devices: 25.7 us -> 31.1 us  [across(): lax.ppermute(v, axis, [(i, i ^ bits) for i in range(lax.axis_size(axis))])]
    ppermute x15, waiting for transfers between devices: 14.2 us -> 11.1 us  [across(): lax.ppermute(v, axis, [(i, i ^ bits) for i in range(lax.axis_size(axis))])]
    unnamed x19 -> x21, local copies, waits for them, and re-layouts: 1.69 us -> 4.06 us
  transfers between devices with their start and end apart: 21 -> 21, of which waited for: 8 -> 10; matrix products, arithmetic and copies ran while one was open for 0% -> 0% of each run, Pallas kernels for 28% -> 18%
where the time goes in v5:
time: 140 us; the launch traced here: 139 us
  waiting for transfers between devices  48.4 us (35%)
  starting transfers between devices  46.1 us (33%)
  Pallas kernels  39.7 us (28%)
  local copies, waits for them, and re-layouts  4.14 us (3%)
    ppermute x3, waiting for transfers between devices, to_next(): return lax.ppermute(v, 'tile', [(i, i + 1) for i in range(size - 1)])  34.2 us
    ppermute x15, starting transfers between devices, across(): lax.ppermute(v, axis, [(i, i ^ bits) for i in range(lax.axis_size(axis))])  31.1 us
    pallas_call x2, Pallas kernels, two_steps(): pl.pallas_call(functools.partial(step_kernel, first), in_specs=specs + [A...  19.7 us
    ppermute x3, starting transfers between devices, to_next(): return lax.ppermute(v, 'tile', [(i, i + 1) for i in range(size - 1)])  11.2 us
    ppermute x15, waiting for transfers between devices, across(): lax.ppermute(v, axis, [(i, i ^ bits) for i in range(lax.axis_size(axis))])  11.1 us
    pallas_call x2, Pallas kernels, pack(): pl.pallas_call(functools.partial(pack_kernel, first), in_specs=[HBM] + [A...  5.84 us
    pallas_call x1, Pallas kernels, pair_sums(): pl.pallas_call(pair_kernel, in_specs=[SMEM, HBM, HBM], out_specs=[VMEM] *...  4.8 us
    pallas_call x1, Pallas kernels, analysis(): pl.pallas_call(analysis_kernel, in_specs=[VMEM] * 6, out_specs=VMEM, out_...  4.19 us
  transfers between devices with their start and end apart: 21, of which 10 were waited for; matrix products, arithmetic and copies ran while one was open for 0% of the time, Pallas kernels for 18%

profile of v5, /device:TPU:1, one launch (start us, length us, event | category | flops | bytes accessed | tf_op | source)
XLA Modules:
  0.0 139.4 jit_solution(6952307010871176325)
XLA Ops:
  0.6 4.8 %pair_sums.1 = (f32[3,8,16,1024]{3,2,1,0:T(8,128)}, f32[56,1024]{1,0:T(8,128)}, f32[56,1024]{1,0:T(8,128)}) custom-call(s32[32]{0:T(128)} %slot_ref.1, f32[8,8,1024]{2,1,0:T(8,128)} %k_ref.7, f32[32,8,8,1024]{3,2,1,0:T(8,128)} %u_ref.9), custom_call_target="tpu_custom_call" | custom-call | bytes 6291456 | tf_op jit(solution)/shard_map/pair_sums/pallas_call | solution.py:91
  5.4 4.0 %collective-permute-start = (f32[56,1024]{1,0:T(8,128)}, f32[56,1024]{1,0:T(8,128)S(1)}, u32[]{:S(2)}, u32[]{:S(2)}) collective-permute-start(f32[56,1024]{1,0:T(8,128)} %get-tuple-element.26), channel_id=1, source_target_pairs={{0,1},{1,2},{2,3},{3,4},{4,5},{5,6},{6,7},{7,8},{8,9},{9,10},{10,1... | collective-permute-start | bytes 688136 | tf_op jit(solution)/shard_map/ppermute | solution.py:561
  11.7 1.6 %pack_edges.2 = (f32[1,2,8,8,1024]{4,3,2,1,0:T(8,128)S(1)}, f32[1,2,8,8,1024]{4,3,2,1,0:T(8,128)S(1)}) custom-call(f32[32,8,8,1024]{3,2,1,0:T(8,128)} %u_ref.9, f32[56,1024]{1,0:T(8,128)S(1)} %copy-done.5), custom_call_target="tpu_custom_call" | custom-call | bytes 2097152 | tf_op jit(solution)/shard_map/pack_edges/pallas_call | solution.py:134
  13.5 2.4 %sensor_sums.1 = (f32[16,128]{1,0:T(8,128)S(1)}, f32[64,128]{1,0:T(8,128)S(1)}, f32[32,64]{1,0:T(8,128)S(1)}, f32[16,32]{1,0:T(8,128)S(1)}) custom-call(s32[2]{0:T(128)S(1)} %pad_add_fusion.at_ref.place_ref, s32[32,128]{1,0:T(8,128)S(1)} %bitcast.25, f32[32,128]{1,0:T(8,128)S(1)} %bitcast.26, f32[32,128]{1,0:T(8,128)S(1)} %bitcast.27, ...), custom_call_target="tpu_custom_call" | custom-call | bytes 4194304 | tf_op jit(solution)/shard_map/sensor_sums/pallas_call | solution.py:387
  15.8 1.8 %collective-permute-done.1.after_ref = f32[56,1024]{1,0:T(8,128)S(1)} collective-permute-done((f32[56,1024]{1,0:T(8,128)}, f32[56,1024]{1,0:T(8,128)S(1)}, u32[]{:S(2)}, u32[]{:S(2)}) %collective-permute-start.1) | collective-permute-done | bytes 229408 | tf_op jit(solution)/shard_map/ppermute | solution.py:566
  18.9 1.9 %collective-permute-start.2 = (f32[4,8,16,128]{3,2,1,0:T(8,128)S(1)}, f32[4,8,16,128]{3,2,1,0:T(8,128)S(1)}, u32[]{:S(2)}, u32[]{:S(2)}) collective-permute-start(f32[4,8,16,128]{3,2,1,0:T(8,128)S(1)} %get-tuple-element.52), channel_id=1, source_target_pairs={{0,16},{16,0},{32,48},{48,32},{64,80},{80,64},{96,112},{112,96},{1... | collective-permute-start | bytes 786440 | tf_op jit(solution)/shard_map/ppermute | solution.py:570
  23.4 3.4 %collective-permute-done.3.rest_0_.r1_ref = f32[2,8,16,128]{3,2,1,0:T(8,128)S(1)} collective-permute-done((f32[2,8,16,128]{3,2,1,0:T(8,128)S(1)}, f32[2,8,16,128]{3,2,1,0:T(8,128)S(1)}, u32[]{:S(2)}, u32[]{:S(2)}) %collective-permute-start.3) | collective-permute-done | bytes 131104 | tf_op jit(solution)/shard_map/ppermute | solution.py:570
  26.8 4.3 %pack_edges.3 = (f32[3,2,8,8,1024]{4,3,2,1,0:T(8,128)}, f32[3,2,8,8,1024]{4,3,2,1,0:T(8,128)}) custom-call(f32[32,8,8,1024]{3,2,1,0:T(8,128)} %u_ref.9, f32[2,8,16,128]{3,2,1,0:T(8,128)S(1)} %collective-permute-done.3.rest_0_.r1_ref), custom_call_target="tpu_custom_call" | custom-call | bytes 6291456 | tf_op jit(solution)/shard_map/pack_edges/pallas_call | solution.py:134
  31.1 3.2 %collective-permute-start.4 = (f32[3,2,8,8,1024]{4,3,2,1,0:T(8,128)}, f32[3,2,8,8,1024]{4,3,2,1,0:T(8,128)S(1)}, u32[]{:S(2)}, u32[]{:S(2)}) collective-permute-start(f32[3,2,8,8,1024]{4,3,2,1,0:T(8,128)} %get-tuple-element.30), channel_id=1, source_target_pairs={{0,1},{1,2},{2,3},{3,4},{4,5},{5,6},{6,7},{7,8},{8,9},{9,10},{10,1... | collective-permute-start | bytes 4718600 | tf_op jit(solution)/shard_map/ppermute | solution.py:561
  35.6 4.0 %collective-permute-start.8 = (f32[1,2,8,8,1024]{4,3,2,1,0:T(8,128)S(1)}, f32[1,2,8,8,1024]{4,3,2,1,0:T(8,128)S(1)}, u32[]{:S(2)}, u32[]{:S(2)}) collective-permute-start(f32[1,2,8,8,1024]{4,3,2,1,0:T(8,128)S(1)} %get-tuple-element.32), channel_id=1, source_target_pairs={{0,1},{1,2},{2,3},{3,4},{4,5},{5,6},{6,7},{7,8},{8,9},{9,10},{10,1... | collective-permute-start | bytes 1572872 | tf_op jit(solution)/shard_map/ppermute | solution.py:561
  40.9 3.0 %collective-permute-start.6 = (f32[2,8,16,128]{3,2,1,0:T(8,128)S(1)}, f32[2,8,16,128]{3,2,1,0:T(8,128)S(1)}, u32[]{:S(2)}, u32[]{:S(2)}) collective-permute-start(f32[2,8,16,128]{3,2,1,0:T(8,128)S(1)} %get-tuple-element.50), channel_id=1, source_target_pairs={{0,64},{16,80},{32,96},{48,112},{64,0},{80,16},{96,32},{112,48},{1... | collective-permute-start | bytes 393224 | tf_op jit(solution)/shard_map/ppermute | solution.py:570
  43.9 34.2 %collective-permute-done.8.before_ref = f32[1,2,8,8,1024]{4,3,2,1,0:T(8,128)S(1)} collective-permute-done((f32[1,2,8,8,1024]{4,3,2,1,0:T(8,128)S(1)}, f32[1,2,8,8,1024]{4,3,2,1,0:T(8,128)S(1)}, u32[]{:S(2)}, u32[]{:S(2)}) %collective-permute-start.8) | collective-permute-done | bytes 524320 | tf_op jit(solution)/shard_map/ppermute | solution.py:561
  78.1 2.7 %collective-permute-start.7 = (f32[2,8,16,128]{3,2,1,0:T(8,128)S(1)}, f32[2,8,16,128]{3,2,1,0:T(8,128)S(1)}, u32[]{:S(2)}, u32[]{:S(2)}) collective-permute-start(f32[2,8,16,128]{3,2,1,0:T(8,128)S(1)} %get-tuple-element.51), channel_id=1, source_target_pairs={{0,96},{16,112},{32,64},{48,80},{64,32},{80,48},{96,0},{112,16},{1... | collective-permute-start | bytes 393224 | tf_op jit(solution)/shard_map/ppermute | solution.py:570
  83.2 1.4 %copy-done.3 = f32[3,2,8,8,1024]{4,3,2,1,0:T(8,128)S(1)} copy-done((f32[3,2,8,8,1024]{4,3,2,1,0:T(8,128)S(1)}, f32[3,2,8,8,1024]{4,3,2,1,0:T(8,128)}, u32[]{:S(2)}) %copy-start.3) | copy-done | bytes 1572888
  84.6 1.7 %gram_sums.1 = (f32[144,128]{1,0:T(8,128)S(1)}, f32[128,1024]{1,0:T(8,128)S(1)}, f32[8,128]{1,0:T(8,128)S(1)}) custom-call(s32[2]{0:T(128)S(1)} %pad_add_fusion.at_ref.place_ref, f32[16,128]{1,0:T(8,128)S(1)} %get-tuple-element.29.rest_0_.obs_ref, f32[2,8,16,128]{3,2,1,0:T(8,128)S(1)} %get-tuple-element.48.own_ref, ...), custom_call_target="tpu_custom_call" | custom-call | bytes 4194304 | tf_op jit(solution)/shard_map/gram_sums/pallas_call | solution.py:440
  86.3 3.3 %collective-permute-start.10 = (f32[72,128]{1,0:T(8,128)S(1)}, f32[72,128]{1,0:T(8,128)S(1)}, u32[]{:S(2)}, u32[]{:S(2)}) collective-permute-start(f32[72,128]{1,0:T(8,128)S(1)} %dynamic-slice_bitcast_fusion.1), channel_id=1, source_target_pairs={{0,16},{16,0},{32,48},{48,32},{64,80},{80,64},{96,112},{112,96},{1... | collective-permute-start | bytes 110600 | tf_op jit(solution)/shard_map/ppermute | solution.py:570
  90.5 2.7 %collective-permute-start.13 = (f32[72,128]{1,0:T(8,128)S(1)}, f32[72,128]{1,0:T(8,128)S(1)}, u32[]{:S(2)}, u32[]{:S(2)}) collective-permute-start(f32[72,128]{1,0:T(8,128)S(1)} %bitcast_add_fusion.a_ref), channel_id=1, source_target_pairs={{0,96},{16,112},{32,64},{48,80},{64,32},{80,48},{96,0},{112,16},{1... | collective-permute-start | bytes 110600 | tf_op jit(solution)/shard_map/ppermute | solution.py:570
  93.9 5.9 %two_steps.2 = (f32[32,8,8,1024]{3,2,1,0:T(8,128)}, f32[8,128]{1,0:T(8,128)S(1)}) custom-call(f32[32,8,8,1024]{3,2,1,0:T(8,128)} %u_ref.9, f32[1,2,8,8,1024]{4,3,2,1,0:T(8,128)S(1)} %collective-permute-done.8.before_ref, f32[1,2,8,8,1024]{4,3,2,1,0:T(8,128)S(1)} %collective-permute-done.9.after_ref, f32[8,8,1024]{2,1,0:T(8,128)S(1)} %copy-done.2, ...), custom_call_target="tpu_custom_call" | custom-call | bytes 8388608 | tf_op jit(solution)/shard_map/two_steps/pallas_call | solution.py:275
  99.9 8.0 %collective-permute-start.16 = (f32[72,128]{1,0:T(8,128)S(1)}, f32[72,128]{1,0:T(8,128)S(1)}, u32[]{:S(2)}, u32[]{:S(2)}) collective-permute-start(f32[72,128]{1,0:T(8,128)S(1)} %add_up.3.a_ref), channel_id=1, source_target_pairs={{0,12},{1,13},{2,14},{3,15},{4,8},{5,9},{6,10},{7,11},{8,4},{9,5},... | collective-permute-start | bytes 110600 | tf_op jit(solution)/shard_map/ppermute | solution.py:570
  109.3 3.0 %collective-permute-done.15.c_ref = f32[72,128]{1,0:T(8,128)S(1)} collective-permute-done((f32[72,128]{1,0:T(8,128)S(1)}, f32[72,128]{1,0:T(8,128)S(1)}, u32[]{:S(2)}, u32[]{:S(2)}) %collective-permute-start.15) | collective-permute-done | bytes 36896 | tf_op jit(solution)/shard_map/ppermute | solution.py:570
  114.3 2.9 %collective-permute-start.17 = (f32[72,128]{1,0:T(8,128)S(1)}, f32[72,128]{1,0:T(8,128)S(1)}, u32[]{:S(2)}, u32[]{:S(2)}) collective-permute-start(f32[72,128]{1,0:T(8,128)S(1)} %add_up.4.rest_1_.a_ref), channel_id=1, source_target_pairs={{0,1},{1,0},{2,3},{3,2},{4,5},{5,4},{6,7},{7,6},{8,9},{9,8},{10,11... | collective-permute-start | bytes 110600 | tf_op jit(solution)/shard_map/ppermute | solution.py:570
  117.1 13.8 %two_steps.3 = (f32[32,8,8,1024]{3,2,1,0:T(8,128)}, f32[8,128]{1,0:T(8,128)S(1)}) custom-call(f32[32,8,8,1024]{3,2,1,0:T(8,128)} %u_ref.9, f32[3,2,8,8,1024]{4,3,2,1,0:T(8,128)} %copy-done, f32[3,2,8,8,1024]{4,3,2,1,0:T(8,128)} %copy-done.1, f32[8,8,1024]{2,1,0:T(8,128)S(1)} %copy-done.2, ...), custom_call_target="tpu_custom_call", output_to_operand_aliasing={{0}: (6, {})} | custom-call | bytes 25165824 | tf_op jit(solution)/shard_map/two_steps/pallas_call | solution.py:275
  131.0 3.4 %collective-permute-start.20 = (f32[72,128]{1,0:T(8,128)S(1)}, f32[72,128]{1,0:T(8,128)S(1)}, u32[]{:S(2)}, u32[]{:S(2)}) collective-permute-start(f32[72,128]{1,0:T(8,128)S(1)} %add_up.5), channel_id=1, source_target_pairs={{0,16},{16,0},{32,48},{48,32},{64,80},{80,64},{96,112},{112,96},{1... | collective-permute-start | bytes 110600 | tf_op jit(solution)/shard_map/ppermute | solution.py:570
  135.2 4.2 %analysis.1 = f32[8,128]{1,0:T(8,128)} custom-call(f32[144,128]{1,0:T(8,128)S(1)} %maximum_select_fusion.sums_ref, f32[64,128]{1,0:T(8,128)S(1)} %get-tuple-element.43.mix0_ref, f32[32,64]{1,0:T(8,128)S(1)} %get-tuple-element.44.mix1_ref, f32[16,32]{1,0:T(8,128)S(1)} %get-tuple-element.45.mix2_ref, f32[128,1024]{1,0:T(8,128)S(1)} %get-tuple-element.46.s_ref, ...), custom_call_target="tpu_custom_call" | custom-call | bytes 16777216 | tf_op jit(solution)/shard_map/analysis/pallas_call | solution.py:532
  (59 shorter events, 17.0 us)
Async XLA Ops:
  5.4 10.4 %collective-permute-start = (f32[56,1024]{1,0:T(8,128)}, f32[56,1024]{1,0:T(8,128)S(1)}, u32[]{:S(2)}, u32[]{:S(2)}) collective-permute-start(f32[56,1024]{1,0:T(8,128)} %get-tuple-element.26), channel_id=1, source_target_pairs={{0,1},{1,2},{2,3},{3,4},{4,5},{5,6},{6,7},{7,8},{8,9},{9,10},{10,1... | collective-permute-start | bytes 688136 | tf_op jit(solution)/shard_map/ppermute | solution.py:561
  9.4 8.3 %collective-permute-start.1 = (f32[56,1024]{1,0:T(8,128)}, f32[56,1024]{1,0:T(8,128)S(1)}, u32[]{:S(2)}, u32[]{:S(2)}) collective-permute-start(f32[56,1024]{1,0:T(8,128)} %get-tuple-element.27.rest_0_), channel_id=1, source_target_pairs={{1,0},{2,1},{3,2},{4,3},{5,4},{6,5},{7,6},{8,7},{9,8},{10,9},{11,1... | collective-permute-start | bytes 688136 | tf_op jit(solution)/shard_map/ppermute | solution.py:566
  11.7 1.8 %copy-start.8 = (f32[4096]{0:T(1024)S(1)}, f32[4096]{0:T(1024)}, u32[]{:S(2)}) copy-start(f32[4096]{0:T(1024)} %param.13) | copy-start | bytes 49156
  11.7 6.0 %copy-start.2 = (f32[8,8,1024]{2,1,0:T(8,128)S(1)}, f32[8,8,1024]{2,1,0:T(8,128)}, u32[]{:S(2)}) copy-start(f32[8,8,1024]{2,1,0:T(8,128)} %k_ref.7) | copy-start | bytes 786436
  11.7 6.0 %copy-start.4 = (f32[3,8,16,1024]{3,2,1,0:T(8,128)S(1)}, f32[3,8,16,1024]{3,2,1,0:T(8,128)}, u32[]{:S(2)}) copy-start(f32[3,8,16,1024]{3,2,1,0:T(8,128)} %get-tuple-element.25.p_ref) | copy-start | bytes 4718596
  18.9 3.1 %collective-permute-start.2 = (f32[4,8,16,128]{3,2,1,0:T(8,128)S(1)}, f32[4,8,16,128]{3,2,1,0:T(8,128)S(1)}, u32[]{:S(2)}, u32[]{:S(2)}) collective-permute-start(f32[4,8,16,128]{3,2,1,0:T(8,128)S(1)} %get-tuple-element.52), channel_id=1, source_target_pairs={{0,16},{16,0},{32,48},{48,32},{64,80},{80,64},{96,112},{112,96},{1... | collective-permute-start | bytes 786440 | tf_op jit(solution)/shard_map/ppermute | solution.py:570
  22.0 4.8 %collective-permute-start.3 = (f32[2,8,16,128]{3,2,1,0:T(8,128)S(1)}, f32[2,8,16,128]{3,2,1,0:T(8,128)S(1)}, u32[]{:S(2)}, u32[]{:S(2)}) collective-permute-start(f32[2,8,16,128]{3,2,1,0:T(8,128)S(1)} %get-tuple-element.49), channel_id=1, source_target_pairs={{0,32},{16,48},{32,0},{48,16},{64,96},{80,112},{96,64},{112,80},{1... | collective-permute-start | bytes 393224 | tf_op jit(solution)/shard_map/ppermute | solution.py:570
  31.1 81.1 %collective-permute-start.4 = (f32[3,2,8,8,1024]{4,3,2,1,0:T(8,128)}, f32[3,2,8,8,1024]{4,3,2,1,0:T(8,128)S(1)}, u32[]{:S(2)}, u32[]{:S(2)}) collective-permute-start(f32[3,2,8,8,1024]{4,3,2,1,0:T(8,128)} %get-tuple-element.30), channel_id=1, source_target_pairs={{0,1},{1,2},{2,3},{3,4},{4,5},{5,6},{6,7},{7,8},{8,9},{9,10},{10,1... | collective-permute-start | bytes 4718600 | tf_op jit(solution)/shard_map/ppermute | solution.py:561
  34.3 77.9 %collective-permute-start.5 = (f32[3,2,8,8,1024]{4,3,2,1,0:T(8,128)}, f32[3,2,8,8,1024]{4,3,2,1,0:T(8,128)S(1)}, u32[]{:S(2)}, u32[]{:S(2)}) collective-permute-start(f32[3,2,8,8,1024]{4,3,2,1,0:T(8,128)} %get-tuple-element.31.rest_0_), channel_id=1, source_target_pairs={{1,0},{2,1},{3,2},{4,3},{5,4},{6,5},{7,6},{8,7},{9,8},{10,9},{11,1... | collective-permute-start | bytes 4718600 | tf_op jit(solution)/shard_map/ppermute | solution.py:566
  35.6 42.5 %collective-permute-start.8 = (f32[1,2,8,8,1024]{4,3,2,1,0:T(8,128)S(1)}, f32[1,2,8,8,1024]{4,3,2,1,0:T(8,128)S(1)}, u32[]{:S(2)}, u32[]{:S(2)}) collective-permute-start(f32[1,2,8,8,1024]{4,3,2,1,0:T(8,128)S(1)} %get-tuple-element.32), channel_id=1, source_target_pairs={{0,1},{1,2},{2,3},{3,4},{4,5},{5,6},{6,7},{7,8},{8,9},{9,10},{10,1... | collective-permute-start | bytes 1572872 | tf_op jit(solution)/shard_map/ppermute | solution.py:561
  39.6 42.4 %collective-permute-start.9 = (f32[1,2,8,8,1024]{4,3,2,1,0:T(8,128)S(1)}, f32[1,2,8,8,1024]{4,3,2,1,0:T(8,128)S(1)}, u32[]{:S(2)}, u32[]{:S(2)}) collective-permute-start(f32[1,2,8,8,1024]{4,3,2,1,0:T(8,128)S(1)} %get-tuple-element.28.rest_0_), channel_id=1, source_target_pairs={{1,0},{2,1},{3,2},{4,3},{5,4},{6,5},{7,6},{8,7},{9,8},{10,9},{11,1... | collective-permute-start | bytes 1572872 | tf_op jit(solution)/shard_map/ppermute | solution.py:566
  40.9 41.1 %collective-permute-start.6 = (f32[2,8,16,128]{3,2,1,0:T(8,128)S(1)}, f32[2,8,16,128]{3,2,1,0:T(8,128)S(1)}, u32[]{:S(2)}, u32[]{:S(2)}) collective-permute-start(f32[2,8,16,128]{3,2,1,0:T(8,128)S(1)} %get-tuple-element.50), channel_id=1, source_target_pairs={{0,64},{16,80},{32,96},{48,112},{64,0},{80,16},{96,32},{112,48},{1... | collective-permute-start | bytes 393224 | tf_op jit(solution)/shard_map/ppermute | solution.py:570
  78.1 5.1 %collective-permute-start.7 = (f32[2,8,16,128]{3,2,1,0:T(8,128)S(1)}, f32[2,8,16,128]{3,2,1,0:T(8,128)S(1)}, u32[]{:S(2)}, u32[]{:S(2)}) collective-permute-start(f32[2,8,16,128]{3,2,1,0:T(8,128)S(1)} %get-tuple-element.51), channel_id=1, source_target_pairs={{0,96},{16,112},{32,64},{48,80},{64,32},{80,48},{96,0},{112,16},{1... | collective-permute-start | bytes 393224 | tf_op jit(solution)/shard_map/ppermute | solution.py:570
  86.3 4.2 %collective-permute-start.10 = (f32[72,128]{1,0:T(8,128)S(1)}, f32[72,128]{1,0:T(8,128)S(1)}, u32[]{:S(2)}, u32[]{:S(2)}) collective-permute-start(f32[72,128]{1,0:T(8,128)S(1)} %dynamic-slice_bitcast_fusion.1), channel_id=1, source_target_pairs={{0,16},{16,0},{32,48},{48,32},{64,80},{80,64},{96,112},{112,96},{1... | collective-permute-start | bytes 110600 | tf_op jit(solution)/shard_map/ppermute | solution.py:570
  90.5 9.3 %collective-permute-start.13 = (f32[72,128]{1,0:T(8,128)S(1)}, f32[72,128]{1,0:T(8,128)S(1)}, u32[]{:S(2)}, u32[]{:S(2)}) collective-permute-start(f32[72,128]{1,0:T(8,128)S(1)} %bitcast_add_fusion.a_ref), channel_id=1, source_target_pairs={{0,96},{16,112},{32,64},{48,80},{64,32},{80,48},{96,0},{112,16},{1... | collective-permute-start | bytes 110600 | tf_op jit(solution)/shard_map/ppermute | solution.py:570
  93.2 6.6 %collective-permute-start.12 = (f32[72,128]{1,0:T(8,128)S(1)}, f32[72,128]{1,0:T(8,128)S(1)}, u32[]{:S(2)}, u32[]{:S(2)}) collective-permute-start(f32[72,128]{1,0:T(8,128)S(1)} %bitcast_add_fusion.a_ref), channel_id=1, source_target_pairs={{0,64},{16,80},{32,96},{48,112},{64,0},{80,16},{96,32},{112,48},{1... | collective-permute-start | bytes 110600 | tf_op jit(solution)/shard_map/ppermute | solution.py:570
  93.2 6.6 %collective-permute-start.11 = (f32[72,128]{1,0:T(8,128)S(1)}, f32[72,128]{1,0:T(8,128)S(1)}, u32[]{:S(2)}, u32[]{:S(2)}) collective-permute-start(f32[72,128]{1,0:T(8,128)S(1)} %bitcast_add_fusion.a_ref), channel_id=1, source_target_pairs={{0,32},{16,48},{32,0},{48,16},{64,96},{80,112},{96,64},{112,80},{1... | collective-permute-start | bytes 110600 | tf_op jit(solution)/shard_map/ppermute | solution.py:570
  99.9 9.4 %collective-permute-start.16 = (f32[72,128]{1,0:T(8,128)S(1)}, f32[72,128]{1,0:T(8,128)S(1)}, u32[]{:S(2)}, u32[]{:S(2)}) collective-permute-start(f32[72,128]{1,0:T(8,128)S(1)} %add_up.3.a_ref), channel_id=1, source_target_pairs={{0,12},{1,13},{2,14},{3,15},{4,8},{5,9},{6,10},{7,11},{8,4},{9,5},... | collective-permute-start | bytes 110600 | tf_op jit(solution)/shard_map/ppermute | solution.py:570
  107.9 4.3 %collective-permute-start.15 = (f32[72,128]{1,0:T(8,128)S(1)}, f32[72,128]{1,0:T(8,128)S(1)}, u32[]{:S(2)}, u32[]{:S(2)}) collective-permute-start(f32[72,128]{1,0:T(8,128)S(1)} %add_up.3.a_ref), channel_id=1, source_target_pairs={{0,8},{1,9},{2,10},{3,11},{4,12},{5,13},{6,14},{7,15},{8,0},{9,1},... | collective-permute-start | bytes 110600 | tf_op jit(solution)/shard_map/ppermute | solution.py:570
  107.9 4.3 %collective-permute-start.14 = (f32[72,128]{1,0:T(8,128)S(1)}, f32[72,128]{1,0:T(8,128)S(1)}, u32[]{:S(2)}, u32[]{:S(2)}) collective-permute-start(f32[72,128]{1,0:T(8,128)S(1)} %add_up.3.a_ref), channel_id=1, source_target_pairs={{0,4},{1,5},{2,6},{3,7},{4,0},{5,1},{6,2},{7,3},{8,12},{9,13},{10,... | collective-permute-start | bytes 110600 | tf_op jit(solution)/shard_map/ppermute | solution.py:570
  113.9 17.0 %collective-permute-start.19 = (f32[72,128]{1,0:T(8,128)S(1)}, f32[72,128]{1,0:T(8,128)S(1)}, u32[]{:S(2)}, u32[]{:S(2)}) collective-permute-start(f32[72,128]{1,0:T(8,128)S(1)} %add_up.4.rest_1_.a_ref), channel_id=1, source_target_pairs={{0,3},{1,2},{2,1},{3,0},{4,7},{5,6},{6,5},{7,4},{8,11},{9,10},{10,... | collective-permute-start | bytes 110600 | tf_op jit(solution)/shard_map/ppermute | solution.py:570
  114.3 16.6 %collective-permute-start.18 = (f32[72,128]{1,0:T(8,128)S(1)}, f32[72,128]{1,0:T(8,128)S(1)}, u32[]{:S(2)}, u32[]{:S(2)}) collective-permute-start(f32[72,128]{1,0:T(8,128)S(1)} %add_up.4.rest_1_.a_ref), channel_id=1, source_target_pairs={{0,2},{1,3},{2,0},{3,1},{4,6},{5,7},{6,4},{7,5},{8,10},{9,11},{10,... | collective-permute-start | bytes 110600 | tf_op jit(solution)/shard_map/ppermute | solution.py:570
  114.3 16.7 %collective-permute-start.17 = (f32[72,128]{1,0:T(8,128)S(1)}, f32[72,128]{1,0:T(8,128)S(1)}, u32[]{:S(2)}, u32[]{:S(2)}) collective-permute-start(f32[72,128]{1,0:T(8,128)S(1)} %add_up.4.rest_1_.a_ref), channel_id=1, source_target_pairs={{0,1},{1,0},{2,3},{3,2},{4,5},{5,4},{6,7},{7,6},{8,9},{9,8},{10,11... | collective-permute-start | bytes 110600 | tf_op jit(solution)/shard_map/ppermute | solution.py:570
  131.0 4.3 %collective-permute-start.20 = (f32[72,128]{1,0:T(8,128)S(1)}, f32[72,128]{1,0:T(8,128)S(1)}, u32[]{:S(2)}, u32[]{:S(2)}) collective-permute-start(f32[72,128]{1,0:T(8,128)S(1)} %add_up.5), channel_id=1, source_target_pairs={{0,16},{16,0},{32,48},{48,32},{64,80},{80,64},{96,112},{112,96},{1... | collective-permute-start | bytes 110600 | tf_op jit(solution)/shard_map/ppermute | solution.py:570
  (7 other events, 10.3 us)
